TPU v7x, 32 devices: a whole 2x2x4 slice. The times are simulated.
32 devices in a mesh: seq: 8 (over y, x, core), wa: 4 (over z).
Axes of the slice: x: 2, y: 2, z: 4, core: 2. Of those that a mesh axis runs over, the one named last changes fastest.
Arguments:
- x_in: float32 [2048, 1024], P('seq'), may hold values from -6 to 6
- d_out: float32 [2048, 1024], P('seq'), may hold values from -6 to 6
- segment_ids: int32 [2048], replicated, may hold values from 0 to 3, never falling along the last dimension, each value on 1 to 1536 neighbouring positions
- norm_gains: float32 [2, 2, 1024], replicated, may hold values from 0.5 to 1.5
- w_zx: bfloat16 [2, 1024, 2, 1536], P(None, None, None, 'wa'), may hold values from -0.1875 to 0.1875
- w_bc: bfloat16 [2, 1024, 256], replicated, may hold values from -0.1875 to 0.1875
- w_dt: bfloat16 [2, 1024, 24], P(None, None, 'wa'), may hold values from -0.1875 to 0.1875
- conv_x: float32 [2, 5, 1536], P(None, None, 'wa'), may hold values from -4 to 4
- conv_bc: float32 [2, 5, 256], replicated, may hold values from -4 to 4
- dt_bias: float32 [2, 24], P(None, 'wa'), may hold values from -5 to 1
- a_log: float32 [2, 24], P(None, 'wa'), may hold values from -9 to 1
- d_skip: float32 [2, 24], P(None, 'wa'), may hold values from 0 to 4
- w_out: bfloat16 [2, 1536, 1024], P(None, 'wa'), may hold values from -0.15625 to 0.15625
- w_q: bfloat16 [2, 1024, 512], P(None, None, 'wa'), may hold values from -0.1875 to 0.1875
- key_value_weight: bfloat16 [2, 1024, 2, 128], replicated, may hold values from -0.1875 to 0.1875
- w_ao: bfloat16 [2, 512, 1024], P(None, 'wa'), may hold values from -1 to 1
- w_gu: bfloat16 [2, 1024, 2, 2048], P(None, None, None, 'wa'), may hold values from -0.1875 to 0.1875
- w_down: bfloat16 [2, 2048, 1024], P(None, 'wa'), may hold values from -0.125 to 0.125
Outputs:
- x_out: float32 [2048, 1024], P('seq')
- d_x: float32 [2048, 1024], P('seq')
- g_norm_first: float32 [2, 1024], replicated
- g_norm_second: float32 [2, 1024], replicated
- g_w_zx: float32 [2, 1024, 2, 1536], P(None, 'seq', None, 'wa')
- g_w_bc: float32 [2, 1024, 256], P(None, 'seq')
- g_w_dt: float32 [2, 1024, 24], P(None, 'seq', 'wa')
- g_conv_x: float32 [2, 5, 1536], P(None, None, 'wa')
- g_conv_bc: float32 [2, 5, 256], replicated
- g_dt_bias: float32 [2, 24], P(None, 'wa')
- g_a_log: float32 [2, 24], P(None, 'wa')
- g_d_skip: float32 [2, 24], P(None, 'wa')
- g_w_out: float32 [2, 1536, 1024], P(None, 'wa', 'seq')
- g_w_q: float32 [2, 1024, 512], P(None, 'seq', 'wa')
- g_w_kv: float32 [2, 1024, 2, 128], P(None, 'seq')
- g_w_ao: float32 [2, 512, 1024], P(None, 'wa', 'seq')
- g_w_gu: float32 [2, 1024, 2, 2048], P(None, 'seq', None, 'wa')
- g_w_down: float32 [2, 2048, 1024], P(None, 'wa', 'seq')
Inputs may be any that keep to these rules, and one draw needn't show every extreme that they name: `segment_ids`: segment numbers never fall along the tokens; each of the 4 documents has 1 to 1536 tokens and one has exactly 1536.
All inputs are finite; a program needn't handle non-finite values.
Results may differ from a plain program's by a relative error of at most 0.025.
Values may be sent and summed in bfloat16 or wider, within the bound.
No kernel may reach another device: no remote copies, remote signals or barrier semaphores. Data moves between devices by JAX's collectives and lax.ppermute only.
A program may use at most 192 MiB of HBM per device.

v0:
```python
import math

import jax
import jax.numpy as jnp
from jax import lax
from jax.sharding import PartitionSpec as P

MODEL_WIDTH = 1024
HEAD_SIZE = 64
NS = 128
KC = 4
QUERY_HEADS = 8
KEY_VALUE_HEADS = 2
LAYER_COUNT = 2


eps = 1e-05
theta = 10000.0
neg_big = -1e30


def from_behind(block, axis, distance):
    devices = range(lax.axis_size(axis))
    route = [(i - distance, i) for i in devices if i - distance in devices]
    return lax.ppermute(block, axis, route)


def entering(shard, axis, combine, identity, reverse):
    length, here = (lax.axis_size(axis), lax.axis_index(axis))
    everything = jax.tree.map(lambda part: lax.all_gather(part, axis), shard)
    start = jax.tree.map(
        lambda part, zero: jnp.broadcast_to(jnp.asarray(zero, part.dtype), part.shape),
        shard,
        identity,
    )

    def hop(k, before):
        at = length - 1 - k if reverse else k
        reached = at > here if reverse else at < here
        new = combine(before, jax.tree.map(lambda part: part[at], everything))
        return jax.tree.map(lambda a, b: jnp.where(reached, a, b), new, before)

    return lax.fori_loop(0, length, hop, start)


def norm_apply(values, gain):
    return values * lax.rsqrt(jnp.mean(values * values, axis=-1, keepdims=True) + eps) * gain


def swiglu(gate_part, up_part):
    return jax.nn.silu(gate_part) * up_part


def rotate(tensor, position):
    half_width = tensor.shape[-1] // 2
    frequency = jnp.exp(jnp.arange(half_width, dtype=jnp.float32) * (-math.log(theta) / half_width))
    angles = position[:, None] * frequency[None, :]
    cosine = jnp.cos(angles)[:, None, :]
    sine_part = jnp.sin(angles)[:, None, :]
    first_half = tensor[..., :half_width]
    second = tensor[..., half_width:]
    return jnp.concatenate(
        [first_half * cosine - second * sine_part, second * cosine + first_half * sine_part],
        axis=-1,
    )


def rotate_back(grad_in, like, position):
    return jax.vjp(lambda tensor: rotate(tensor, position), like)[1](grad_in)[0]


def mixer_front(
    inputs, edge_rows, conv_w, dt_raw, dt_bias, a_log, d_skip, seg_here, seg_edge, seg_before
):
    length = inputs.shape[0]
    head_count = dt_raw.shape[1]
    inner_width = head_count * HEAD_SIZE
    padded = jnp.concatenate([edge_rows, inputs], axis=0)
    seg_full = jnp.concatenate([seg_edge, seg_here])
    conv_sum = jnp.broadcast_to(conv_w[KC], inputs.shape)
    for offset in range(KC):
        usable = (seg_full[offset : offset + length] == seg_here).astype(jnp.float32)
        conv_sum = conv_sum + conv_w[offset] * padded[offset : offset + length] * usable[:, None]
    active = jax.nn.silu(conv_sum)
    x_heads = active[:, :inner_width].reshape(length, head_count, HEAD_SIZE)
    b_mat = active[:, inner_width : inner_width + NS]
    c_mat = active[:, inner_width + NS :]
    dt_val = jax.nn.softplus(dt_raw + dt_bias)
    log_decay = -dt_val * jnp.exp(a_log)
    cumulative = jnp.cumsum(log_decay, axis=0)
    places = jnp.arange(length)
    allowed = (seg_here[:, None] == seg_here[None, :]) & (places[None, :] <= places[:, None])
    differences = cumulative.T[:, :, None] - cumulative.T[:, None, :]
    decay_pair = jnp.exp(jnp.where(allowed[None], differences, neg_big))
    intersection = jnp.dot(c_mat, b_mat.T, precision=lax.Precision.HIGHEST)
    x_scaled = x_heads * dt_val[:, :, None]
    within = jnp.einsum(
        "hts,shp->thp", decay_pair * intersection[None], x_scaled, precision=lax.Precision.HIGHEST
    )
    y_local = within + d_skip[None, :, None] * x_heads
    inside = (seg_here == seg_before).astype(jnp.float32)
    decay_in = jnp.exp(cumulative) * inside[:, None]
    same_last = (seg_here == seg_here[length - 1])[:, None]
    to_last = jnp.exp(jnp.where(same_last, cumulative[length - 1][None, :] - cumulative, neg_big))
    block_decay = jnp.exp(cumulative[length - 1]) * inside[length - 1]
    local_state = jnp.einsum(
        "shp,sn->hpn", x_scaled * to_last[:, :, None], b_mat, precision=lax.Precision.HIGHEST
    )
    return (y_local, decay_in, c_mat, block_decay, local_state)


def mixer_back(y_local, decay_in, c_mat, state_in, gate_raw):
    inflow = (
        jnp.einsum("tn,hpn->thp", c_mat, state_in, precision=lax.Precision.HIGHEST)
        * decay_in[:, :, None]
    )
    mixed_y = (y_local + inflow).reshape(y_local.shape[0], -1)
    return mixed_y * jax.nn.silu(gate_raw)


def mixer_all(
    inputs,
    edge_rows,
    conv_w,
    dt_raw,
    dt_bias,
    a_log,
    d_skip,
    gate_raw,
    state_in,
    seg_here,
    seg_edge,
    seg_before,
):
    front = mixer_front(
        inputs, edge_rows, conv_w, dt_raw, dt_bias, a_log, d_skip, seg_here, seg_edge, seg_before
    )
    return (mixer_back(front[0], front[1], front[2], state_in, gate_raw), front[3], front[4])


def chain_pair(earlier, later):
    return (earlier[0] * later[0], later[0] * earlier[1] + later[1])


def sum_heads(partial_sum):
    return lax.psum(partial_sum, "wa")


def attend_block(carry, key_rows, value_row_list, queries, q_pos, q_seg, segment_ids, score_scale):
    running_max, running_sum, running_out = carry
    key_count = key_rows.shape[0]
    scores = (
        jnp.einsum("rd,kd->rk", queries, key_rows, preferred_element_type=jnp.float32) * score_scale
    )
    k_pos = jnp.arange(key_count, dtype=jnp.int32)
    allowed = (k_pos[None, :] <= q_pos[:, None]) & (segment_ids[None, :] == q_seg[:, None])
    new_max = jnp.maximum(running_max, jnp.max(jnp.where(allowed, scores, neg_big), axis=1))
    weights = jnp.where(allowed, jnp.exp(scores - new_max[:, None]), 0.0)
    running_sum = jnp.sum(weights, axis=1)
    running_out = jnp.dot(
        weights, value_row_list.astype(jnp.float32), precision=lax.Precision.HIGHEST
    )
    return (new_max, running_sum, running_out)


def stack_layers(layer_items):
    return tuple(
        (
            jnp.stack([layer_entry[member] for layer_entry in layer_items])
            for member in range(len(layer_items[0]))
        )
    )


def per_device(
    x_in,
    d_out,
    segment_ids,
    norm_gains,
    w_zx,
    w_bc,
    w_dt,
    conv_x,
    conv_bc,
    dt_bias,
    a_log,
    d_skip,
    w_out,
    w_q,
    key_value_weight,
    w_ao,
    w_gu,
    w_down,
):
    seq_count = lax.axis_size("seq")
    tok_rows = x_in.shape[0]
    start_row = lax.axis_index("seq") * tok_rows
    inner_local = w_zx.shape[3]
    head_local = w_dt.shape[2]
    query_local = w_q.shape[2] // HEAD_SIZE
    hidden_local = w_gu.shape[3]
    query_group_width = QUERY_HEADS // KEY_VALUE_HEADS
    key_value_head = lax.axis_index("wa") * query_local // query_group_width
    score_scale = 1.0 / math.sqrt(HEAD_SIZE)
    query_rows = query_local * tok_rows
    positions = start_row + jnp.arange(tok_rows, dtype=jnp.int32)
    pos_float = positions.astype(jnp.float32)
    seg_here = lax.dynamic_slice_in_dim(segment_ids, start_row, tok_rows)
    seg_padded = jnp.concatenate([jnp.full((KC - 1,), -1, jnp.int32), segment_ids])
    seg_edge = lax.dynamic_slice_in_dim(seg_padded, start_row, KC - 1)
    seg_before = seg_edge[KC - 2]
    q_pos = jnp.tile(positions, query_local)
    q_seg = jnp.tile(seg_here, query_local)
    state_ident = (
        jnp.ones((head_local, 1, 1), jnp.float32),
        jnp.zeros((head_local, HEAD_SIZE, NS), jnp.float32),
    )
    hidden = x_in
    saved = []
    for layer_number in range(LAYER_COUNT):
        gains = norm_gains[layer_number]
        wzx_flat = w_zx[layer_number].reshape(MODEL_WIDTH, 2 * inner_local)
        normalized_input = norm_apply(hidden, gains[0]).astype(jnp.bfloat16)
        zx_raw = jnp.dot(normalized_input, wzx_flat, preferred_element_type=jnp.float32)
        gate_raw = zx_raw[:, :inner_local]
        bc_raw = jnp.dot(normalized_input, w_bc[layer_number], preferred_element_type=jnp.float32)
        dt_raw = jnp.dot(normalized_input, w_dt[layer_number], preferred_element_type=jnp.float32)
        mix_in = jnp.concatenate([zx_raw[:, inner_local:], bc_raw], axis=1)
        conv_w = jnp.concatenate([conv_x[layer_number], conv_bc[layer_number]], axis=1)
        edge_rows = from_behind(mix_in[tok_rows - (KC - 1) :], "seq", 1)
        front = mixer_front(
            mix_in,
            edge_rows,
            conv_w,
            dt_raw,
            dt_bias[layer_number],
            a_log[layer_number],
            d_skip[layer_number],
            seg_here,
            seg_edge,
            seg_before,
        )
        state_in = entering(
            (front[3][:, None, None], front[4]), "seq", chain_pair, state_ident, False
        )[1]
        gated = mixer_back(front[0], front[1], front[2], state_in, gate_raw).astype(jnp.bfloat16)
        mamba_part = jnp.dot(gated, w_out[layer_number], preferred_element_type=jnp.float32)
        q_raw = jnp.dot(
            normalized_input, w_q[layer_number], preferred_element_type=jnp.float32
        ).reshape(tok_rows, query_local, HEAD_SIZE)
        queries = (
            rotate(q_raw, pos_float)
            .astype(jnp.bfloat16)
            .transpose(1, 0, 2)
            .reshape(query_rows, HEAD_SIZE)
        )
        kv_weight = lax.dynamic_slice_in_dim(
            key_value_weight[layer_number], key_value_head * HEAD_SIZE, HEAD_SIZE, axis=2
        ).reshape(MODEL_WIDTH, 2 * HEAD_SIZE)
        key_value_unrotated = jnp.dot(
            normalized_input, kv_weight, preferred_element_type=jnp.float32
        )
        key_rows = rotate(key_value_unrotated[:, None, :HEAD_SIZE], pos_float)[:, 0].astype(
            jnp.bfloat16
        )
        value_row_list = key_value_unrotated[:, HEAD_SIZE:].astype(jnp.bfloat16)
        start_fold = (
            jnp.full((query_rows,), neg_big, jnp.float32),
            jnp.zeros((query_rows,), jnp.float32),
            jnp.zeros((query_rows, HEAD_SIZE), jnp.float32),
        )
        running = attend_block(
            start_fold,
            lax.all_gather(key_rows, "seq", axis=0, tiled=True),
            lax.all_gather(value_row_list, "seq", axis=0, tiled=True),
            queries,
            q_pos,
            q_seg,
            segment_ids,
            score_scale,
        )
        kept_keys = None
        attn_out = running[2] / running[1][:, None]
        log_total = running[0] + jnp.log(running[1])
        attn_flat = (
            attn_out.reshape(query_local, tok_rows, HEAD_SIZE)
            .transpose(1, 0, 2)
            .reshape(tok_rows, query_local * HEAD_SIZE)
            .astype(jnp.bfloat16)
        )
        attn_part = jnp.dot(attn_flat, w_ao[layer_number], preferred_element_type=jnp.float32)
        mixed = hidden + sum_heads(mamba_part + attn_part)
        normed_two = norm_apply(mixed, gains[1]).astype(jnp.bfloat16)
        gate_up = jnp.dot(
            normed_two,
            w_gu[layer_number].reshape(MODEL_WIDTH, 2 * hidden_local),
            preferred_element_type=jnp.float32,
        )
        act_ff = swiglu(gate_up[:, :hidden_local], gate_up[:, hidden_local:]).astype(jnp.bfloat16)
        output = mixed + sum_heads(
            jnp.dot(act_ff, w_down[layer_number], preferred_element_type=jnp.float32)
        )
        saved.append(
            (
                hidden,
                normalized_input,
                mix_in,
                gate_raw,
                dt_raw,
                edge_rows,
                front,
                state_in,
                gated,
                q_raw,
                queries,
                key_value_unrotated,
                key_rows,
                value_row_list,
                kept_keys,
                attn_out,
                log_total,
                attn_flat,
                mixed,
                normed_two,
                gate_up,
                act_ff,
            )
        )
        hidden = output
    grad = d_out
    big_list = [None] * LAYER_COUNT
    small_list = [None] * LAYER_COUNT
    for layer_number in reversed(range(LAYER_COUNT)):
        (
            hidden_in,
            normalized_input,
            mix_in,
            gate_raw,
            dt_raw,
            edge_rows,
            front,
            state_in,
            gated,
            q_raw,
            queries,
            key_value_unrotated,
            key_rows,
            value_row_list,
            kept_keys,
            attn_out,
            log_total,
            attn_flat,
            mixed,
            normed_two,
            gate_up,
            act_ff,
        ) = saved[layer_number]
        gains = norm_gains[layer_number]
        wzx_flat = w_zx[layer_number].reshape(MODEL_WIDTH, 2 * inner_local)
        wgu_flat = w_gu[layer_number].reshape(MODEL_WIDTH, 2 * hidden_local)
        kv_weight = lax.dynamic_slice_in_dim(
            key_value_weight[layer_number], key_value_head * HEAD_SIZE, HEAD_SIZE, axis=2
        ).reshape(MODEL_WIDTH, 2 * HEAD_SIZE)
        conv_w = jnp.concatenate([conv_x[layer_number], conv_bc[layer_number]], axis=1)
        grad_b = grad.astype(jnp.bfloat16)
        g_down = jnp.einsum("sf,sd->fd", act_ff, grad_b, preferred_element_type=jnp.float32)
        d_act = jnp.einsum(
            "sd,fd->sf", grad_b, w_down[layer_number], preferred_element_type=jnp.float32
        )
        d_gate, d_up = jax.vjp(swiglu, gate_up[:, :hidden_local], gate_up[:, hidden_local:])[1](
            d_act
        )
        d_gu = jnp.concatenate([d_gate, d_up], axis=1).astype(jnp.bfloat16)
        g_gu = jnp.einsum(
            "sd,sc->dc", normed_two, d_gu, preferred_element_type=jnp.float32
        ).reshape(MODEL_WIDTH, 2, hidden_local)
        d_normed_two = sum_heads(
            jnp.einsum("sc,dc->sd", d_gu, wgu_flat, preferred_element_type=jnp.float32)
        )
        d_mixed_n, g_gain_two = jax.vjp(norm_apply, mixed, gains[1])[1](d_normed_two)
        d_mixed = grad + d_mixed_n
        mixed_b = d_mixed.astype(jnp.bfloat16)
        g_out = jnp.einsum("sc,sd->cd", gated, mixed_b, preferred_element_type=jnp.float32)
        d_gated = jnp.einsum(
            "sd,cd->sc", mixed_b, w_out[layer_number], preferred_element_type=jnp.float32
        )
        g_ao = jnp.einsum("sc,sd->cd", attn_flat, mixed_b, preferred_element_type=jnp.float32)
        d_attn = jnp.einsum(
            "sd,cd->sc", mixed_b, w_ao[layer_number], preferred_element_type=jnp.float32
        )
        d_attn = (
            d_attn.reshape(tok_rows, query_local, HEAD_SIZE)
            .transpose(1, 0, 2)
            .reshape(query_rows, HEAD_SIZE)
        )
        delta_rows = jnp.sum(d_attn * attn_out, axis=1)
        d_attn_b = d_attn.astype(jnp.bfloat16)
        all_keys, all_values = (
            lax.all_gather(key_rows, "seq", axis=0, tiled=True),
            lax.all_gather(value_row_list, "seq", axis=0, tiled=True),
        )

        def back_block(d_query, block_no):
            key_start = block_no * tok_rows
            key_blk = lax.dynamic_slice_in_dim(all_keys, key_start, tok_rows)
            value_blk = lax.dynamic_slice_in_dim(all_values, key_start, tok_rows)
            scores = (
                jnp.einsum("rd,kd->rk", queries, key_blk, preferred_element_type=jnp.float32)
                * score_scale
            )
            k_pos = key_start + jnp.arange(tok_rows, dtype=jnp.int32)
            k_seg = lax.dynamic_slice_in_dim(segment_ids, key_start, tok_rows)
            allowed = (k_pos[None, :] <= q_pos[:, None]) & (k_seg[None, :] == q_seg[:, None])
            probs = jnp.where(allowed, jnp.exp(scores - log_total[:, None]), 0.0)
            d_value = jnp.einsum(
                "rk,rd->kd",
                probs.astype(jnp.bfloat16),
                d_attn_b,
                preferred_element_type=jnp.float32,
            )
            d_probs = jnp.einsum(
                "rd,kd->rk", d_attn_b, value_blk, preferred_element_type=jnp.float32
            )
            d_scores = (probs * (d_probs - delta_rows[:, None])).astype(jnp.bfloat16)
            d_query = (
                d_query
                + jnp.dot(d_scores, key_blk, preferred_element_type=jnp.float32) * score_scale
            )
            d_key = (
                jnp.einsum("rk,rd->kd", d_scores, queries, preferred_element_type=jnp.float32)
                * score_scale
            )
            return (d_query, (d_key, d_value))

        d_query, (key_terms, value_terms) = lax.scan(
            back_block,
            jnp.zeros((query_rows, HEAD_SIZE), jnp.float32),
            jnp.arange(seq_count, dtype=jnp.int32),
        )
        d_key_own, d_value_own = (
            lax.psum_scatter(
                key_terms.reshape(seq_count * tok_rows, HEAD_SIZE),
                "seq",
                scatter_dimension=0,
                tiled=True,
            ),
            lax.psum_scatter(
                value_terms.reshape(seq_count * tok_rows, HEAD_SIZE),
                "seq",
                scatter_dimension=0,
                tiled=True,
            ),
        )
        d_q_tok = d_query.reshape(query_local, tok_rows, HEAD_SIZE).transpose(1, 0, 2)
        dq_b = (
            rotate_back(d_q_tok, q_raw, pos_float)
            .reshape(tok_rows, query_local * HEAD_SIZE)
            .astype(jnp.bfloat16)
        )
        grad_key_unrotated = rotate_back(
            d_key_own[:, None, :], key_value_unrotated[:, None, :HEAD_SIZE], pos_float
        )[:, 0]
        grad_key_value_block = jnp.concatenate([grad_key_unrotated, d_value_own], axis=1).astype(
            jnp.bfloat16
        )
        state_grad = jax.vjp(
            lambda state_part: mixer_back(front[0], front[1], front[2], state_part, gate_raw),
            state_in,
        )[1](d_gated)[0]
        later_grad = entering(
            (front[3][:, None, None], state_grad), "seq", chain_pair, state_ident, True
        )[1]
        d_decay = jnp.sum(later_grad * state_in, axis=(1, 2))

        def whole(inputs, edges, conv_part, dt_part, bias_part, log_part, skip_part, gate_part):
            return mixer_all(
                inputs,
                edges,
                conv_part,
                dt_part,
                bias_part,
                log_part,
                skip_part,
                gate_part,
                state_in,
                seg_here,
                seg_edge,
                seg_before,
            )

        grad_list = jax.vjp(
            whole,
            mix_in,
            edge_rows,
            conv_w,
            dt_raw,
            dt_bias[layer_number],
            a_log[layer_number],
            d_skip[layer_number],
            gate_raw,
        )[1]((d_gated, d_decay, later_grad))
        from_next = from_behind(grad_list[1], "seq", -1)
        d_mix = grad_list[0].at[tok_rows - (KC - 1) :].add(from_next)
        g_conv = grad_list[2]
        dzx_b = jnp.concatenate([grad_list[7], d_mix[:, :inner_local]], axis=1).astype(jnp.bfloat16)
        dbc_b = d_mix[:, inner_local:].astype(jnp.bfloat16)
        ddt_b = grad_list[3].astype(jnp.bfloat16)
        g_zx = jnp.einsum(
            "sd,sc->dc", normalized_input, dzx_b, preferred_element_type=jnp.float32
        ).reshape(MODEL_WIDTH, 2, inner_local)
        g_bc = jnp.einsum("sd,sc->dc", normalized_input, dbc_b, preferred_element_type=jnp.float32)
        g_dt = jnp.einsum("sd,sc->dc", normalized_input, ddt_b, preferred_element_type=jnp.float32)
        g_q = jnp.einsum("sd,sc->dc", normalized_input, dq_b, preferred_element_type=jnp.float32)
        grad_key_value_head = jnp.einsum(
            "sd,sc->dc", normalized_input, grad_key_value_block, preferred_element_type=jnp.float32
        ).reshape(MODEL_WIDTH, 2, HEAD_SIZE)
        grad_key_value = lax.dynamic_update_slice_in_dim(
            jnp.zeros((MODEL_WIDTH, 2, KEY_VALUE_HEADS * HEAD_SIZE), jnp.float32),
            grad_key_value_head,
            key_value_head * HEAD_SIZE,
            axis=2,
        )
        d_normed = jnp.einsum("sc,dc->sd", dzx_b, wzx_flat, preferred_element_type=jnp.float32)
        d_normed = d_normed + jnp.einsum(
            "sc,dc->sd", dbc_b, w_bc[layer_number], preferred_element_type=jnp.float32
        )
        d_normed = d_normed + jnp.einsum(
            "sc,dc->sd", ddt_b, w_dt[layer_number], preferred_element_type=jnp.float32
        )
        d_normed = d_normed + jnp.einsum(
            "sc,dc->sd", dq_b, w_q[layer_number], preferred_element_type=jnp.float32
        )
        d_normed = d_normed + jnp.einsum(
            "sc,dc->sd", grad_key_value_block, kv_weight, preferred_element_type=jnp.float32
        )
        d_normed = sum_heads(d_normed)
        d_hidden_n, g_gain_one = jax.vjp(norm_apply, hidden_in, gains[0])[1](d_normed)
        grad = d_mixed + d_hidden_n
        big_local = (g_zx, g_dt, g_q, g_out, g_ao, g_gu, g_down, g_bc, grad_key_value)
        big_list[layer_number] = big_local
        small_list[layer_number] = (
            jnp.stack([g_gain_one, g_gain_two]),
            grad_list[4],
            grad_list[5],
            grad_list[6],
            g_conv[:, :inner_local],
            g_conv[:, inner_local:],
        )
    big_all = stack_layers(big_list)
    big_all = (
        lax.psum_scatter(big_all[0], "seq", scatter_dimension=1, tiled=True),
        lax.psum_scatter(big_all[1], "seq", scatter_dimension=1, tiled=True),
        lax.psum_scatter(big_all[2], "seq", scatter_dimension=1, tiled=True),
        lax.psum_scatter(big_all[3], "seq", scatter_dimension=2, tiled=True),
        lax.psum_scatter(big_all[4], "seq", scatter_dimension=2, tiled=True),
        lax.psum_scatter(big_all[5], "seq", scatter_dimension=1, tiled=True),
        lax.psum_scatter(big_all[6], "seq", scatter_dimension=2, tiled=True),
        lax.psum_scatter(big_all[7], "seq", scatter_dimension=1, tiled=True),
        lax.psum_scatter(big_all[8], "seq", scatter_dimension=1, tiled=True),
    )
    small_all = lax.psum(stack_layers(small_list), "seq")
    shared = lax.psum((big_all[7], big_all[8], small_all[5]), "wa")
    return (
        hidden,
        grad,
        small_all[0][:, 0],
        small_all[0][:, 1],
        big_all[0],
        shared[0],
        big_all[1],
        small_all[4],
        shared[2],
        small_all[1],
        small_all[2],
        small_all[3],
        big_all[3],
        big_all[2],
        shared[1],
        big_all[4],
        big_all[5],
        big_all[6],
    )


def solution(mesh):
    return jax.shard_map(
        per_device,
        mesh=mesh,
        in_specs=(
            P("seq", None),
            P("seq", None),
            P(),
            P(),
            P(None, None, None, "wa"),
            P(),
            P(None, None, "wa"),
            P(None, None, "wa"),
            P(),
            P(None, "wa"),
            P(None, "wa"),
            P(None, "wa"),
            P(None, "wa", None),
            P(None, None, "wa"),
            P(),
            P(None, "wa", None),
            P(None, None, None, "wa"),
            P(None, "wa", None),
        ),
        out_specs=(
            P("seq", None),
            P("seq", None),
            P(),
            P(),
            P(None, "seq", None, "wa"),
            P(None, "seq", None),
            P(None, "seq", "wa"),
            P(None, None, "wa"),
            P(),
            P(None, "wa"),
            P(None, "wa"),
            P(None, "wa"),
            P(None, "wa", "seq"),
            P(None, "seq", "wa"),
            P(None, "seq", None, None),
            P(None, "wa", "seq"),
            P(None, "seq", None, "wa"),
            P(None, "wa", "seq"),
        ),
        check_vma=False,
    )
```

profile of v0, /device:TPU:0, one launch (start us, length us, event | category | flops | bytes accessed | tf_op | source)
XLA Modules:
  0.0 1844.1 jit_solution(1463556223886140397)
XLA Ops:
  58.9 10.9 all-gather.2
  119.3 44.8 %all-reduce.47.cloned.1.call-done = f32[256,1024]{1,0:T(8,128)} async-done(((f32[256,1024]{1,0:T(8,128)}), f32[256,1024]{1,0:T(8,128)}) %all-reduce.47.cloned.1.call-update) | async-done | bytes 1048592 | tf_op jit(solution)/shard_map/psum | solution.py:146
  177.9 43.3 %all-reduce.49.cloned.1.call-done = f32[256,1024]{1,0:T(8,128)} async-done(((f32[256,1024]{1,0:T(8,128)}), f32[256,1024]{1,0:T(8,128)}) %all-reduce.49.cloned.1.call-update) | async-done | bytes 1048592 | tf_op jit(solution)/shard_map/psum | solution.py:146
  235.6 9.7 all-gather.9
  255.0 12.0 all-gather.5
  267.0 9.8 all_gather.57
  314.7 47.3 %all-reduce.51.cloned.1.call-done = f32[256,1024]{1,0:T(8,128)} async-done(((f32[256,1024]{1,0:T(8,128)}), f32[256,1024]{1,0:T(8,128)}) %all-reduce.51.cloned.1.call-update) | async-done | bytes 1048592 | tf_op jit(solution)/shard_map/psum | solution.py:146
  374.7 46.4 %all-reduce.53.cloned.1.call-done = f32[256,1024]{1,0:T(8,128)} async-done(((f32[256,1024]{1,0:T(8,128)}), f32[256,1024]{1,0:T(8,128)}) %all-reduce.53.cloned.1.call-update) | async-done | bytes 1048592 | tf_op jit(solution)/shard_map/psum | solution.py:146
  430.5 103.2 %while.95 = (s32[]{:T(128)}, f32[512,64]{0,1:T(8,128)}, f32[8,256,64]{1,0,2:T(8,128)}, f32[8,256,64]{1,0,2:T(8,128)}, s32[8]{0:T(128)}, /*index=5*/s32[2048]{0:T...) while((s32[]{:T(128)}, f32[512,64]{0,1:T(8,128)}, ...), condition=%wide.region_38.40_spmd.clone, body=%wide.region_37.39_spmd.clone.sunk | while | flops 85311744 | bytes 3730701 | solution.py:435
  560.2 9.4 reduce-scatter.25.cloned.1.call-done
  570.4 36.7 %reduce-scatter.23.cloned.1.call-done = f32[256,64]{0,1:T(8,128)} async-done(((f32[2048,64]{0,1:T(8,128)}), f32[256,64]{0,1:T(8,128)}) %reduce-scatter.23.cloned.1.call-update) | async-done | bytes 65552 | tf_op jit(solution)/shard_map/reduce_scatter | solution.py:441
  610.4 24.9 %all-gather.19.cloned.1.call-done = f32[48,64,128]{2,1,0:T(8,128)} async-done(((f32[6,64,128]{2,1,0:T(8,128)}), f32[48,64,128]{2,1,0:T(8,128)}) %all-gather.19.cloned.1.call-update) | async-done | bytes 1572880 | tf_op jit(solution)/shard_map/all_gather | solution.py:30
  635.4 13.5 while.94
  686.6 53.7 %all-reduce.55.cloned.1.call-done = f32[256,1024]{1,0:T(8,128)} async-done(((f32[256,1024]{1,0:T(8,128)}), f32[256,1024]{1,0:T(8,128)}) %all-reduce.55.cloned.1.call-update) | async-done | bytes 1048592 | tf_op jit(solution)/shard_map/psum | solution.py:146
  749.7 49.9 %all-reduce.57.cloned.1.call-done = f32[256,1024]{1,0:T(8,128)} async-done(((f32[256,1024]{1,0:T(8,128)}), f32[256,1024]{1,0:T(8,128)}) %all-reduce.57.cloned.1.call-update) | async-done | bytes 1048592 | tf_op jit(solution)/shard_map/psum | solution.py:146
  808.1 89.7 %while.97 = (s32[]{:T(128)}, f32[512,64]{0,1:T(8,128)}, f32[8,256,64]{1,0,2:T(8,128)}, f32[8,256,64]{1,0,2:T(8,128)}, s32[8]{0:T(128)S(1)}, /*index=5*/s32[2048]...) while((s32[]{:T(128)}, f32[512,64]{0,1:T(8,128)}, ...), condition=%wide.region_61.63_spmd.clone, body=%wide.region_60.62_spmd.clone.sunk | while | flops 85311744 | bytes 3665165 | solution.py:435
  920.0 31.8 %dynamic_update_slice.22 = f32[1,1024,2,128]{3,2,1,0:T(2,128)} dynamic-update-slice(f32[1,1024,2,128]{3,2,1,0:T(2,128)} %stack.156.clone, f32[1,1024,2,64]{3,2,1,0:T(2,128)} %copy.320, s32[]{:T(128)} %constant.315.clone.1, s32[]{:T(128)} %constant.315.clone.1, s32[]{:T(128)} %constant.315.clone.1, s32[]{:T(128)S(6)} %select_n.224) | dynamic-update-slice | bytes 1048580 | tf_op jit(solution)/shard_map/dynamic_update_slice | solution.py:517
  960.8 10.9 reduce-scatter.27.cloned.1.call-done
  977.2 31.7 %dynamic_update_slice.21 = f32[1,1024,2,128]{3,2,1,0:T(2,128)} dynamic-update-slice(f32[1,1024,2,128]{3,2,1,0:T(2,128)} %stack.156.clone.1, f32[1,1024,2,64]{3,2,1,0:T(2,128)} %copy.319, s32[]{:T(128)} %constant.315.clone.1, s32[]{:T(128)} %constant.315.clone.1, s32[]{:T(128)} %constant.315.clone.1, s32[]{:T(128)S(6)} %select_n.224) | dynamic-update-slice | bytes 1048580 | tf_op jit(solution)/shard_map/dynamic_update_slice | solution.py:517
  1016.3 13.5 while.96
  1084.6 236.5 %reduce-scatter.45.cloned.1.call-done = f32[128,512]{1,0:T(8,128)} async-done(((f32[1024,512]{1,0:T(8,128)}), f32[128,512]{1,0:T(8,128)}) %reduce-scatter.45.cloned.1.call-update) | async-done | bytes 262160
  1323.0 42.9 %reduce-scatter.31.cloned.1.call-done = f32[2,128,256]{2,1,0:T(8,128)} async-done(((f32[2,1024,256]{2,1,0:T(8,128)}), f32[2,128,256]{2,1,0:T(8,128)}) %reduce-scatter.31.cloned.1.call-update) | async-done | bytes 262160 | tf_op jit(solution)/shard_map/reduce_scatter | solution.py:558
  1396.0 11.8 reshape.886
  1457.8 52.6 %all-reduce.59.cloned.1.call-done = (f32[256,1024]{1,0:T(8,128)}, f32[256,1024]{1,0:T(8,128)}, f32[2,128,256]{2,1,0:T(8,128)}, f32[2,128,2,128]{3,2,1,0:T(2,128)}) async-done(((f32[256,1024]{1,0:T(8,128)}, f32[256,1024]{1,0:T(8,128)}, f32[2,128,256]{2,1,0:T(8,128)}, f32[2,128,2,128]{3,2,1,0:T(2,128)}), (f32[256,1024]{1,0:T(8,128)}, f32[256,1024]{1,0:T(8,128)}, f32[2,128,256]{2,1,0:T(8,128)}, ...) | async-done | bytes 2621456 | tf_op jit(solution)/shard_map/psum | solution.py:146
  1513.3 24.5 %all-reduce.37 = (f32[2,2,1024]{2,0,1:T(2,128)S(1)}, f32[2,5,384]{2,1,0:T(8,128)S(1)}, f32[2,5,256]{2,1,0:T(8,128)S(1)}, f32[2,6]{1,0:T(2,128)}, f32[2,6]{1,0:T(2,128)}, /*index=5*/f32[2,6]{1,0:T(2,128)}) all-reduce(f32[2,2,1024]{2,0,1:T(2,128)S(1)} %pad_maximum_fusion.32, ...), channel_id=1, replica_groups=mesh['seq'=8,'wa'=4] {'seq'}, use_global_device_ids=true, to_apply=%region_70.72 | all-reduce | flops 10532 | bytes 84256 | tf_op jit(solution)/shard_map/psum | solution.py:561
  1538.4 17.2 psum.131
  1558.1 26.4 %reduce-scatter.47.cloned.1.call-done = f32[128,2048]{1,0:T(8,128)} async-done(((f32[1024,2048]{1,0:T(8,128)}), f32[128,2048]{1,0:T(8,128)}) %reduce-scatter.47.cloned.1.call-update) | async-done | bytes 1048592
  1588.0 61.6 %reduce-scatter.43.cloned.1.call-done = f32[128,1536]{1,0:T(8,128)} async-done(((f32[1024,1536]{1,0:T(8,128)}), f32[128,1536]{1,0:T(8,128)}) %reduce-scatter.43.cloned.1.call-update) | async-done | bytes 786448
  1652.4 37.4 %reduce-scatter.37.cloned.1.call-done = f32[2,128,128]{2,1,0:T(8,128)} async-done(((f32[2,1024,128]{2,1,0:T(8,128)}), f32[2,128,128]{2,1,0:T(8,128)}) %reduce-scatter.37.cloned.1.call-update) | async-done | bytes 131088 | tf_op jit(solution)/shard_map/reduce_scatter | solution.py:553
  1689.7 40.1 %reduce-scatter.39.cloned.1.call-done = f32[2,128,128]{2,1,0:T(8,128)} async-done(((f32[2,128,1024]{2,1,0:T(8,128)}), f32[2,128,128]{2,1,0:T(8,128)}) %reduce-scatter.39.cloned.1.call-update) | async-done | bytes 131088 | tf_op jit(solution)/shard_map/reduce_scatter | solution.py:555
  1729.9 50.6 %reduce-scatter.35.cloned.1.call-done = f32[2,384,128]{2,1,0:T(8,128)} async-done(((f32[2,384,1024]{2,1,0:T(8,128)}), f32[2,384,128]{2,1,0:T(8,128)}) %reduce-scatter.35.cloned.1.call-update) | async-done | bytes 393232 | tf_op jit(solution)/shard_map/reduce_scatter | solution.py:554
  1780.5 55.1 %reduce-scatter.41.cloned.1.call-done = f32[2,512,128]{2,1,0:T(8,128)} async-done(((f32[2,512,1024]{2,1,0:T(8,128)}), f32[2,512,128]{2,1,0:T(8,128)}) %reduce-scatter.41.cloned.1.call-update) | async-done | bytes 524304 | tf_op jit(solution)/shard_map/reduce_scatter | solution.py:557
  (1333 shorter events, 700.8 us)
Async XLA Ops:
  7.2 86.8 %all-gather.15.cloned.1.call-start = ((), (), s32[]{:S(2)}) async-start(), calls=%async_computation.29 | async-start | bytes 1769472 | tf_op jit(solution)/shard_map/all_gather | solution.py:30
  19.4 32.1 %collective-permute-start = (f32[3,640]{1,0:T(4,128)}, f32[3,640]{1,0:T(4,128)}, u32[]{:S(2)}, u32[]{:S(2)}) collective-permute-start(f32[3,640]{1,0:T(4,128)} %fusion.363), channel_id=1, source_target_pairs={{0,4},{4,8},{8,12},{12,16},{16,20},{20,24},{24,28},{1,5},{5,9},{9,... | collective-permute-start | bytes 23048 | tf_op jit(solution)/shard_map/ppermute | solution.py:25
  58.7 105.4 %all-reduce.47.cloned.1.call-start = ((), (), s32[]{:S(2)}) async-start(), calls=%async_computation.13 | async-start | bytes 2097152 | tf_op jit(solution)/shard_map/psum | solution.py:146
  111.7 109.5 %all-reduce.49.cloned.1.call-start = ((), (), s32[]{:S(2)}) async-start(), calls=%async_computation.14 | async-start | bytes 2097152 | tf_op jit(solution)/shard_map/psum | solution.py:146
  169.8 121.3 %all-gather.17.cloned.1.call-start = ((), (), s32[]{:S(2)}) async-start(), calls=%async_computation.30 | async-start | bytes 1769472 | tf_op jit(solution)/shard_map/all_gather | solution.py:30
  227.4 17.9 collective-permute-start.1
  254.7 107.3 %all-reduce.51.cloned.1.call-start = ((), (), s32[]{:S(2)}) async-start(), calls=%async_computation.15 | async-start | bytes 2097152 | tf_op jit(solution)/shard_map/psum | solution.py:146
  311.2 109.9 %all-reduce.53.cloned.1.call-start = ((), (), s32[]{:S(2)}) async-start(), calls=%async_computation.16 | async-start | bytes 2097152 | tf_op jit(solution)/shard_map/psum | solution.py:146
  369.8 199.8 %reduce-scatter.25.cloned.1.call-start = ((), (), s32[]{:S(2)}) async-start(), calls=%async_computation.18 | async-start | bytes 589824 | tf_op jit(solution)/shard_map/reduce_scatter | solution.py:447
  535.9 71.2 %reduce-scatter.23.cloned.1.call-start = ((), (), s32[]{:S(2)}) async-start(), calls=%async_computation.17 | async-start | bytes 589824 | tf_op jit(solution)/shard_map/reduce_scatter | solution.py:441
  538.7 96.6 %all-gather.19.cloned.1.call-start = ((), (), s32[]{:S(2)}) async-start(), calls=%async_computation.31 | async-start | bytes 1769472 | tf_op jit(solution)/shard_map/all_gather | solution.py:30
  550.4 189.8 %all-reduce.55.cloned.1.call-start = ((), (), s32[]{:S(2)}) async-start(), calls=%async_computation.19 | async-start | bytes 2097152 | tf_op jit(solution)/shard_map/psum | solution.py:146
  665.2 13.5 collective-permute-start.2
  686.3 113.2 %all-reduce.57.cloned.1.call-start = ((), (), s32[]{:S(2)}) async-start(), calls=%async_computation.20 | async-start | bytes 2097152 | tf_op jit(solution)/shard_map/psum | solution.py:146
  748.2 211.8 %reduce-scatter.29.cloned.1.call-start = ((), (), s32[]{:S(2)}) async-start(), calls=%async_computation.22 | async-start | bytes 589824 | tf_op jit(solution)/shard_map/reduce_scatter | solution.py:447
  899.9 71.9 %reduce-scatter.27.cloned.1.call-start = ((), (), s32[]{:S(2)}) async-start(), calls=%async_computation.21 | async-start | bytes 589824 | tf_op jit(solution)/shard_map/reduce_scatter | solution.py:441
  902.6 113.7 %all-gather.21.cloned.1.call-start = ((), (), s32[]{:S(2)}) async-start(), calls=%async_computation.32 | async-start | bytes 1769472 | tf_op jit(solution)/shard_map/all_gather | solution.py:30
  915.1 406.0 %reduce-scatter.45.cloned.1.call-start = ((), (), s32[]{:S(2)}) async-start(), calls=%async_computation.34 | async-start | bytes 2359296
  1016.1 349.8 %reduce-scatter.31.cloned.1.call-start = ((), (), s32[]{:S(2)}) async-start(), calls=%async_computation.23 | async-start | bytes 2359296 | tf_op jit(solution)/shard_map/reduce_scatter | solution.py:558
  1046.2 3.1 collective-permute-start.3
  1051.4 405.1 %reduce-scatter.33.cloned.1.call-start = ((), (), s32[]{:S(2)}) async-start(), calls=%async_computation.24 | async-start | bytes 73728 | tf_op jit(solution)/shard_map/reduce_scatter | solution.py:552
  1079.7 430.7 %all-reduce.59.cloned.1.call-start = ((), (), s32[]{:S(2)}) async-start(), calls=%async_computation.36 | async-start | bytes 5242880 | tf_op jit(solution)/shard_map/psum | solution.py:146
  1084.6 281.6 %copy-start.94 = (bf16[256,512]{1,0:T(8,128)(2,1)S(1)}, bf16[256,512]{1,0:T(8,128)(2,1)}, u32[]{:S(2)}) copy-start(bf16[256,512]{1,0:T(8,128)(2,1)} %copy-done.93) | copy-start | bytes 786436
  1084.6 281.6 %copy-start.96 = (bf16[256,512]{1,0:T(8,128)(2,1)S(1)}, bf16[256,512]{1,0:T(8,128)(2,1)}, u32[]{:S(2)}) copy-start(bf16[256,512]{1,0:T(8,128)(2,1)} %copy-done.95) | copy-start | bytes 786436
  1084.6 281.6 %copy-start.155 = (f32[256]{0:T(256)S(1)}, f32[256]{0:T(256)}, u32[]{:S(2)}) copy-start(f32[256]{0:T(256)} %copy-done.154) | copy-start | bytes 3076
  1365.9 218.6 %reduce-scatter.47.cloned.1.call-start = ((), (), s32[]{:S(2)}) async-start(), calls=%async_computation.35 | async-start | bytes 9437184
  1407.8 241.8 %reduce-scatter.43.cloned.1.call-start = ((), (), s32[]{:S(2)}) async-start(), calls=%async_computation.33 | async-start | bytes 7077888
  1442.0 247.7 %reduce-scatter.37.cloned.1.call-start = ((), (), s32[]{:S(2)}) async-start(), calls=%async_computation.26 | async-start | bytes 1179648 | tf_op jit(solution)/shard_map/reduce_scatter | solution.py:553
  1444.7 285.2 %reduce-scatter.39.cloned.1.call-start = ((), (), s32[]{:S(2)}) async-start(), calls=%async_computation.27 | async-start | bytes 1179648 | tf_op jit(solution)/shard_map/reduce_scatter | solution.py:555
  1446.4 334.0 %reduce-scatter.35.cloned.1.call-start = ((), (), s32[]{:S(2)}) async-start(), calls=%async_computation.25 | async-start | bytes 3538944 | tf_op jit(solution)/shard_map/reduce_scatter | solution.py:554
  1449.7 385.9 %reduce-scatter.41.cloned.1.call-start = ((), (), s32[]{:S(2)}) async-start(), calls=%async_computation.28 | async-start | bytes 4718592 | tf_op jit(solution)/shard_map/reduce_scatter | solution.py:557
  1588.0 248.3 %copy-start.141 = (f32[2,128,2,128]{3,2,1,0:T(2,128)S(1)}, f32[2,128,2,128]{3,2,1,0:T(2,128)}, u32[]{:S(2)}) copy-start(f32[2,128,2,128]{3,2,1,0:T(2,128)} %get-tuple-element.1922) | copy-start | bytes 786436
  (285 other events, 3414.1 us)
Sparse Core Ops, SparseCore 0:
  58.8 26.0 all-gather.14
  111.8 52.2 all-reduce.46
  169.9 51.2 all-reduce.48
  254.8 25.0 all-gather.16
  311.3 50.6 all-reduce.50
  369.9 51.1 all-reduce.52
  536.0 33.5 reduce-scatter.24
  573.0 34.1 reduce-scatter.22
  609.6 25.6 all-gather.18
  686.5 53.7 all-reduce.54
  748.3 51.1 all-reduce.56
  900.0 33.5 reduce-scatter.28
  937.0 34.7 reduce-scatter.26
  973.5 25.8 all-gather.20
  1016.2 304.9 reduce-scatter.44
  1324.6 41.2 reduce-scatter.30
  1369.3 31.4 reduce-scatter.32
  1405.2 105.1 all-reduce.58
  1514.2 70.2 reduce-scatter.46
  1587.8 61.7 reduce-scatter.42
  1653.6 36.0 reduce-scatter.36
  1693.8 36.0 reduce-scatter.38
  1734.2 46.2 reduce-scatter.34
  1784.2 51.3 reduce-scatter.40
where the time goes:
time: 1860 us; the launch traced here: 1840 us
  waiting for transfers between devices  972 us (52%)
  local copies, waits for them, and re-layouts  357 us (19%)
  matrix products  216 us (12%)
  other arithmetic  157 us (8%)
  blocking collectives  102 us (5%)
  between operations  18.6 us (1%)
    psum x7, waiting for transfers between devices, sum_heads(): return lax.psum(partial_sum, 'wa')  338 us
    unnamed x27, waiting for transfers between devices  325 us
    unnamed x616, local copies, waits for them, and re-layouts  83.8 us
    dynamic_update_slice x64, local copies, waits for them, and re-layouts, per_device(): lax.scan(back_block, jnp.zeros((query_rows, HEAD_SIZE), jnp.float32), jnp...  78.6 us
    dynamic_update_slice x2, local copies, waits for them, and re-layouts, per_device(): lax.dynamic_update_slice_in_dim(jnp.zeros((MODEL_WIDTH, 2, KEY_VALUE_HEAD...  63.5 us
    reduce_scatter x1, waiting for transfers between devices, per_device(): lax.psum_scatter(big_all[6], 'seq', scatter_dimension=2, tiled=True)  55.1 us
    reduce_scatter x1, waiting for transfers between devices, per_device(): lax.psum_scatter(big_all[3], 'seq', scatter_dimension=2, tiled=True)  50.6 us
    reduce_scatter x2, waiting for transfers between devices, per_device(): lax.psum_scatter(key_terms.reshape(seq_count * tok_rows, HEAD_SIZE), 'seq...  47.6 us
  transfers between devices with their start and end apart: 28, of which 20 were waited for; matrix products, arithmetic and copies ran while one was open for 21% of the time, Pallas kernels for 0%

commit v1 on v0

v1 whole, which is shorter than its diff:
```python
import math

import jax
import jax.numpy as jnp
from jax import lax
from jax.experimental import pallas as pl
from jax.experimental.pallas import tpu as pltpu
from jax.sharding import PartitionSpec as P

MODEL_WIDTH = 1024
HEAD_SIZE = 64
NS = 128
KC = 4
QUERY_HEADS = 8
KEY_VALUE_HEADS = 2
LAYER_COUNT = 2
DIRECT_MOST = 8

eps = 1e-05
theta = 10000.0
neg_big = -1e30
score_scale = 1.0 / math.sqrt(HEAD_SIZE)

BF = jnp.bfloat16
F32 = jnp.float32
HI = lax.Precision.HIGHEST


def mm(a, b):
    return lax.dot_general(
        a.astype(BF), b.astype(BF), (((1,), (0,)), ((), ())), preferred_element_type=F32
    )


def mm_nt(a, b):
    return lax.dot_general(
        a.astype(BF), b.astype(BF), (((1,), (1,)), ((), ())), preferred_element_type=F32
    )


def mm_tn(a, b):
    return lax.dot_general(
        a.astype(BF), b.astype(BF), (((0,), (0,)), ((), ())), preferred_element_type=F32
    )


def mm_hi(a, b):
    return jnp.dot(a, b, precision=HI, preferred_element_type=F32)


def iota(shape, dim):
    return lax.broadcasted_iota(jnp.int32, shape, dim)


def sigmoid(v):
    return 1.0 / (1.0 + jnp.exp(-v))


def from_earlier(block):
    n = lax.axis_size("seq")
    if n <= DIRECT_MOST:
        return [
            lax.ppermute(block, "seq", [(i, i + d) for i in range(n - d)]) for d in range(1, n)
        ]
    here = lax.axis_index("seq")
    every = lax.all_gather(block, "seq")
    return [
        jnp.where(here >= d, every[(here - d) % n], jnp.zeros_like(block)) for d in range(1, n)
    ]


def from_later(block):
    n = lax.axis_size("seq")
    if n <= DIRECT_MOST:
        return [
            lax.ppermute(block, "seq", [(i + d, i) for i in range(n - d)]) for d in range(1, n)
        ]
    here = lax.axis_index("seq")
    every = lax.all_gather(block, "seq")
    return [
        jnp.where(here + d < n, every[(here + d) % n], jnp.zeros_like(block)) for d in range(1, n)
    ]


def to_earlier(blocks):
    n = lax.axis_size("seq")
    if n <= DIRECT_MOST:
        return [
            lax.ppermute(blocks[d - 1], "seq", [(i + d, i) for i in range(n - d)])
            for d in range(1, n)
        ]
    here = lax.axis_index("seq")
    stacked = jnp.stack([jnp.zeros_like(blocks[0])] + list(blocks))
    places = jnp.arange(n)
    placed = jnp.where((places < here)[:, None, None], stacked[(here - places) % n], 0)
    return [lax.psum_scatter(placed, "seq", scatter_dimension=0, tiled=True)[0]]


def scatter_rows(blocks):
    n = lax.axis_size("seq")
    if n <= DIRECT_MOST:
        got = [
            lax.ppermute(blocks[d], "seq", [(i, (i + d) % n) for i in range(n)])
            for d in range(1, n)
        ]
        total = blocks[0].astype(F32)
        for part in got:
            total = total + part.astype(F32)
        return total
    return lax.psum_scatter(blocks[0], "seq", scatter_dimension=0, tiled=True).astype(F32)


def gather_wa(block):
    n = lax.axis_size("wa")
    return [block] + [
        lax.ppermute(block, "wa", [((i + d) % n, i) for i in range(n)]) for d in range(1, n)
    ]


def scatter_wa(blocks):
    n = lax.axis_size("wa")
    return [blocks[0]] + [
        lax.ppermute(blocks[d], "wa", [(i, (i + d) % n) for i in range(n)]) for d in range(1, n)
    ]


def sum_seq(block):
    n = lax.axis_size("seq")
    if n > DIRECT_MOST:
        return lax.psum(block, "seq")
    total = block
    for d in range(1, n):
        total = total + lax.ppermute(block, "seq", [(i, (i + d) % n) for i in range(n)])
    return total


def layer_of(array, layer):
    return (array, layer)


def kernel_call(name, body, outs, args, scratch=(), flops=0, bytes_accessed=0):
    in_specs, arrays = [], []
    for item in args:
        if isinstance(item, tuple):
            array, layer = item
            rest = array.ndim - 1
            spec = pl.BlockSpec(
                (None,) + array.shape[1:], lambda i, layer=layer, rest=rest: (layer,) + (0,) * rest
            )
        else:
            array = item
            if array.ndim == 1:
                spec = pl.BlockSpec(memory_space=pltpu.SMEM)
            else:
                spec = pl.BlockSpec(array.shape, lambda i, rest=array.ndim: (0,) * rest)
        in_specs.append(spec)
        arrays.append(array)
    out_shape = [jax.ShapeDtypeStruct(shape, kind) for shape, kind in outs]
    out_specs = [
        pl.BlockSpec(shape, lambda i, rest=len(shape): (0,) * rest) for shape, kind in outs
    ]
    if not bytes_accessed:
        bytes_accessed = sum(math.prod(s) * jnp.dtype(k).itemsize for s, k in outs) + sum(
            a.size * a.dtype.itemsize for a in arrays
        )
    return pl.pallas_call(
        body,
        grid=(1,),
        in_specs=in_specs,
        out_specs=out_specs,
        out_shape=out_shape,
        scratch_shapes=list(scratch),
        compiler_params=pltpu.CompilerParams(vmem_limit_bytes=48 * 1024 * 1024),
        cost_estimate=pl.CostEstimate(
            flops=flops, bytes_accessed=bytes_accessed, transcendentals=0
        ),
        name=name,
    )(*arrays)


def ordered(me_ref, parts, nat_ref):
    n = len(parts)
    rows = parts[0].shape[0]
    for d in range(n):
        at = pl.multiple_of(lax.rem(me_ref[0] + d, n) * rows, rows)
        nat_ref[pl.ds(at, rows), :] = parts[d][...]


def rotated(me_ref, nat_ref, blocks):
    n = len(blocks)
    rows = blocks[0].shape[0]
    for d in range(n):
        at = pl.multiple_of(lax.rem(me_ref[0] + d, n) * rows, rows)
        blocks[d][...] = nat_ref[pl.ds(at, rows), :].astype(blocks[d].dtype)


def halves_swapped(v):
    width = v.shape[1]
    half = HEAD_SIZE // 2
    first = iota(v.shape, 1) % HEAD_SIZE < half
    return jnp.where(first, pltpu.roll(v, width - half, 1), pltpu.roll(v, half, 1))


def expand(v, width):
    k = v.shape[1]
    pick = (iota((k, width), 1) // HEAD_SIZE == iota((k, width), 0)).astype(F32)
    return mm_hi(v, pick)


def head_sum(v):
    width = v.shape[1]
    pick = (iota((width, 128), 0) // HEAD_SIZE == iota((width, 128), 1)).astype(F32)
    return mm_hi(v, pick)


def decay_rows(block_decay):
    high = block_decay.astype(BF).astype(F32)
    low = block_decay - high
    row = iota((16, 128), 0)
    return jnp.where(row == 0, high, jnp.where(row == 1, low, 0.0)).astype(BF)


def fold_states(packs, inner):
    heads = inner // HEAD_SIZE
    state = jnp.zeros((inner, NS), F32)
    for pack in reversed(packs):
        tail = pack[inner : inner + 16, :].astype(F32)
        decay = tail[0:1, :] + tail[1:2, :]
        full = jnp.concatenate(
            [jnp.broadcast_to(decay[:, h : h + 1], (HEAD_SIZE, NS)) for h in range(heads)], axis=0
        )
        state = state * full + pack[:inner, :].astype(F32)
    return state


def norm_first(hidden, gain):
    rows, width = hidden.shape

    def body(h_ref, g_ref, n_ref):
        h = h_ref[...]
        scale = lax.rsqrt(jnp.mean(h * h, axis=-1, keepdims=True) + eps)
        n_ref[...] = (h * scale * g_ref[...]).astype(BF)

    return kernel_call("norm_first", body, [((rows, width), BF)], [hidden, gain])[0]


def norm_step(parts, hidden, gain):
    rows, width = hidden.shape
    n = len(parts)

    def body(*refs):
        h_ref, g_ref, out_ref, n_ref = refs[n:]
        total = refs[0][...]
        for part in refs[1:n]:
            total = total + part[...].astype(F32)
        h = h_ref[...] + total
        out_ref[...] = h
        scale = lax.rsqrt(jnp.mean(h * h, axis=-1, keepdims=True) + eps)
        n_ref[...] = (h * scale * g_ref[...]).astype(BF)

    return kernel_call(
        "norm_step", body, [((rows, width), F32), ((rows, width), BF)], [*parts, hidden, gain]
    )


def norm_back(parts, hidden, gain, grad):
    rows, width = hidden.shape
    n = len(parts)

    def body(*refs):
        h_ref, g_ref, grad_ref, out_ref, b_ref, gain_ref = refs[n:]
        total = refs[0][...]
        for part in refs[1:n]:
            total = total + part[...].astype(F32)
        h = h_ref[...]
        scale = lax.rsqrt(jnp.mean(h * h, axis=-1, keepdims=True) + eps)
        unit = h * scale
        through = total * g_ref[...]
        out = grad_ref[...] + scale * (
            through - unit * jnp.mean(through * unit, axis=-1, keepdims=True)
        )
        out_ref[...] = out
        b_ref[...] = out.astype(BF)
        gain_ref[...] = jnp.sum(total * unit, axis=0, keepdims=True)

    return kernel_call(
        "norm_back",
        body,
        [((rows, width), F32), ((rows, width), BF), ((1, width), F32)],
        [*parts, hidden, gain, grad],
    )


def keys_values(me, parts, kvw, cos_kv, sin_kv):
    n = len(parts)
    rows, width = parts[0].shape
    tokens = n * rows

    def body(*refs):
        me_ref = refs[0]
        w_ref, c_ref, s_ref, nat_ref, kv_ref, edge_ref = refs[1 + n :]
        ordered(me_ref, refs[1 : 1 + n], nat_ref)
        raw = mm(nat_ref[...], w_ref[...])
        kv_ref[...] = (raw * c_ref[...] + halves_swapped(raw) * s_ref[...]).astype(BF)
        edge_ref[...] = nat_ref[tokens - 16 :, :]

    return kernel_call(
        "keys_values",
        body,
        [((tokens, width), BF), ((tokens, 128), BF), ((16, width), BF)],
        [me, *parts, kvw, cos_kv, sin_kv],
        flops=2 * tokens * width * 128,
    )


def mixer_front(nat, edge, wzx, wbc, wdt, wq, conv_w, hp, tok, cos_q, sin_q):
    tokens, width = nat.shape
    inner = wzx[0].shape[2] // 2
    mix = inner + 2 * NS

    def body(
        nat_ref, edge_ref, wzx_ref, wbc_ref, wdt_ref, wq_ref, cw_ref, hp_ref, tok_ref, c_ref, s_ref,
        gate_ref, pad_ref, act_ref, slope_ref, hd_ref, q2_ref, pack_ref,
    ):
        x = nat_ref[...]
        e = edge_ref[...]
        gate_ref[...] = mm(x, wzx_ref[:, :inner])
        pad_ref[16:, :inner] = mm(x, wzx_ref[:, inner:])
        pad_ref[16:, inner:] = mm(x, wbc_ref[...])
        pad_ref[:16, :inner] = mm(e, wzx_ref[:, inner:])
        pad_ref[:16, inner:] = mm(e, wbc_ref[...])
        q = mm(x, wq_ref[...])
        q = (q * c_ref[...] + halves_swapped(q) * s_ref[...]).astype(BF).astype(F32)
        lane = iota((tokens, 128), 1)
        q2_ref[:tokens, :] = jnp.where(lane < HEAD_SIZE, q, 0.0).astype(BF)
        q2_ref[tokens:, :] = jnp.where(
            lane < HEAD_SIZE, pltpu.roll(q, HEAD_SIZE, 1), 0.0
        ).astype(BF)
        tk = tok_ref[...]
        conv = jnp.broadcast_to(cw_ref[KC : KC + 1, :], (tokens, mix))
        for j in range(KC):
            shifted = pad_ref[16 - (KC - 1) + j : 16 - (KC - 1) + j + tokens, :]
            conv = conv + cw_ref[j : j + 1, :] * shifted * tk[:, j : j + 1]
        sg = sigmoid(conv)
        act = conv * sg
        act_ref[...] = act
        slope_ref[...] = sg * (1.0 + conv * (1.0 - sg))
        r = mm(x, wdt_ref[...]) + hp_ref[0:1, :]
        dt = jnp.maximum(r, 0.0) + jnp.log1p(jnp.exp(-jnp.abs(r)))
        log_decay = -dt * jnp.exp(hp_ref[1:2, :])
        lower = (iota((tokens, tokens), 0) >= iota((tokens, tokens), 1)).astype(F32)
        cum = mm_hi(lower, log_decay)
        hd_ref[0] = r
        hd_ref[1] = dt
        hd_ref[2] = cum
        last = cum[tokens - 1 :, :]
        to_last = jnp.where(tk[:, 5:6] > 0.5, jnp.exp(last - cum), 0.0)
        scaled = act[:, :inner] * expand(dt * to_last, inner)
        pack_ref[:inner, :] = mm_tn(scaled, act[:, inner : inner + NS]).astype(BF)
        pack_ref[inner:, :] = decay_rows(jnp.exp(last) * tk[tokens - 1 :, 4:5])

    return kernel_call(
        "mixer_front",
        body,
        [
            ((tokens, inner), F32),
            ((tokens + 16, mix), F32),
            ((tokens, mix), F32),
            ((tokens, mix), F32),
            ((3, tokens, 128), F32),
            ((2 * tokens, 128), BF),
            ((inner + 16, NS), BF),
        ],
        [nat, edge, wzx, wbc, wdt, wq, conv_w, hp, tok, cos_q, sin_q],
        flops=2 * tokens * width * 1280,
    )


def allowed_pair(segc, segr, tokens, steps_back):
    heads = segc.shape[0] // tokens
    row = iota((heads * tokens, tokens), 0) % tokens
    column = iota((heads * tokens, tokens), 1)
    return (segc == segr) & (column - tokens * steps_back <= row)


def within_decay(cum, cum_t, h, allowed):
    return jnp.exp(jnp.where(allowed, cum[:, h : h + 1] - cum_t[h : h + 1, :], neg_big))


def attend(kvs, q2, segc, segrel, blocks, act, hd, hp, inner):
    n = len(kvs)
    tokens = kvs[0].shape[0]
    rows = q2.shape[0]

    def body(*refs):
        (q2_ref, segc_ref, segr_ref, nb_ref, act_ref, hd_ref, hp_ref) = refs[n : n + 7]
        o2_ref, lse_ref, flat_ref, y_ref, kv_ref = refs[n + 7 :]
        for d in range(n):
            kv_ref[d] = refs[d][...]
        q = q2_ref[...]
        seg_own = segc_ref[...]
        seg_two = jnp.concatenate([seg_own] * (rows // tokens), axis=0)

        def step(d, carry):
            top, total, out = carry
            kv = kv_ref[d]
            allowed = allowed_pair(seg_two, segr_ref[d], tokens, d)
            scores = jnp.where(allowed, mm_nt(q, kv) * score_scale, neg_big)
            new_top = jnp.maximum(top, jnp.max(scores, axis=1, keepdims=True))
            weights = jnp.where(allowed, jnp.exp(scores - new_top), 0.0)
            shrink = jnp.exp(top - new_top)
            return (
                new_top,
                total * shrink + jnp.sum(weights, axis=1, keepdims=True),
                out * shrink + mm(weights, kv),
            )

        top, total, out = lax.fori_loop(
            0,
            nb_ref[0],
            step,
            (
                jnp.full((rows, 1), neg_big, F32),
                jnp.zeros((rows, 1), F32),
                jnp.zeros((rows, 128), F32),
            ),
        )
        out = out / total
        o2_ref[...] = out
        lse_ref[...] = jnp.broadcast_to(top + jnp.log(total), (rows, 128))
        lane = iota((tokens, 128), 1)
        flat_ref[...] = jnp.where(
            lane < HEAD_SIZE, pltpu.roll(out[:tokens], HEAD_SIZE, 1), out[tokens:]
        ).astype(BF)
        act_all = act_ref[...]
        b_mat = act_all[:, inner : inner + NS]
        c_mat = act_all[:, inner + NS :]
        both = mm_nt(c_mat, b_mat)
        dt, cum = hd_ref[1], hd_ref[2]
        cum_t = cum.T
        allowed = allowed_pair(seg_own, segr_ref[0], tokens, 0)
        scaled = act_all[:, :inner] * expand(dt, inner)
        skip = expand(hp_ref[...], inner)[2:3, :]
        for p in range(inner // 128):
            cols = slice(128 * p, 128 * (p + 1))
            pair = [
                mm(within_decay(cum, cum_t, 2 * p + k, allowed) * both, scaled[:, cols])
                for k in range(2)
            ]
            y_ref[:, cols] = (
                jnp.where(lane < HEAD_SIZE, pair[0], pair[1])
                + skip[:, cols] * act_all[:, cols]
            )

    return kernel_call(
        "attend",
        body,
        [
            ((rows, 128), F32),
            ((rows, 128), F32),
            ((tokens, 128), BF),
            ((tokens, inner), F32),
        ],
        [*kvs, q2, segc, segrel, blocks, act, hd, hp],
        scratch=[pltpu.VMEM((n, tokens, 128), BF)],
        flops=2 * rows * tokens * 128 * 2 * n,
    )


def mixer_out(me, packs, y_local, act, hd, tok, gate, flat, wout, wao, wa_count):
    m = len(packs)
    tokens, inner = y_local.shape
    width = wout[0].shape[2]
    rows = tokens // wa_count

    def body(*refs):
        me_ref = refs[0]
        y_ref, act_ref, hd_ref, tok_ref, gate_ref, flat_ref, wout_ref, wao_ref = refs[
            1 + m : 9 + m
        ]
        state_ref, yy_ref, gated_ref = refs[9 + m : 12 + m]
        blocks = refs[12 + m : 12 + m + wa_count]
        full_ref = refs[-1]
        state = fold_states([r[...] for r in refs[1 : 1 + m]], inner)
        state_ref[...] = state
        decay_in = jnp.exp(hd_ref[2]) * tok_ref[:, 4:5]
        y = y_ref[...] + mm_nt(act_ref[:, inner + NS :], state) * expand(decay_in, inner)
        yy_ref[...] = y
        gate_raw = gate_ref[...]
        gated = (y * gate_raw * sigmoid(gate_raw)).astype(BF)
        gated_ref[...] = gated
        full_ref[...] = mm(gated, wout_ref[...]) + mm(flat_ref[...], wao_ref[...])
        rotated(me_ref, full_ref, blocks)

    return kernel_call(
        "mixer_out",
        body,
        [((inner, NS), F32), ((tokens, inner), F32), ((tokens, inner), BF)]
        + [((rows, width), F32)]
        + [((rows, width), BF)] * (wa_count - 1),
        [me, *packs, y_local, act, hd, tok, gate, flat, wout, wao],
        scratch=[pltpu.VMEM((tokens, width), F32)],
        flops=2 * tokens * width * 512,
    )


def feed_forward(parts, wgu, wdown):
    n = len(parts)
    rows, width = parts[0].shape
    tokens = n * rows
    hidden = wdown[0].shape[1]

    def body(*refs):
        wgu_ref, wdown_ref, n_ref, gu_ref, act_ref = refs[n : n + 5]
        blocks = refs[n + 5 : n + 5 + n]
        for d in range(n):
            n_ref[d * rows : (d + 1) * rows, :] = refs[d][...]
        x = n_ref[...]
        gate = mm(x, wgu_ref[:, :hidden])
        up = mm(x, wgu_ref[:, hidden:])
        gu_ref[:, :hidden] = gate
        gu_ref[:, hidden:] = up
        act = (gate * sigmoid(gate) * up).astype(BF)
        act_ref[...] = act
        for d in range(n):
            blocks[d][...] = mm(act[d * rows : (d + 1) * rows], wdown_ref[...]).astype(
                blocks[d].dtype
            )

    return kernel_call(
        "feed_forward",
        body,
        [((tokens, width), BF), ((tokens, 2 * hidden), F32), ((tokens, hidden), BF)]
        + [((rows, width), F32)]
        + [((rows, width), BF)] * (n - 1),
        [*parts, wgu, wdown],
        flops=2 * tokens * width * 3 * hidden,
    )


def feed_back(parts, gu, wgu, wdown):
    n = len(parts)
    rows, width = parts[0].shape
    tokens = n * rows
    hidden = wdown[0].shape[1]

    def body(*refs):
        gu_ref, wgu_ref, wdown_ref, gb_ref, dgu_ref = refs[n : n + 5]
        blocks = refs[n + 5 : n + 5 + n]
        for d in range(n):
            gb_ref[d * rows : (d + 1) * rows, :] = refs[d][...]
        d_act = mm_nt(gb_ref[...], wdown_ref[...])
        gate = gu_ref[:, :hidden]
        up = gu_ref[:, hidden:]
        sg = sigmoid(gate)
        dgu_ref[:, :hidden] = (d_act * up * sg * (1.0 + gate * (1.0 - sg))).astype(BF)
        dgu_ref[:, hidden:] = (d_act * gate * sg).astype(BF)
        for d in range(n):
            blocks[d][...] = mm_nt(dgu_ref[d * rows : (d + 1) * rows, :], wgu_ref[...]).astype(
                blocks[d].dtype
            )

    return kernel_call(
        "feed_back",
        body,
        [((tokens, width), BF), ((tokens, 2 * hidden), BF)]
        + [((rows, width), F32)]
        + [((rows, width), BF)] * (n - 1),
        [*parts, gu, wgu, wdown],
        flops=2 * tokens * width * 3 * hidden,
    )


def weight_grads(here, pairs, n):
    width = pairs[0][0].shape[1]
    columns = sum(right.shape[1] for left, right in pairs)
    flat = [a for pair in pairs for a in pair]
    direct = n <= DIRECT_MOST
    blocks = n if direct else 1
    rows = width // blocks

    def body(*refs):
        here_ref = refs[0]
        outs = refs[1 + len(flat) :]
        for d in range(blocks):
            start = 0
            for k in range(len(pairs)):
                left, right = refs[1 + 2 * k], refs[2 + 2 * k]
                wide = right.shape[1]
                if direct:
                    at = pl.multiple_of(lax.rem(here_ref[0] + d, n) * rows, rows)
                    piece = left[:, pl.ds(at, rows)]
                else:
                    piece = left[...]
                outs[d][:, start : start + wide] = mm_tn(piece, right[...]).astype(outs[d].dtype)
                start += wide

    return kernel_call(
        "weight_grads",
        body,
        [((rows, columns), F32 if direct and d == 0 else BF) for d in range(blocks)],
        [here, *flat],
        flops=2 * pairs[0][0].shape[0] * width * columns,
    )


def mixer_grad_in(me, parts, wout, wao, gate, y, act, hd, tok, o2):
    n = len(parts)
    rows, width = parts[0].shape
    tokens, inner = y.shape

    def body(*refs):
        me_ref = refs[0]
        wout_ref, wao_ref, gate_ref, y_ref, act_ref, hd_ref, tok_ref, o2_ref = refs[1 + n : 9 + n]
        nat_ref, dy_ref, dgate_ref, pack_ref, da2_ref, delta_ref = refs[9 + n :]
        ordered(me_ref, refs[1 : 1 + n], nat_ref)
        mb = nat_ref[...]
        d_gated = mm_nt(mb, wout_ref[...])
        gate_raw = gate_ref[...]
        sg = sigmoid(gate_raw)
        dy = d_gated * gate_raw * sg
        dy_ref[...] = dy
        dgate_ref[...] = (
            d_gated * y_ref[...] * sg * (1.0 + gate_raw * (1.0 - sg))
        ).astype(BF)
        cum = hd_ref[2]
        decay_in = jnp.exp(cum) * tok_ref[:, 4:5]
        pack_ref[:inner, :] = mm_tn(
            dy * expand(decay_in, inner), act_ref[:, inner + NS :]
        ).astype(BF)
        pack_ref[inner:, :] = decay_rows(decay_in[tokens - 1 :, :])
        d_attn = mm_nt(mb, wao_ref[...])
        lane = iota((tokens, 128), 1)
        da2 = jnp.concatenate(
            [
                jnp.where(lane >= HEAD_SIZE, pltpu.roll(d_attn, HEAD_SIZE, 1), 0.0),
                jnp.where(lane >= HEAD_SIZE, d_attn, 0.0),
            ],
            axis=0,
        )
        da2_ref[...] = da2.astype(BF)
        delta_ref[...] = jnp.broadcast_to(
            jnp.sum(da2 * o2_ref[...], axis=1, keepdims=True), da2.shape
        )

    return kernel_call(
        "mixer_grad_in",
        body,
        [
            ((tokens, width), BF),
            ((tokens, inner), F32),
            ((tokens, inner), BF),
            ((inner + 16, NS), BF),
            ((2 * tokens, 128), BF),
            ((2 * tokens, 128), F32),
        ],
        [me, *parts, wout, wao, gate, y, act, hd, tok, o2],
        flops=2 * tokens * width * 512,
    )


def attend_back(kvs, q2, da2, delta, lse, segc, segrel, blocks, cos_q, sin_q):
    n = len(kvs)
    tokens = kvs[0].shape[0]
    rows = q2.shape[0]

    def body(*refs):
        (q2_ref, da_ref, delta_ref, lse_ref, segc_ref, segr_ref, nb_ref, c_ref, s_ref) = refs[
            n : n + 9
        ]
        dq_ref = refs[n + 9]
        outs = refs[n + 10 : n + 10 + n]
        kv_ref, dkv_ref = refs[n + 10 + n :]
        for d in range(n):
            kv_ref[d] = refs[d][...]
        for d in range(1, n):
            dkv_ref[d] = jnp.zeros((tokens, 128), F32)
        q = q2_ref[...]
        da = da_ref[...]
        lse_col = lse_ref[:, 0:1]
        delta_col = delta_ref[:, 0:1]
        seg_two = jnp.concatenate([segc_ref[...]] * (rows // tokens), axis=0)

        def step(d, dq):
            kv = kv_ref[d]
            allowed = allowed_pair(seg_two, segr_ref[d], tokens, d)
            scores = mm_nt(q, kv) * score_scale
            probs = jnp.exp(jnp.where(allowed, scores - lse_col, neg_big))
            d_scores = (probs * (mm_nt(da, kv) - delta_col)).astype(BF)
            dkv_ref[d] = mm_tn(d_scores, q) * score_scale + mm_tn(probs, da)
            return dq + mm(d_scores, kv)

        dq = lax.fori_loop(0, nb_ref[0], step, jnp.zeros((rows, 128), F32)) * score_scale
        lane = iota((tokens, 128), 1)
        flat = jnp.where(lane < HEAD_SIZE, dq[:tokens], pltpu.roll(dq[tokens:], HEAD_SIZE, 1))
        dq_ref[...] = (flat * c_ref[...] - halves_swapped(flat) * s_ref[...]).astype(BF)
        for d in range(n):
            outs[d][...] = dkv_ref[d].astype(outs[d].dtype)

    return kernel_call(
        "attend_back",
        body,
        [((tokens, 128), BF), ((tokens, 128), F32)] + [((tokens, 128), BF)] * (n - 1),
        [*kvs, q2, da2, delta, lse, segc, segrel, blocks, cos_q, sin_q],
        scratch=[pltpu.VMEM((n, tokens, 128), BF), pltpu.VMEM((n, tokens, 128), F32)],
        flops=2 * rows * tokens * 128 * 5 * n,
    )


def mixer_grad(packs, state_in, dy, act, slope, pad, hd, tok, segc, segrel, hp, conv_w):
    m = len(packs)
    tokens, inner = dy.shape
    mix = act.shape[1]

    def body(*refs):
        (
            state_ref, dy_ref, act_ref, slope_ref, pad_ref, hd_ref, tok_ref, segc_ref, segr_ref,
            hp_ref, cw_ref, dmix_ref, tail_ref, edge_ref, ddt_ref, gconv_ref, ghead_ref,
            dconv_ref, dpad_ref, dxs_ref,
        ) = refs[m:]
        later = fold_states([r[...] for r in refs[:m]], inner)
        state = state_ref[...]
        tk = tok_ref[...]
        act_all = act_ref[...]
        x = act_all[:, :inner]
        b_mat = act_all[:, inner : inner + NS]
        c_mat = act_all[:, inner + NS :]
        dy_all = dy_ref[...]
        r, dt, cum = hd_ref[0], hd_ref[1], hd_ref[2]
        cum_t = cum.T
        last = cum[tokens - 1 :, :]
        to_last = jnp.where(tk[:, 5:6] > 0.5, jnp.exp(last - cum), 0.0)
        decay_in = jnp.exp(cum) * tk[:, 4:5]
        dt_wide = expand(dt, inner)
        last_wide = expand(to_last, inner)
        in_wide = expand(decay_in, inner)
        xs = x * dt_wide
        allowed = allowed_pair(segc_ref[...], segr_ref[0], tokens, 0)
        both = mm_nt(c_mat, b_mat)
        lane = iota((tokens, 128), 1)
        lane_row = iota((128, tokens), 0)
        d_both = jnp.zeros((tokens, tokens), F32)
        d_cum = jnp.zeros((tokens, 128), F32)
        d_cum_t = jnp.zeros((128, tokens), F32)
        for p in range(inner // 128):
            cols = slice(128 * p, 128 * (p + 1))
            xs_pair = xs[:, cols].astype(BF)
            dy_pair = dy_all[:, cols]
            pieces = []
            for k in range(2):
                h = 2 * p + k
                decay = within_decay(cum, cum_t, h, allowed)
                weight = decay * both
                mine = (lane >= HEAD_SIZE) if k else (lane < HEAD_SIZE)
                d_weight = mm_nt(jnp.where(mine, dy_pair, 0.0), xs_pair)
                d_both = d_both + d_weight * decay
                flow = d_weight * weight
                d_cum = d_cum + jnp.where(lane == h, jnp.sum(flow, axis=1, keepdims=True), 0.0)
                d_cum_t = d_cum_t + jnp.where(
                    lane_row == h, jnp.sum(flow, axis=0, keepdims=True), 0.0
                )
                pieces.append(mm_tn(weight, dy_pair))
            dxs_ref[:, cols] = jnp.where(lane < HEAD_SIZE, pieces[0], pieces[1])
        from_state = mm_nt(b_mat, later)
        d_xs = dxs_ref[...] + from_state * last_wide
        dy_in = dy_all * in_wide
        inflow = mm_nt(c_mat, state)
        d_c = mm(d_both, b_mat) + mm(dy_in, state)
        d_b = mm_tn(d_both, c_mat) + mm(xs * last_wide, later)
        carried = head_sum(from_state * xs * last_wide)
        d_cum = d_cum - d_cum_t.T + head_sum(dy_in * inflow) - carried
        row_sum = jnp.sum(later * state, axis=1, keepdims=True)
        pick = (iota((inner, 128), 0) // HEAD_SIZE == iota((inner, 128), 1)).astype(F32)
        d_decay = jnp.sum(row_sum * pick, axis=0, keepdims=True)
        d_last = jnp.sum(carried, axis=0, keepdims=True) + decay_in[tokens - 1 :, :] * d_decay
        d_cum = d_cum + jnp.where(iota((tokens, 128), 0) == tokens - 1, d_last, 0.0)
        upper = (iota((tokens, tokens), 0) <= iota((tokens, tokens), 1)).astype(F32)
        d_log = mm_hi(upper, d_cum)
        rate = jnp.exp(hp_ref[1:2, :])
        d_dt = head_sum(d_xs * x) - rate * d_log
        d_r = d_dt * sigmoid(r)
        ddt_ref[...] = d_r.astype(BF)
        g_bias = jnp.sum(d_r, axis=0, keepdims=True)
        g_log = -jnp.sum(d_log * dt, axis=0, keepdims=True) * rate
        g_skip = jnp.sum(head_sum(dy_all * x), axis=0, keepdims=True)
        row8 = iota((8, 128), 0)
        ghead_ref[...] = jnp.where(
            row8 == 0, g_bias, jnp.where(row8 == 1, g_log, jnp.where(row8 == 2, g_skip, 0.0))
        )
        skip = expand(hp_ref[...], inner)[2:3, :]
        dconv_ref[:, :inner] = (dy_all * skip + d_xs * dt_wide) * slope_ref[:, :inner]
        dconv_ref[:, inner : inner + NS] = d_b * slope_ref[:, inner : inner + NS]
        dconv_ref[:, inner + NS :] = d_c * slope_ref[:, inner + NS :]
        dpad_ref[...] = jnp.zeros((tokens + 16, mix), F32)
        gconv_ref[...] = jnp.zeros((8, mix), F32)
        dconv = dconv_ref[...]
        gconv_ref[KC : KC + 1, :] = jnp.sum(dconv, axis=0, keepdims=True)
        for j in range(KC):
            at = 16 - (KC - 1) + j
            used = dconv * tk[:, j : j + 1]
            gconv_ref[j : j + 1, :] = jnp.sum(
                used * pad_ref[at : at + tokens, :], axis=0, keepdims=True
            )
            dpad_ref[at : at + tokens, :] = (
                dpad_ref[at : at + tokens, :] + used * cw_ref[j : j + 1, :]
            )
        dmix_ref[...] = dpad_ref[16:, :].astype(BF)
        tail_ref[...] = dpad_ref[tokens:, :]
        edge_ref[...] = dpad_ref[8:16, :]

    return kernel_call(
        "mixer_grad",
        body,
        [
            ((tokens, mix), BF),
            ((16, mix), F32),
            ((8, mix), F32),
            ((tokens, 128), BF),
            ((8, mix), F32),
            ((8, 128), F32),
        ],
        [*packs, state_in, dy, act, slope, pad, hd, tok, segc, segrel, hp, conv_w],
        scratch=[
            pltpu.VMEM((tokens, mix), F32),
            pltpu.VMEM((tokens + 16, mix), F32),
            pltpu.VMEM((tokens, inner), F32),
        ],
        flops=2 * tokens * tokens * 128 * 24,
    )


def grads_out(
    me, dgate, dmix, tail, next_edge, ddt, dq, dkv_own, dkv_got, cos_kv, sin_kv,
    wzx, wbc, wdt, wq, kvw, wa_count,
):
    m = len(dkv_got)
    tokens, inner = dgate.shape
    mix = dmix.shape[1]
    width = wzx[0].shape[1]
    rows = tokens // wa_count
    wide = inner + mix + 3 * 128

    def body(*refs):
        me_ref = refs[0]
        got = refs[1 : 1 + m]
        (
            dgate_ref, dmix_ref, tail_ref, edge_ref, ddt_ref, dq_ref, own_ref, c_ref, s_ref,
            wzx_ref, wbc_ref, wdt_ref, wq_ref, kvw_ref, right_ref,
        ) = refs[1 + m : 16 + m]
        blocks = refs[16 + m : 16 + m + wa_count]
        full_ref = refs[-1]
        right_ref[:, :inner] = dgate_ref[...]
        right_ref[: tokens - 16, inner : inner + mix] = dmix_ref[: tokens - 16, :]
        right_ref[tokens - 16 :, inner : inner + mix] = (
            tail_ref[...]
            + jnp.concatenate([jnp.zeros((8, mix), F32), edge_ref[...]], axis=0)
        ).astype(BF)
        at = inner + mix
        right_ref[:, at : at + 128] = dq_ref[...]
        dkv = own_ref[...]
        for part in got:
            dkv = dkv + part[...].astype(F32)
        right_ref[:, at + 128 : at + 256] = (
            dkv * c_ref[...] - halves_swapped(dkv) * s_ref[...]
        ).astype(BF)
        right_ref[:, at + 256 :] = ddt_ref[...]
        full_ref[...] = (
            mm_nt(right_ref[:, : 2 * inner], wzx_ref[...])
            + mm_nt(right_ref[:, 2 * inner : at], wbc_ref[...])
            + mm_nt(right_ref[:, at : at + 128], wq_ref[...])
            + mm_nt(right_ref[:, at + 128 : at + 256], kvw_ref[...])
            + mm_nt(right_ref[:, at + 256 :], wdt_ref[...])
        )
        rotated(me_ref, full_ref, blocks)

    return kernel_call(
        "grads_out",
        body,
        [((tokens, wide), BF), ((rows, width), F32)] + [((rows, width), BF)] * (wa_count - 1),
        [
            me, *dkv_got, dgate, dmix, tail, next_edge, ddt, dq, dkv_own, cos_kv, sin_kv,
            wzx, wbc, wdt, wq, kvw,
        ],
        scratch=[pltpu.VMEM((tokens, width), F32)],
        flops=2 * tokens * width * wide,
    )


def per_device(
    x_in,
    d_out,
    segment_ids,
    norm_gains,
    w_zx,
    w_bc,
    w_dt,
    conv_x,
    conv_bc,
    dt_bias,
    a_log,
    d_skip,
    w_out,
    w_q,
    key_value_weight,
    w_ao,
    w_gu,
    w_down,
):
    seq_count = lax.axis_size("seq")
    wa_count = lax.axis_size("wa")
    tokens, width = x_in.shape
    rows = tokens // wa_count
    seq_here = lax.axis_index("seq")
    wa_here = lax.axis_index("wa")
    start_row = seq_here * tokens
    inner = w_zx.shape[3]
    heads = w_dt.shape[2]
    hidden = w_gu.shape[3]
    query_local = w_q.shape[2] // HEAD_SIZE
    group = QUERY_HEADS // KEY_VALUE_HEADS
    kv_head = wa_here * query_local // group
    me = wa_here.astype(jnp.int32).reshape(1)
    here = seq_here.astype(jnp.int32).reshape(1)

    seg_blocks = segment_ids.reshape(seq_count, tokens)
    seg_here = lax.dynamic_slice_in_dim(segment_ids, start_row, tokens)
    seg_padded = jnp.concatenate([jnp.full((KC - 1,), -1, jnp.int32), segment_ids])
    seg_edge = lax.dynamic_slice_in_dim(seg_padded, start_row, KC - 1)
    seg_full = jnp.concatenate([seg_edge, seg_here])
    steps = jnp.arange(seq_count, dtype=jnp.int32)
    segrel = jnp.where(
        (steps <= seq_here)[:, None], seg_blocks[(seq_here - steps) % seq_count], -1
    )
    blocks_used = (
        1 + jnp.sum((segrel[1:, tokens - 1] == seg_here[0]).astype(jnp.int32))
    ).astype(jnp.int32).reshape(1)
    segrel = segrel[:, None, :]
    segc = seg_here[:, None]
    columns = [(seg_full[j : j + tokens] == seg_here).astype(F32) for j in range(KC)]
    columns.append((seg_here == seg_edge[KC - 2]).astype(F32))
    columns.append((seg_here == seg_here[tokens - 1]).astype(F32))
    tok = jnp.pad(jnp.stack(columns, axis=1), ((0, 0), (0, 128 - len(columns))))
    half = HEAD_SIZE // 2
    frequency = jnp.exp(jnp.arange(half, dtype=F32) * (-math.log(theta) / half))
    positions = (start_row + jnp.arange(tokens, dtype=jnp.int32)).astype(F32)
    angles = positions[:, None] * frequency[None, :]
    cosine, sine = jnp.cos(angles), jnp.sin(angles)
    cos_q = jnp.concatenate([cosine] * 4, axis=1)
    sin_q = jnp.concatenate([-sine, sine, -sine, sine], axis=1)
    ones = jnp.ones((tokens, HEAD_SIZE), F32)
    cos_kv = jnp.concatenate([cosine, cosine, ones], axis=1)
    sin_kv = jnp.concatenate([-sine, sine, 0.0 * ones], axis=1)

    wzx_all = w_zx.reshape(LAYER_COUNT, width, 2 * inner)
    wgu_all = w_gu.reshape(LAYER_COUNT, width, 2 * hidden)
    wdt_all = jnp.pad(w_dt, ((0, 0), (0, 0), (0, 128 - heads)))
    kvw_all = lax.dynamic_slice_in_dim(
        key_value_weight, kv_head * HEAD_SIZE, HEAD_SIZE, axis=3
    ).reshape(LAYER_COUNT, width, 2 * HEAD_SIZE)
    conv_all = jnp.pad(
        jnp.concatenate([conv_x, conv_bc], axis=2), ((0, 0), (0, 8 - (KC + 1)), (0, 0))
    )
    hp_all = jnp.pad(
        jnp.stack([dt_bias, a_log, d_skip], axis=1), ((0, 0), (0, 5), (0, 128 - heads))
    )

    def own_rows(array):
        return lax.dynamic_slice_in_dim(array, wa_here * rows, rows)

    h = own_rows(x_in)
    normed = norm_first(h, norm_gains[0, 0][None, :])
    saved = []
    for layer in range(LAYER_COUNT):
        wzx, wbc, wdt, wq = [(a, layer) for a in (wzx_all, w_bc, wdt_all, w_q)]
        kvw, conv_w, hp = [(a, layer) for a in (kvw_all, conv_all, hp_all)]
        wout, wao, wgu, wdown = [(a, layer) for a in (w_out, w_ao, wgu_all, w_down)]
        nat, kv, edge = keys_values(me, gather_wa(normed), kvw, cos_kv, sin_kv)
        n = seq_count
        edge = lax.ppermute(edge, "seq", [(i, i + 1) for i in range(n - 1)])
        kvs = [kv] + from_earlier(kv)
        gate, pad, act, slope, hd, q2, pack = mixer_front(
            nat, edge, wzx, wbc, wdt, wq, conv_w, hp, tok, cos_q, sin_q
        )
        packs = from_earlier(pack)
        o2, lse, flat, y_local = attend(
            kvs, q2, segc, segrel, blocks_used, act, hd, hp, inner
        )
        state_in, y, gated, *parts = mixer_out(
            me, packs, y_local, act, hd, tok, gate, flat, wout, wao, wa_count
        )
        mixed, normed_two = norm_step(scatter_wa(parts), h, norm_gains[layer, 1][None, :])
        n2, gu, act_ff, *parts = feed_forward(gather_wa(normed_two), wgu, wdown)
        saved.append(
            (h, nat, kvs, gate, pad, act, slope, hd, q2, o2, lse, flat, state_in, y, gated,
             mixed, n2, gu, act_ff)
        )
        following = norm_gains[min(layer + 1, LAYER_COUNT - 1), 0][None, :]
        h, normed = norm_step(scatter_wa(parts), mixed, following)

    def whole_rows(parts):
        full = jnp.zeros((tokens, width), F32)
        for d, part in enumerate(parts):
            at = (wa_here + d) % wa_count * rows
            full = lax.dynamic_update_slice_in_dim(full, part.astype(F32), at, axis=0)
        return full

    x_out = whole_rows(gather_wa(h.astype(BF)))

    grad = own_rows(d_out)
    grad_parts = [
        lax.dynamic_slice_in_dim(d_out, (wa_here + d) % wa_count * rows, rows).astype(BF)
        for d in range(wa_count)
    ]
    sums = [None] * LAYER_COUNT
    small = [None] * LAYER_COUNT
    for layer in reversed(range(LAYER_COUNT)):
        wzx, wbc, wdt, wq = [(a, layer) for a in (wzx_all, w_bc, wdt_all, w_q)]
        kvw, conv_w, hp = [(a, layer) for a in (kvw_all, conv_all, hp_all)]
        wout, wao, wgu, wdown = [(a, layer) for a in (w_out, w_ao, wgu_all, w_down)]
        (h_in, nat, kvs, gate, pad, act, slope, hd, q2, o2, lse, flat, state_in, y, gated,
         mixed, n2, gu, act_ff) = saved[layer]
        gb, dgu, *parts = feed_back(grad_parts, gu, wgu, wdown)
        parts = scatter_wa(parts)
        sum_ff = scatter_rows(weight_grads(here, [(gb, act_ff), (n2, dgu)], seq_count))
        d_mixed, mixed_b, gain_two = norm_back(
            parts, mixed, norm_gains[layer, 1][None, :], grad
        )
        mb, dy, dgate, pack, da2, delta = mixer_grad_in(
            me, gather_wa(mixed_b), wout, wao, gate, y, act, hd, tok, o2
        )
        packs = from_later(pack)
        dq, dkv_own, *dkv_rest = attend_back(
            kvs, q2, da2, delta, lse, segc, segrel, blocks_used, cos_q, sin_q
        )
        dkv_got = to_earlier(dkv_rest)
        sum_mix = scatter_rows(weight_grads(here, [(mb, gated), (mb, flat)], seq_count))
        dmix, tail, edge_grad, ddt, gconv, ghead = mixer_grad(
            packs, state_in, dy, act, slope, pad, hd, tok, segc, segrel, hp, conv_w
        )
        next_edge = lax.ppermute(
            edge_grad, "seq", [(i + 1, i) for i in range(seq_count - 1)]
        )
        right, *parts = grads_out(
            me, dgate, dmix, tail, next_edge, ddt, dq, dkv_own, dkv_got, cos_kv, sin_kv,
            wzx, wbc, wdt, wq, kvw, wa_count,
        )
        parts = scatter_wa(parts)
        sum_in = scatter_rows(weight_grads(here, [(nat, right)], seq_count))
        grad, grad_b, gain_one = norm_back(
            parts, h_in, norm_gains[layer, 0][None, :], d_mixed
        )
        grad_parts = gather_wa(grad_b)
        sums[layer] = (sum_ff, sum_mix, sum_in)
        small[layer] = (gain_one, gain_two, gconv, ghead)
    d_x = whole_rows(grad_parts)

    gains = [small[layer][k].reshape(width // 128, 128) for layer in range(LAYER_COUNT) for k in (0, 1)]
    convs = [
        jnp.concatenate([small[layer][2][j].reshape(-1, 128) for j in range(KC + 1)])
        for layer in range(LAYER_COUNT)
    ]
    packed = jnp.concatenate(gains + convs + [small[layer][3] for layer in range(LAYER_COUNT)])
    packed = sum_seq(packed)
    gain_rows = 4 * width // 128
    gain_sum = packed[:gain_rows]
    mix = inner + 2 * NS
    conv_sum = packed[gain_rows : gain_rows + LAYER_COUNT * (KC + 1) * (mix // 128)].reshape(
        LAYER_COUNT, KC + 1, mix
    )
    head_part = packed[gain_rows + LAYER_COUNT * (KC + 1) * (mix // 128) :].reshape(
        LAYER_COUNT, 8, 128
    )
    shared = jnp.concatenate(
        [gain_sum, conv_sum[:, :, inner:].reshape(-1, 128)], axis=0
    )
    shared_parts = gather_wa(shared)
    shared = shared_parts[0]
    for part in shared_parts[1:]:
        shared = shared + part
    gain_sum = shared[:gain_rows].reshape(LAYER_COUNT, 2, width)
    g_conv_bc = shared[gain_rows:].reshape(LAYER_COUNT, KC + 1, 2 * NS)

    at = 2 * inner
    after = at + 2 * NS
    every = jnp.stack(
        [
            jnp.concatenate([s[2][:, at:after], s[2][:, after + 128 : after + 256]], axis=1)
            for s in sums
        ]
    ).astype(BF)
    every_parts = gather_wa(every)
    g_bc = sum(part[:, :, : 2 * NS].astype(F32) for part in every_parts)
    kv_columns = []
    for head in range(KEY_VALUE_HEADS):
        total = 0.0
        for d, part in enumerate(every_parts):
            source = (wa_here + d) % wa_count * query_local // group
            total = total + jnp.where(source == head, part[:, :, 2 * NS :].astype(F32), 0.0)
        kv_columns.append(total.reshape(total.shape[0], total.shape[1], 2, HEAD_SIZE))
    g_kv = jnp.concatenate(kv_columns, axis=3)

    block = sums[0][0].shape[0]

    def stacked(pick):
        return jnp.stack([pick(s) for s in sums])

    g_down = stacked(lambda s: s[0][:, :hidden].T)
    g_gu = stacked(lambda s: s[0][:, hidden:].reshape(block, 2, hidden))
    g_out = stacked(lambda s: s[1][:, :inner].T)
    g_ao = stacked(lambda s: s[1][:, inner:].T)
    g_zx = stacked(lambda s: s[2][:, : 2 * inner].reshape(block, 2, inner))
    g_q = stacked(lambda s: s[2][:, after : after + 128])
    g_dt = stacked(lambda s: s[2][:, after + 256 : after + 256 + heads])
    return (
        x_out,
        d_x,
        gain_sum[:, 0],
        gain_sum[:, 1],
        g_zx,
        g_bc,
        g_dt,
        conv_sum[:, :, :inner],
        g_conv_bc,
        head_part[:, 0, :heads],
        head_part[:, 1, :heads],
        head_part[:, 2, :heads],
        g_out,
        g_q,
        g_kv,
        g_ao,
        g_gu,
        g_down,
    )


def solution(mesh):
    return jax.shard_map(
        per_device,
        mesh=mesh,
        in_specs=(
            P("seq", None),
            P("seq", None),
            P(),
            P(),
            P(None, None, None, "wa"),
            P(),
            P(None, None, "wa"),
            P(None, None, "wa"),
            P(),
            P(None, "wa"),
            P(None, "wa"),
            P(None, "wa"),
            P(None, "wa", None),
            P(None, None, "wa"),
            P(),
            P(None, "wa", None),
            P(None, None, None, "wa"),
            P(None, "wa", None),
        ),
        out_specs=(
            P("seq", None),
            P("seq", None),
            P(),
            P(),
            P(None, "seq", None, "wa"),
            P(None, "seq", None),
            P(None, "seq", "wa"),
            P(None, None, "wa"),
            P(),
            P(None, "wa"),
            P(None, "wa"),
            P(None, "wa"),
            P(None, "wa", "seq"),
            P(None, "seq", "wa"),
            P(None, "seq", None, None),
            P(None, "wa", "seq"),
            P(None, "seq", None, "wa"),
            P(None, "wa", "seq"),
        ),
        check_vma=False,
    )
```

time: 1860 us -> 675 us (0.36)
  the two profiles are of different devices: /device:TPU:0 before, /device:TPU:19 now
where the time goes in v1:
time: 675 us; the launch traced here: 664 us
  starting transfers between devices  247 us (37%)
  waiting for transfers between devices  166 us (25%)
  local copies, waits for them, and re-layouts  131 us (19%)
  Pallas kernels  80.9 us (12%)
  other arithmetic  33.7 us (5%)
    pallas_call x35, Pallas kernels, kernel_call(): pl.pallas_call(body, grid=(1,), in_specs=in_specs, out_specs=out_specs, o...  80.9 us
    unnamed x626, local copies, waits for them, and re-layouts  79.7 us
    ppermute x42, waiting for transfers between devices, scatter_rows(): lax.ppermute(blocks[d], 'seq', [(i, (i + d) % n) for i in range(n)])  64.4 us
    ppermute x42, starting transfers between devices, scatter_rows(): lax.ppermute(blocks[d], 'seq', [(i, (i + d) % n) for i in range(n)])  59.3 us
    ppermute x33, waiting for transfers between devices, gather_wa(): lax.ppermute(block, 'wa', [((i + d) % n, i) for i in range(n)])  55.9 us
    ppermute x28, starting transfers between devices, from_earlier(): lax.ppermute(block, 'seq', [(i, i + d) for i in range(n - d)])  52.6 us
    ppermute x24, waiting for transfers between devices, scatter_wa(): lax.ppermute(blocks[d], 'wa', [(i, (i + d) % n) for i in range(n)])  45.1 us
    ppermute x33, starting transfers between devices, gather_wa(): lax.ppermute(block, 'wa', [((i + d) % n, i) for i in range(n)])  43 us
  transfers between devices with their start and end apart: 166, of which 39 were waited for; matrix products, arithmetic and copies ran while one was open for 13% of the time, Pallas kernels for 9%

profile of v1, /device:TPU:19, one launch (start us, length us, event | category | flops | bytes accessed | tf_op | source)
XLA Modules:
  0.0 663.6 jit_solution(15330412944492939550)
XLA Ops:
  20.8 4.2 collective-permute-start.11
  35.4 8.2 %reshape.183.wzx_ref.refs_17_ = bf16[2,1024,768]{2,1,0:T(8,128)(2,1)} reshape(bf16[2,1024,2,384]{3,2,1,0:T(2,128)(2,1)} %param.22) | data formatting | bytes 6291456 | tf_op jit(solution)/shard_map/reshape | solution.py:954
  51.7 5.0 mixer_front.2
  94.7 5.2 collective-permute-done.19.refs_2_
  108.0 7.8 %reshape.186.refs_4_.refs_5_ = bf16[2,1024,1024]{2,1,0:T(8,128)(2,1)} reshape(bf16[2,1024,2,512]{3,2,1,0:T(2,128)(2,1)} %param.34) | data formatting | bytes 8388608 | tf_op jit(solution)/shard_map/reshape | solution.py:955
  131.1 4.3 collective-permute-done.26.refs_3_
  140.2 8.0 %collective-permute-done.28.refs_3_ = bf16[64,1024]{1,0:T(8,128)(2,1)S(1)} collective-permute-done((bf16[64,1024]{1,0:T(8,128)(2,1)S(1)}, bf16[64,1024]{1,0:T(8,128)(2,1)S(1)}, u32[]{:S(2)}, u32[]{:S(2)}) %collective-permute-start.28) | collective-permute-done | bytes 131104 | tf_op jit(solution)/shard_map/ppermute | solution.py:116
  154.8 7.8 %collective-permute-start.39 = (bf16[256,128]{1,0:T(8,128)(2,1)S(1)}, bf16[256,128]{1,0:T(8,128)(2,1)S(1)}, u32[]{:S(2)}, u32[]{:S(2)}) collective-permute-start(bf16[256,128]{1,0:T(8,128)(2,1)S(1)} %get-tuple-element.228.refs_0_), channel_id=1, source_target_pairs={{0,8},{4,12},{8,16},{12,20},{16,24},{20,28},{1,9},{5,13},{9,17},{1... | collective-permute-start | bytes 196616 | tf_op jit(solution)/shard_map/ppermute | solution.py:63
  165.9 4.3 mixer_front.3
  178.3 6.8 %collective-permute-start.33 = (bf16[400,128]{1,0:T(8,128)(2,1)S(1)}, bf16[400,128]{1,0:T(8,128)(2,1)S(1)}, u32[]{:S(2)}, u32[]{:S(2)}) collective-permute-start(bf16[400,128]{1,0:T(8,128)(2,1)S(1)} %get-tuple-element.227), channel_id=1, source_target_pairs={{0,12},{4,16},{8,20},{12,24},{16,28},{1,13},{5,17},{9,21},{13,25},... | collective-permute-start | bytes 307208 | tf_op jit(solution)/shard_map/ppermute | solution.py:63
  201.9 5.8 collective-permute-done.47.refs_3_
  214.2 7.9 %collective-permute-done.49.refs_2_ = bf16[64,1024]{1,0:T(8,128)(2,1)} collective-permute-done((bf16[64,1024]{1,0:T(8,128)(2,1)}, bf16[64,1024]{1,0:T(8,128)(2,1)}, u32[]{:S(2)}, u32[]{:S(2)}) %collective-permute-start.49) | collective-permute-done | bytes 131104 | tf_op jit(solution)/shard_map/ppermute | solution.py:116
  229.7 4.8 feed_back.2
  242.0 4.6 collective-permute-done.59.refs_3_
  255.0 10.7 %collective-permute-done.61.refs_3_ = bf16[64,1024]{1,0:T(8,128)(2,1)S(1)} collective-permute-done((bf16[64,1024]{1,0:T(8,128)(2,1)S(1)}, bf16[64,1024]{1,0:T(8,128)(2,1)S(1)}, u32[]{:S(2)}, u32[]{:S(2)}) %collective-permute-start.61) | collective-permute-done | bytes 131104 | tf_op jit(solution)/shard_map/ppermute | solution.py:116
  275.0 5.7 collective-permute-start.63
  280.7 5.0 collective-permute-start.64
  320.0 6.2 mixer_grad.2
  341.1 5.1 collective-permute-start.146
  348.7 5.4 collective-permute-start.148
  365.4 4.2 collective-permute-start.161
  379.4 5.2 feed_back.3
  401.7 14.0 %collective-permute-done.163 = bf16[128,1536]{1,0:T(8,128)(2,1)S(1)} collective-permute-done((bf16[128,1536]{1,0:T(8,128)(2,1)S(1)}, bf16[128,1536]{1,0:T(8,128)(2,1)S(1)}, u32[]{:S(2)}, u32[]{:S(2)}) %collective-permute-start.163) | collective-permute-done | bytes 393248 | tf_op jit(solution)/shard_map/ppermute | solution.py:103
  418.7 7.4 %collective-permute-done.129 = bf16[128,1408]{1,0:T(8,128)(2,1)S(1)} collective-permute-done((bf16[128,1408]{1,0:T(8,128)(2,1)S(1)}, bf16[128,1408]{1,0:T(8,128)(2,1)S(1)}, u32[]{:S(2)}, u32[]{:S(2)}) %collective-permute-start.129) | collective-permute-done | bytes 360480 | tf_op jit(solution)/shard_map/ppermute | solution.py:103
  448.9 7.1 %collective-permute-done.132 = bf16[128,1408]{1,0:T(8,128)(2,1)S(1)} collective-permute-done((bf16[128,1408]{1,0:T(8,128)(2,1)}, bf16[128,1408]{1,0:T(8,128)(2,1)S(1)}, u32[]{:S(2)}, u32[]{:S(2)}) %collective-permute-start.132) | collective-permute-done | bytes 360480 | tf_op jit(solution)/shard_map/ppermute | solution.py:103
  480.7 5.9 mixer_grad.3
  532.9 9.4 %collective-permute-done.155 = bf16[128,1536]{1,0:T(8,128)(2,1)S(1)} collective-permute-done((bf16[128,1536]{1,0:T(8,128)(2,1)}, bf16[128,1536]{1,0:T(8,128)(2,1)S(1)}, u32[]{:S(2)}, u32[]{:S(2)}) %collective-permute-start.155) | collective-permute-done | bytes 393248 | tf_op jit(solution)/shard_map/ppermute | solution.py:103
  564.5 4.8 collective-permute-done.106.refs_2_
  615.7 20.6 %collective-permute-done.125 = bf16[128,1408]{1,0:T(8,128)(2,1)S(1)} collective-permute-done((bf16[128,1408]{1,0:T(8,128)(2,1)S(1)}, bf16[128,1408]{1,0:T(8,128)(2,1)S(1)}, u32[]{:S(2)}, u32[]{:S(2)}) %collective-permute-start.125) | collective-permute-done | bytes 360480 | tf_op jit(solution)/shard_map/ppermute | solution.py:103
  638.0 4.7 collective-permute-start.136
  647.0 8.2 %collective-permute-done.136 = bf16[2,128,384]{2,1,0:T(8,128)(2,1)S(1)} collective-permute-done((bf16[2,128,384]{2,1,0:T(8,128)(2,1)S(1)}, bf16[2,128,384]{2,1,0:T(8,128)(2,1)S(1)}, u32[]{:S(2)}, u32[]{:S(2)}) %collective-permute-start.136) | collective-permute-done | bytes 196640 | tf_op jit(solution)/shard_map/ppermute | solution.py:116
  655.2 4.5 collective-permute-done.137
  (1073 shorter events, 438.9 us)
Async XLA Ops:
  20.8 39.9 %collective-permute-start.11 = (bf16[256,128]{1,0:T(8,128)(2,1)}, bf16[256,128]{1,0:T(8,128)(2,1)}, u32[]{:S(2)}, u32[]{:S(2)}) collective-permute-start(bf16[256,128]{1,0:T(8,128)(2,1)} %get-tuple-element.207.refs_0_), channel_id=1, source_target_pairs={{0,4},{4,8},{8,12},{12,16},{16,20},{20,24},{24,28},{1,5},{5,9},{9,... | collective-permute-start | bytes 196616 | tf_op jit(solution)/shard_map/ppermute | solution.py:63
  25.0 36.3 %collective-permute-start.12 = (bf16[256,128]{1,0:T(8,128)(2,1)}, bf16[256,128]{1,0:T(8,128)(2,1)}, u32[]{:S(2)}, u32[]{:S(2)}) collective-permute-start(bf16[256,128]{1,0:T(8,128)(2,1)} %get-tuple-element.207.refs_0_), channel_id=1, source_target_pairs={{0,8},{4,12},{8,16},{12,20},{16,24},{20,28},{1,9},{5,13},{9,17},{1... | collective-permute-start | bytes 196616 | tf_op jit(solution)/shard_map/ppermute | solution.py:63
  28.2 33.9 %collective-permute-start.13 = (bf16[256,128]{1,0:T(8,128)(2,1)}, bf16[256,128]{1,0:T(8,128)(2,1)}, u32[]{:S(2)}, u32[]{:S(2)}) collective-permute-start(bf16[256,128]{1,0:T(8,128)(2,1)} %get-tuple-element.207.refs_0_), channel_id=1, source_target_pairs={{0,12},{4,16},{8,20},{12,24},{16,28},{1,13},{5,17},{9,21},{13,25},... | collective-permute-start | bytes 196616 | tf_op jit(solution)/shard_map/ppermute | solution.py:63
  30.1 32.6 %collective-permute-start.14 = (bf16[256,128]{1,0:T(8,128)(2,1)}, bf16[256,128]{1,0:T(8,128)(2,1)}, u32[]{:S(2)}, u32[]{:S(2)}) collective-permute-start(bf16[256,128]{1,0:T(8,128)(2,1)} %get-tuple-element.207.refs_0_), channel_id=1, source_target_pairs={{0,16},{4,20},{8,24},{12,28},{1,17},{5,21},{9,25},{13,29},{2,18},{... | collective-permute-start | bytes 196616 | tf_op jit(solution)/shard_map/ppermute | solution.py:63
  251.5 34.2 %collective-permute-start.51 = (bf16[64,1024]{1,0:T(8,128)(2,1)S(1)}, bf16[64,1024]{1,0:T(8,128)(2,1)S(1)}, u32[]{:S(2)}, u32[]{:S(2)}) collective-permute-start(bf16[64,1024]{1,0:T(8,128)(2,1)S(1)} %get-tuple-element.242), channel_id=1, source_target_pairs={{0,1},{1,2},{2,3},{3,0},{4,5},{5,6},{6,7},{7,4},{8,9},{9,10},{10,1... | collective-permute-start | bytes 393224 | tf_op jit(solution)/shard_map/ppermute | solution.py:123
  253.2 35.1 %collective-permute-start.52 = (bf16[64,1024]{1,0:T(8,128)(2,1)S(1)}, bf16[64,1024]{1,0:T(8,128)(2,1)S(1)}, u32[]{:S(2)}, u32[]{:S(2)}) collective-permute-start(bf16[64,1024]{1,0:T(8,128)(2,1)S(1)} %get-tuple-element.243), channel_id=1, source_target_pairs={{0,2},{1,3},{2,0},{3,1},{4,6},{5,7},{6,4},{7,5},{8,10},{9,11},{10,... | collective-permute-start | bytes 393224 | tf_op jit(solution)/shard_map/ppermute | solution.py:123
  254.2 36.1 %collective-permute-start.53 = (bf16[64,1024]{1,0:T(8,128)(2,1)S(1)}, bf16[64,1024]{1,0:T(8,128)(2,1)S(1)}, u32[]{:S(2)}, u32[]{:S(2)}) collective-permute-start(bf16[64,1024]{1,0:T(8,128)(2,1)S(1)} %get-tuple-element.244), channel_id=1, source_target_pairs={{0,3},{1,0},{2,1},{3,2},{4,7},{5,4},{6,5},{7,6},{8,11},{9,8},{10,9... | collective-permute-start | bytes 393224 | tf_op jit(solution)/shard_map/ppermute | solution.py:123
  356.7 28.8 %collective-permute-start.159 = (bf16[128,1536]{1,0:T(8,128)(2,1)S(1)}, bf16[128,1536]{1,0:T(8,128)(2,1)S(1)}, u32[]{:S(2)}, u32[]{:S(2)}) collective-permute-start(bf16[128,1536]{1,0:T(8,128)(2,1)S(1)} %get-tuple-element.383), channel_id=1, source_target_pairs={{0,4},{4,8},{8,12},{12,16},{16,20},{20,24},{24,28},{28,0},{1,5},{5... | collective-permute-start | bytes 1179656 | tf_op jit(solution)/shard_map/ppermute | solution.py:103
  358.2 29.7 %collective-permute-start.160 = (bf16[128,1536]{1,0:T(8,128)(2,1)S(1)}, bf16[128,1536]{1,0:T(8,128)(2,1)}, u32[]{:S(2)}, u32[]{:S(2)}) collective-permute-start(bf16[128,1536]{1,0:T(8,128)(2,1)S(1)} %get-tuple-element.384), channel_id=1, source_target_pairs={{0,8},{4,12},{8,16},{12,20},{16,24},{20,28},{24,0},{28,4},{1,9},{5... | collective-permute-start | bytes 1179656 | tf_op jit(solution)/shard_map/ppermute | solution.py:103
  365.4 25.9 %collective-permute-start.161 = (bf16[128,1536]{1,0:T(8,128)(2,1)S(1)}, bf16[128,1536]{1,0:T(8,128)(2,1)S(1)}, u32[]{:S(2)}, u32[]{:S(2)}) collective-permute-start(bf16[128,1536]{1,0:T(8,128)(2,1)S(1)} %get-tuple-element.385), channel_id=1, source_target_pairs={{0,12},{4,16},{8,20},{12,24},{16,28},{20,0},{24,4},{28,8},{1,13},{... | collective-permute-start | bytes 1179656 | tf_op jit(solution)/shard_map/ppermute | solution.py:103
  391.3 24.4 %collective-permute-start.163 = (bf16[128,1536]{1,0:T(8,128)(2,1)S(1)}, bf16[128,1536]{1,0:T(8,128)(2,1)S(1)}, u32[]{:S(2)}, u32[]{:S(2)}) collective-permute-start(bf16[128,1536]{1,0:T(8,128)(2,1)S(1)} %get-tuple-element.387), channel_id=1, source_target_pairs={{0,20},{4,24},{8,28},{12,0},{16,4},{20,8},{24,12},{28,16},{1,21},{... | collective-permute-start | bytes 1179656 | tf_op jit(solution)/shard_map/ppermute | solution.py:103
  392.5 23.2 %collective-permute-start.164 = (bf16[128,1536]{1,0:T(8,128)(2,1)S(1)}, bf16[128,1536]{1,0:T(8,128)(2,1)S(1)}, u32[]{:S(2)}, u32[]{:S(2)}) collective-permute-start(bf16[128,1536]{1,0:T(8,128)(2,1)S(1)} %get-tuple-element.388), channel_id=1, source_target_pairs={{0,24},{4,28},{8,0},{12,4},{16,8},{20,12},{24,16},{28,20},{1,25},{... | collective-permute-start | bytes 1179656 | tf_op jit(solution)/shard_map/ppermute | solution.py:103
  399.3 26.8 %collective-permute-start.129 = (bf16[128,1408]{1,0:T(8,128)(2,1)S(1)}, bf16[128,1408]{1,0:T(8,128)(2,1)S(1)}, u32[]{:S(2)}, u32[]{:S(2)}) collective-permute-start(bf16[128,1408]{1,0:T(8,128)(2,1)S(1)} %get-tuple-element.340), channel_id=1, source_target_pairs={{0,8},{4,12},{8,16},{12,20},{16,24},{20,28},{24,0},{28,4},{1,9},{5... | collective-permute-start | bytes 1081352 | tf_op jit(solution)/shard_map/ppermute | solution.py:103
  415.7 26.1 %collective-permute-start.130 = (bf16[128,1408]{1,0:T(8,128)(2,1)}, bf16[128,1408]{1,0:T(8,128)(2,1)}, u32[]{:S(2)}, u32[]{:S(2)}) collective-permute-start(bf16[128,1408]{1,0:T(8,128)(2,1)} %get-tuple-element.341), channel_id=1, source_target_pairs={{0,12},{4,16},{8,20},{12,24},{16,28},{20,0},{24,4},{28,8},{1,13},{... | collective-permute-start | bytes 1081352 | tf_op jit(solution)/shard_map/ppermute | solution.py:103
  415.7 27.5 %collective-permute-start.131 = (bf16[128,1408]{1,0:T(8,128)(2,1)}, bf16[128,1408]{1,0:T(8,128)(2,1)}, u32[]{:S(2)}, u32[]{:S(2)}) collective-permute-start(bf16[128,1408]{1,0:T(8,128)(2,1)} %get-tuple-element.342), channel_id=1, source_target_pairs={{0,16},{4,20},{8,24},{12,28},{16,0},{20,4},{24,8},{28,12},{1,17},{... | collective-permute-start | bytes 1081352 | tf_op jit(solution)/shard_map/ppermute | solution.py:103
  431.8 24.3 %collective-permute-start.132 = (bf16[128,1408]{1,0:T(8,128)(2,1)}, bf16[128,1408]{1,0:T(8,128)(2,1)S(1)}, u32[]{:S(2)}, u32[]{:S(2)}) collective-permute-start(bf16[128,1408]{1,0:T(8,128)(2,1)} %copy-done.213), channel_id=1, source_target_pairs={{0,20},{4,24},{8,28},{12,0},{16,4},{20,8},{24,12},{28,16},{1,21},{... | collective-permute-start | bytes 1081352 | tf_op jit(solution)/shard_map/ppermute | solution.py:103
  431.9 26.1 %collective-permute-start.133 = (bf16[128,1408]{1,0:T(8,128)(2,1)}, bf16[128,1408]{1,0:T(8,128)(2,1)S(1)}, u32[]{:S(2)}, u32[]{:S(2)}) collective-permute-start(bf16[128,1408]{1,0:T(8,128)(2,1)} %copy-done.212), channel_id=1, source_target_pairs={{0,24},{4,28},{8,0},{12,4},{16,8},{20,12},{24,16},{28,20},{1,25},{... | collective-permute-start | bytes 1081352 | tf_op jit(solution)/shard_map/ppermute | solution.py:103
  433.7 29.6 %collective-permute-start.134 = (bf16[128,1408]{1,0:T(8,128)(2,1)}, bf16[128,1408]{1,0:T(8,128)(2,1)S(1)}, u32[]{:S(2)}, u32[]{:S(2)}) collective-permute-start(bf16[128,1408]{1,0:T(8,128)(2,1)} %copy-done.211), channel_id=1, source_target_pairs={{0,28},{4,0},{8,4},{12,8},{16,12},{20,16},{24,20},{28,24},{1,29},{... | collective-permute-start | bytes 1081352 | tf_op jit(solution)/shard_map/ppermute | solution.py:103
  441.8 25.4 %collective-permute-start.100 = (bf16[400,128]{1,0:T(8,128)(2,1)S(1)}, bf16[400,128]{1,0:T(8,128)(2,1)S(1)}, u32[]{:S(2)}, u32[]{:S(2)}) collective-permute-start(bf16[400,128]{1,0:T(8,128)(2,1)S(1)} %get-tuple-element.303), channel_id=1, source_target_pairs={{16,0},{20,4},{24,8},{28,12},{17,1},{21,5},{25,9},{29,13},{18,2},{... | collective-permute-start | bytes 307208 | tf_op jit(solution)/shard_map/ppermute | solution.py:76
  443.2 25.9 %collective-permute-start.101 = (bf16[400,128]{1,0:T(8,128)(2,1)S(1)}, bf16[400,128]{1,0:T(8,128)(2,1)S(1)}, u32[]{:S(2)}, u32[]{:S(2)}) collective-permute-start(bf16[400,128]{1,0:T(8,128)(2,1)S(1)} %get-tuple-element.303), channel_id=1, source_target_pairs={{20,0},{24,4},{28,8},{21,1},{25,5},{29,9},{22,2},{26,6},{30,10},{2... | collective-permute-start | bytes 307208 | tf_op jit(solution)/shard_map/ppermute | solution.py:76
  472.6 37.5 %collective-permute-start.152 = (bf16[128,1536]{1,0:T(8,128)(2,1)}, bf16[128,1536]{1,0:T(8,128)(2,1)}, u32[]{:S(2)}, u32[]{:S(2)}) collective-permute-start(bf16[128,1536]{1,0:T(8,128)(2,1)} %get-tuple-element.371), channel_id=1, source_target_pairs={{0,4},{4,8},{8,12},{12,16},{16,20},{20,24},{24,28},{28,0},{1,5},{5... | collective-permute-start | bytes 1179656 | tf_op jit(solution)/shard_map/ppermute | solution.py:103
  475.2 34.9 %collective-permute-start.153 = (bf16[128,1536]{1,0:T(8,128)(2,1)}, bf16[128,1536]{1,0:T(8,128)(2,1)}, u32[]{:S(2)}, u32[]{:S(2)}) collective-permute-start(bf16[128,1536]{1,0:T(8,128)(2,1)} %get-tuple-element.372), channel_id=1, source_target_pairs={{0,8},{4,12},{8,16},{12,20},{16,24},{20,28},{24,0},{28,4},{1,9},{5... | collective-permute-start | bytes 1179656 | tf_op jit(solution)/shard_map/ppermute | solution.py:103
  503.6 28.9 %collective-permute-start.154 = (bf16[128,1536]{1,0:T(8,128)(2,1)}, bf16[128,1536]{1,0:T(8,128)(2,1)S(1)}, u32[]{:S(2)}, u32[]{:S(2)}) collective-permute-start(bf16[128,1536]{1,0:T(8,128)(2,1)} %copy-done.207), channel_id=1, source_target_pairs={{0,12},{4,16},{8,20},{12,24},{16,28},{20,0},{24,4},{28,8},{1,13},{... | collective-permute-start | bytes 1179656 | tf_op jit(solution)/shard_map/ppermute | solution.py:103
  507.0 35.3 %collective-permute-start.155 = (bf16[128,1536]{1,0:T(8,128)(2,1)}, bf16[128,1536]{1,0:T(8,128)(2,1)S(1)}, u32[]{:S(2)}, u32[]{:S(2)}) collective-permute-start(bf16[128,1536]{1,0:T(8,128)(2,1)} %copy-done.206), channel_id=1, source_target_pairs={{0,16},{4,20},{8,24},{12,28},{16,0},{20,4},{24,8},{28,12},{1,17},{... | collective-permute-start | bytes 1179656 | tf_op jit(solution)/shard_map/ppermute | solution.py:103
  508.1 34.2 %collective-permute-start.156 = (bf16[128,1536]{1,0:T(8,128)(2,1)}, bf16[128,1536]{1,0:T(8,128)(2,1)S(1)}, u32[]{:S(2)}, u32[]{:S(2)}) collective-permute-start(bf16[128,1536]{1,0:T(8,128)(2,1)} %copy-done.205), channel_id=1, source_target_pairs={{0,20},{4,24},{8,28},{12,0},{16,4},{20,8},{24,12},{28,16},{1,21},{... | collective-permute-start | bytes 1179656 | tf_op jit(solution)/shard_map/ppermute | solution.py:103
  510.1 32.3 %collective-permute-start.157 = (bf16[128,1536]{1,0:T(8,128)(2,1)}, bf16[128,1536]{1,0:T(8,128)(2,1)S(1)}, u32[]{:S(2)}, u32[]{:S(2)}) collective-permute-start(bf16[128,1536]{1,0:T(8,128)(2,1)} %copy-done.204), channel_id=1, source_target_pairs={{0,24},{4,28},{8,0},{12,4},{16,8},{20,12},{24,16},{28,20},{1,25},{... | collective-permute-start | bytes 1179656 | tf_op jit(solution)/shard_map/ppermute | solution.py:103
  510.1 33.3 %collective-permute-start.158 = (bf16[128,1536]{1,0:T(8,128)(2,1)}, bf16[128,1536]{1,0:T(8,128)(2,1)S(1)}, u32[]{:S(2)}, u32[]{:S(2)}) collective-permute-start(bf16[128,1536]{1,0:T(8,128)(2,1)} %copy-done.203), channel_id=1, source_target_pairs={{0,28},{4,0},{8,4},{12,8},{16,12},{20,16},{24,20},{28,24},{1,29},{... | collective-permute-start | bytes 1179656 | tf_op jit(solution)/shard_map/ppermute | solution.py:103
  585.6 26.2 %collective-permute-start.121 = (bf16[128,1408]{1,0:T(8,128)(2,1)}, bf16[128,1408]{1,0:T(8,128)(2,1)S(1)}, u32[]{:S(2)}, u32[]{:S(2)}) collective-permute-start(bf16[128,1408]{1,0:T(8,128)(2,1)} %copy-done.210), channel_id=1, source_target_pairs={{0,4},{4,8},{8,12},{12,16},{16,20},{20,24},{24,28},{28,0},{1,5},{5... | collective-permute-start | bytes 1081352 | tf_op jit(solution)/shard_map/ppermute | solution.py:103
  588.2 25.0 %collective-permute-start.122 = (bf16[128,1408]{1,0:T(8,128)(2,1)}, bf16[128,1408]{1,0:T(8,128)(2,1)S(1)}, u32[]{:S(2)}, u32[]{:S(2)}) collective-permute-start(bf16[128,1408]{1,0:T(8,128)(2,1)} %copy-done.209), channel_id=1, source_target_pairs={{0,8},{4,12},{8,16},{12,20},{16,24},{20,28},{24,0},{28,4},{1,9},{5... | collective-permute-start | bytes 1081352 | tf_op jit(solution)/shard_map/ppermute | solution.py:103
  610.5 25.8 %collective-permute-start.125 = (bf16[128,1408]{1,0:T(8,128)(2,1)S(1)}, bf16[128,1408]{1,0:T(8,128)(2,1)S(1)}, u32[]{:S(2)}, u32[]{:S(2)}) collective-permute-start(bf16[128,1408]{1,0:T(8,128)(2,1)S(1)} %get-tuple-element.334), channel_id=1, source_target_pairs={{0,20},{4,24},{8,28},{12,0},{16,4},{20,8},{24,12},{28,16},{1,21},{... | collective-permute-start | bytes 1081352 | tf_op jit(solution)/shard_map/ppermute | solution.py:103
  611.7 24.6 %collective-permute-start.126 = (bf16[128,1408]{1,0:T(8,128)(2,1)S(1)}, bf16[128,1408]{1,0:T(8,128)(2,1)S(1)}, u32[]{:S(2)}, u32[]{:S(2)}) collective-permute-start(bf16[128,1408]{1,0:T(8,128)(2,1)S(1)} %get-tuple-element.335), channel_id=1, source_target_pairs={{0,24},{4,28},{8,0},{12,4},{16,8},{20,12},{24,16},{28,20},{1,25},{... | collective-permute-start | bytes 1081352 | tf_op jit(solution)/shard_map/ppermute | solution.py:103
  613.2 23.1 %collective-permute-start.127 = (bf16[128,1408]{1,0:T(8,128)(2,1)S(1)}, bf16[128,1408]{1,0:T(8,128)(2,1)S(1)}, u32[]{:S(2)}, u32[]{:S(2)}) collective-permute-start(bf16[128,1408]{1,0:T(8,128)(2,1)S(1)} %get-tuple-element.336), channel_id=1, source_target_pairs={{0,28},{4,0},{8,4},{12,8},{16,12},{20,16},{24,20},{28,24},{1,29},{... | collective-permute-start | bytes 1081352 | tf_op jit(solution)/shard_map/ppermute | solution.py:103
  (441 other events, 6214.0 us)

commit v2 on v1

v2 whole, which is shorter than its diff:
```python
import math

import jax
import jax.numpy as jnp
from jax import lax
from jax.experimental import pallas as pl
from jax.experimental.pallas import tpu as pltpu
from jax.sharding import PartitionSpec as P

MODEL_WIDTH = 1024
HEAD_SIZE = 64
NS = 128
KC = 4
QUERY_HEADS = 8
KEY_VALUE_HEADS = 2
LAYER_COUNT = 2
DIRECT_MOST = 8
VMEM_MIB = 48

eps = 1e-05
theta = 10000.0
neg_big = -1e30
score_scale = 1.0 / math.sqrt(HEAD_SIZE)

BF = jnp.bfloat16
F32 = jnp.float32
HI = lax.Precision.HIGHEST


def mm(a, b):
    return lax.dot_general(
        a.astype(BF), b.astype(BF), (((1,), (0,)), ((), ())), preferred_element_type=F32
    )


def mm_nt(a, b):
    return lax.dot_general(
        a.astype(BF), b.astype(BF), (((1,), (1,)), ((), ())), preferred_element_type=F32
    )


def mm_tn(a, b):
    return lax.dot_general(
        a.astype(BF), b.astype(BF), (((0,), (0,)), ((), ())), preferred_element_type=F32
    )


def mm_hi(a, b):
    return jnp.dot(a, b, precision=HI, preferred_element_type=F32)


def iota(shape, dim):
    return lax.broadcasted_iota(jnp.int32, shape, dim)


def sigmoid(v):
    return 1.0 / (1.0 + jnp.exp(-v))


def gather_seq(block):
    return lax.all_gather(block, "seq")


def scatter_rows(blocks):
    n = lax.axis_size("seq")
    if len(blocks) > 1:
        got = [
            lax.ppermute(blocks[d], "seq", [(i, (i + d) % n) for i in range(n)])
            for d in range(1, n)
        ]
        total = blocks[0].astype(F32)
        for part in got:
            total = total + part.astype(F32)
        return total
    return lax.psum_scatter(blocks[0], "seq", scatter_dimension=0, tiled=True).astype(F32)


def gather_wa(block):
    n = lax.axis_size("wa")
    return [block] + [
        lax.ppermute(block, "wa", [(i, (i + d) % n) for i in range(n)]) for d in range(1, n)
    ]


def scatter_wa(blocks):
    n = lax.axis_size("wa")
    return [blocks[0]] + [
        lax.ppermute(blocks[n - d], "wa", [(i, (i + d) % n) for i in range(n)])
        for d in range(1, n)
    ]


def arrive(*refs):
    pass


def kernel_call(name, body, outs, args, scratch=(), flops=0, ties=()):
    in_specs, arrays = [], []
    bytes_accessed = sum(math.prod(s) * jnp.dtype(k).itemsize for s, k in outs)
    for item in args:
        array, layer = item if isinstance(item, tuple) else (item, None)
        arrays.append(array)
        if layer is not None:
            rest = array.ndim - 1
            spec = pl.BlockSpec(
                (None,) + array.shape[1:], lambda i, layer=layer, rest=rest: (layer,) + (0,) * rest
            )
        elif array.ndim == 1:
            spec = pl.BlockSpec(memory_space=pltpu.SMEM)
        else:
            spec = pl.BlockSpec(array.shape, lambda i, rest=array.ndim: (0,) * rest)
        in_specs.append(spec)
        bytes_accessed += array.size * array.dtype.itemsize // (1 if layer is None else array.shape[0])
    count, gap = len(arrays), len(arrays) + len(ties)
    in_specs += [pl.BlockSpec(memory_space=pl.ANY)] * len(ties)

    def whole(*refs):
        body(*refs[:count], *refs[gap:])

    return pl.pallas_call(
        whole,
        grid=(1,),
        in_specs=in_specs,
        out_specs=[
            pl.BlockSpec(shape, lambda i, rest=len(shape): (0,) * rest) for shape, kind in outs
        ],
        out_shape=[jax.ShapeDtypeStruct(shape, kind) for shape, kind in outs],
        scratch_shapes=list(scratch),
        compiler_params=pltpu.CompilerParams(vmem_limit_bytes=VMEM_MIB * 1024 * 1024),
        cost_estimate=pl.CostEstimate(
            flops=flops, bytes_accessed=bytes_accessed, transcendentals=0
        ),
        name=name,
    )(*arrays, *ties)


def ordered(me_ref, parts, nat_ref):
    n = len(parts)
    rows = parts[0].shape[0]
    for d in range(n):
        at = pl.multiple_of(lax.rem(me_ref[0] + n - d, n) * rows, rows)
        nat_ref[pl.ds(at, rows), :] = parts[d][...]


def rotated(me_ref, nat_ref, blocks):
    n = len(blocks)
    rows = blocks[0].shape[0]
    for d in range(n):
        at = pl.multiple_of(lax.rem(me_ref[0] + n - d, n) * rows, rows)
        blocks[d][...] = nat_ref[pl.ds(at, rows), :].astype(blocks[d].dtype)


def halves_swapped(v):
    width = v.shape[1]
    half = HEAD_SIZE // 2
    first = iota(v.shape, 1) % HEAD_SIZE < half
    return jnp.where(first, pltpu.roll(v, width - half, 1), pltpu.roll(v, half, 1))


def expand(v, width):
    k = v.shape[1]
    pick = (iota((k, width), 1) // HEAD_SIZE == iota((k, width), 0)).astype(F32)
    return mm_hi(v, pick)


def head_sum(v):
    width = v.shape[1]
    pick = (iota((width, 128), 0) // HEAD_SIZE == iota((width, 128), 1)).astype(F32)
    return mm_hi(v, pick)


def decay_rows(block_decay):
    high = block_decay.astype(BF).astype(F32)
    low = block_decay - high
    row = iota((16, 128), 0)
    return jnp.where(row == 0, high, jnp.where(row == 1, low, 0.0)).astype(BF)


def fold_states(packs_ref, inner, here, later):
    arrive(packs_ref)
    heads = inner // HEAD_SIZE
    n = packs_ref.shape[0]

    def step(k, state):
        j = n - 1 - k if later else k
        tail = packs_ref[j, inner : inner + 16, :].astype(F32)
        decay = tail[0:1, :] + tail[1:2, :]
        full = jnp.concatenate(
            [jnp.broadcast_to(decay[:, h : h + 1], (HEAD_SIZE, NS)) for h in range(heads)], axis=0
        )
        return state * full + packs_ref[j, :inner, :].astype(F32)

    count = n - 1 - here if later else here
    return lax.fori_loop(0, count, step, jnp.zeros((inner, NS), F32))


def norm_first(hidden, gain):
    rows, width = hidden.shape

    def body(h_ref, g_ref, n_ref):
        h = h_ref[...]
        scale = lax.rsqrt(jnp.mean(h * h, axis=-1, keepdims=True) + eps)
        n_ref[...] = (h * scale * g_ref[...]).astype(BF)

    return kernel_call("norm_first", body, [((rows, width), BF)], [hidden, gain])[0]


def norm_step(parts, hidden, gain, ties=()):
    rows, width = hidden.shape
    n = len(parts)

    def body(*refs):
        h_ref, g_ref, out_ref, n_ref = refs[n:]
        total = refs[0][...]
        for part in refs[1:n]:
            total = total + part[...].astype(F32)
        h = h_ref[...] + total
        out_ref[...] = h
        scale = lax.rsqrt(jnp.mean(h * h, axis=-1, keepdims=True) + eps)
        n_ref[...] = (h * scale * g_ref[...]).astype(BF)

    return kernel_call(
        "norm_step",
        body,
        [((rows, width), F32), ((rows, width), BF)],
        [*parts, hidden, gain],
        ties=ties,
    )


def norm_back(parts, hidden, gain, grad):
    rows, width = hidden.shape
    n = len(parts)

    def body(*refs):
        h_ref, g_ref, grad_ref, out_ref, b_ref, gain_ref = refs[n:]
        total = refs[0][...]
        for part in refs[1:n]:
            total = total + part[...].astype(F32)
        h = h_ref[...]
        scale = lax.rsqrt(jnp.mean(h * h, axis=-1, keepdims=True) + eps)
        unit = h * scale
        through = total * g_ref[...]
        out = grad_ref[...] + scale * (
            through - unit * jnp.mean(through * unit, axis=-1, keepdims=True)
        )
        out_ref[...] = out
        b_ref[...] = out.astype(BF)
        gain_ref[...] = jnp.sum(total * unit, axis=0, keepdims=True)

    return kernel_call(
        "norm_back",
        body,
        [((rows, width), F32), ((rows, width), BF), ((1, width), F32)],
        [*parts, hidden, gain, grad],
    )


def project(me, parts, wzx, wbc, wdt, wq, kvw, cos_q, sin_q, cos_kv, sin_kv):
    n = len(parts)
    rows, width = parts[0].shape
    tokens = n * rows
    inner = wzx[0].shape[2] // 2
    mix = inner + 2 * NS

    def body(*refs):
        me_ref = refs[0]
        (
            kvw_ref, wq_ref, wdt_ref, wbc_ref, wzx_ref, cq_ref, sq_ref, ck_ref, sk_ref,
            nat_ref, gate_ref, u_ref, r_ref, kv_ref, q_ref,
        ) = refs[1 + n :]
        ordered(me_ref, refs[1 : 1 + n], nat_ref)
        x = nat_ref[...]
        kv = mm(x, kvw_ref[...])
        kv_ref[...] = (kv * ck_ref[...] + halves_swapped(kv) * sk_ref[...]).astype(BF)
        q = mm(x, wq_ref[...])
        q_ref[...] = (q * cq_ref[...] + halves_swapped(q) * sq_ref[...]).astype(BF)
        r_ref[...] = mm(x, wdt_ref[...])
        u_ref[:, inner:] = mm(x, wbc_ref[...])
        gate_ref[...] = mm(x, wzx_ref[:, :inner])
        u_ref[:, :inner] = mm(x, wzx_ref[:, inner:])

    return kernel_call(
        "project",
        body,
        [
            ((tokens, width), BF),
            ((tokens, inner), F32),
            ((tokens, mix), F32),
            ((tokens, 128), F32),
            ((tokens, 128), BF),
            ((tokens, 128), BF),
        ],
        [me, *parts, kvw, wq, wdt, wbc, wzx, cos_q, sin_q, cos_kv, sin_kv],
        flops=2 * tokens * width * 1408,
    )


def mixer_front(edge, u, r_raw, wzx, wbc, conv_w, hp, tok):
    tokens, mix = u.shape
    inner = mix - 2 * NS

    def body(
        edge_ref, u_ref, r_ref, wzx_ref, wbc_ref, cw_ref, hp_ref, tok_ref,
        pad_ref, act_ref, slope_ref, hd_ref, pack_ref,
    ):
        e = edge_ref[...]
        pad_ref[:16, :inner] = mm(e, wzx_ref[:, inner:])
        pad_ref[:16, inner:] = mm(e, wbc_ref[...])
        pad_ref[16:, :] = u_ref[...]
        tk = tok_ref[...]
        conv = jnp.broadcast_to(cw_ref[KC : KC + 1, :], (tokens, mix))
        for j in range(KC):
            shifted = pad_ref[16 - (KC - 1) + j : 16 - (KC - 1) + j + tokens, :]
            conv = conv + cw_ref[j : j + 1, :] * shifted * tk[:, j : j + 1]
        sg = sigmoid(conv)
        act = conv * sg
        act_ref[...] = act
        slope_ref[...] = sg * (1.0 + conv * (1.0 - sg))
        r = r_ref[...] + hp_ref[0:1, :]
        dt = jnp.maximum(r, 0.0) + jnp.log1p(jnp.exp(-jnp.abs(r)))
        log_decay = -dt * jnp.exp(hp_ref[1:2, :])
        lower = (iota((tokens, tokens), 0) >= iota((tokens, tokens), 1)).astype(F32)
        cum = mm_hi(lower, log_decay)
        hd_ref[0] = r
        hd_ref[1] = dt
        hd_ref[2] = cum
        last = cum[tokens - 1 :, :]
        to_last = jnp.where(tk[:, 5:6] > 0.5, jnp.exp(last - cum), 0.0)
        scaled = act[:, :inner] * expand(dt * to_last, inner)
        pack_ref[:inner, :] = mm_tn(scaled, act[:, inner : inner + NS]).astype(BF)
        pack_ref[inner:, :] = decay_rows(jnp.exp(last) * tk[tokens - 1 :, 4:5])

    return kernel_call(
        "mixer_front",
        body,
        [
            ((tokens + 16, mix), F32),
            ((tokens, mix), F32),
            ((tokens, mix), F32),
            ((3, tokens, 128), F32),
            ((inner + 16, NS), BF),
        ],
        [edge, u, r_raw, wzx, wbc, conv_w, hp, tok],
        flops=2 * tokens * tokens * 512,
    )


def query_rows(q):
    lane = iota(q.shape, 1)
    wide = q.astype(F32)
    return jnp.concatenate(
        [
            jnp.where(lane < HEAD_SIZE, wide, 0.0),
            jnp.where(lane < HEAD_SIZE, pltpu.roll(wide, HEAD_SIZE, 1), 0.0),
        ],
        axis=0,
    ).astype(BF)


def value_rows(v):
    lane = iota(v.shape, 1)
    wide = v.astype(F32)
    return jnp.concatenate(
        [
            jnp.where(lane >= HEAD_SIZE, pltpu.roll(wide, HEAD_SIZE, 1), 0.0),
            jnp.where(lane >= HEAD_SIZE, wide, 0.0),
        ],
        axis=0,
    )


def allowed_pair(segc, segr, tokens, steps_back):
    heads = segc.shape[0] // tokens
    row = iota((heads * tokens, tokens), 0) % tokens
    column = iota((heads * tokens, tokens), 1)
    return (segc == segr) & (column - tokens * steps_back <= row)


def within_decay(cum, cum_t, h, allowed):
    return jnp.exp(jnp.where(allowed, cum[:, h : h + 1] - cum_t[h : h + 1, :], neg_big))


def mixer_within(act, hd, segc, segrel, hp, inner):
    tokens = act.shape[0]

    def body(act_ref, hd_ref, segc_ref, segr_ref, hp_ref, y_ref):
        lane = iota((tokens, 128), 1)
        act_all = act_ref[...]
        b_mat = act_all[:, inner : inner + NS]
        c_mat = act_all[:, inner + NS :]
        both = mm_nt(c_mat, b_mat)
        dt, cum = hd_ref[1], hd_ref[2]
        cum_t = cum.T
        allowed = allowed_pair(segc_ref[...], segr_ref[0], tokens, 0)
        scaled = act_all[:, :inner] * expand(dt, inner)
        skip = expand(hp_ref[...], inner)[2:3, :]
        for p in range(inner // 128):
            cols = slice(128 * p, 128 * (p + 1))
            pair = [
                mm(within_decay(cum, cum_t, 2 * p + k, allowed) * both, scaled[:, cols])
                for k in range(2)
            ]
            y_ref[:, cols] = (
                jnp.where(lane < HEAD_SIZE, pair[0], pair[1])
                + skip[:, cols] * act_all[:, cols]
            )

    return kernel_call(
        "mixer_within",
        body,
        [((tokens, inner), F32)],
        [act, hd, segc, segrel, hp],
        flops=2 * tokens * tokens * 128 * 8,
    )[0]


def attend(here, every, q_own, segc, segrel, blocks):
    n = every.shape[0]
    tokens = segc.shape[0]
    rows = 2 * tokens

    def body(*refs):
        here_ref, all_ref, q_ref, segc_ref, segr_ref, nb_ref, o2_ref, flat_ref = refs
        arrive(all_ref, segr_ref)
        here_at = here_ref[0]
        q = query_rows(q_ref[...])
        seg_own = segc_ref[...]
        seg_two = jnp.concatenate([seg_own] * (rows // tokens), axis=0)

        def step(d, carry):
            top, total, out = carry
            kv = all_ref[here_at - d]
            allowed = allowed_pair(seg_two, segr_ref[d], tokens, d)
            scores = jnp.where(allowed, mm_nt(q, kv) * score_scale, neg_big)
            new_top = jnp.maximum(top, jnp.max(scores, axis=1, keepdims=True))
            weights = jnp.where(allowed, jnp.exp(scores - new_top), 0.0)
            shrink = jnp.exp(top - new_top)
            return (
                new_top,
                total * shrink + jnp.sum(weights, axis=1, keepdims=True),
                out * shrink + mm(weights, kv),
            )

        top, total, out = lax.fori_loop(
            0,
            nb_ref[0],
            step,
            (
                jnp.full((rows, 1), neg_big, F32),
                jnp.zeros((rows, 1), F32),
                jnp.zeros((rows, 128), F32),
            ),
        )
        out = out / total
        o2_ref[...] = jnp.where(iota((rows, 128), 1) == 0, top + jnp.log(total), out)
        lane = iota((tokens, 128), 1)
        flat_ref[...] = jnp.where(
            lane < HEAD_SIZE, pltpu.roll(out[:tokens], HEAD_SIZE, 1), out[tokens:]
        ).astype(BF)

    return kernel_call(
        "attend",
        body,
        [
            ((rows, 128), F32),
            ((tokens, 128), BF),
        ],
        [here, every, q_own, segc, segrel, blocks],
        flops=2 * rows * tokens * 128 * 2 * n,
    )


def mixer_out(me, here, states, y_local, act, hd, tok, gate, flat, wout, wao, wa_count):
    tokens, inner = y_local.shape
    width = wout[0].shape[2]
    rows = tokens // wa_count

    def body(*refs):
        me_ref, here_ref, all_ref = refs[:3]
        y_ref, act_ref, hd_ref, tok_ref, gate_ref, flat_ref, wout_ref, wao_ref = refs[3:11]
        state_ref, yy_ref, gated_ref = refs[11:14]
        blocks = refs[14 : 14 + wa_count]
        full_ref = refs[-1]
        state = fold_states(all_ref, inner, here_ref[0], False)
        state_ref[...] = state
        decay_in = jnp.exp(hd_ref[2]) * tok_ref[:, 4:5]
        y = y_ref[...] + mm_nt(act_ref[:, inner + NS :], state) * expand(decay_in, inner)
        yy_ref[...] = y
        gate_raw = gate_ref[...]
        gated = (y * gate_raw * sigmoid(gate_raw)).astype(BF)
        gated_ref[...] = gated
        full_ref[...] = mm(gated, wout_ref[...]) + mm(flat_ref[...], wao_ref[...])
        rotated(me_ref, full_ref, blocks)

    return kernel_call(
        "mixer_out",
        body,
        [((inner, NS), F32), ((tokens, inner), F32), ((tokens, inner), BF)]
        + [((rows, width), F32)]
        + [((rows, width), BF)] * (wa_count - 1),
        [me, here, states, y_local, act, hd, tok, gate, flat, wout, wao],
        scratch=[pltpu.VMEM((tokens, width), F32)],
        flops=2 * tokens * width * 512,
    )


def feed_forward(parts, wgu, wdown):
    n = len(parts)
    rows, width = parts[0].shape
    tokens = n * rows
    hidden = wdown[0].shape[1]

    def body(*refs):
        wgu_ref, wdown_ref, n_ref, gu_ref, act_ref = refs[n : n + 5]
        blocks = refs[n + 5 : n + 5 + n]
        for d in range(n):
            n_ref[d * rows : (d + 1) * rows, :] = refs[d][...]
        x = n_ref[...]
        gate = mm(x, wgu_ref[:, :hidden])
        up = mm(x, wgu_ref[:, hidden:])
        gu_ref[:, :hidden] = gate
        gu_ref[:, hidden:] = up
        act = (gate * sigmoid(gate) * up).astype(BF)
        act_ref[...] = act
        for d in range(n):
            blocks[d][...] = mm(act[d * rows : (d + 1) * rows], wdown_ref[...]).astype(
                blocks[d].dtype
            )

    return kernel_call(
        "feed_forward",
        body,
        [((tokens, width), BF), ((tokens, 2 * hidden), F32), ((tokens, hidden), BF)]
        + [((rows, width), F32)]
        + [((rows, width), BF)] * (n - 1),
        [*parts, wgu, wdown],
        flops=2 * tokens * width * 3 * hidden,
    )


def feed_back(parts, gu, wgu, wdown):
    n = len(parts)
    rows, width = parts[0].shape
    tokens = n * rows
    hidden = wdown[0].shape[1]

    def body(*refs):
        gu_ref, wgu_ref, wdown_ref, gb_ref, dgu_ref = refs[n : n + 5]
        blocks = refs[n + 5 : n + 5 + n]
        for d in range(n):
            gb_ref[d * rows : (d + 1) * rows, :] = refs[d][...]
        d_act = mm_nt(gb_ref[...], wdown_ref[...])
        gate = gu_ref[:, :hidden]
        up = gu_ref[:, hidden:]
        sg = sigmoid(gate)
        dgu_ref[:, :hidden] = (d_act * up * sg * (1.0 + gate * (1.0 - sg))).astype(BF)
        dgu_ref[:, hidden:] = (d_act * gate * sg).astype(BF)
        for d in range(n):
            blocks[d][...] = mm_nt(dgu_ref[d * rows : (d + 1) * rows, :], wgu_ref[...]).astype(
                blocks[d].dtype
            )

    return kernel_call(
        "feed_back",
        body,
        [((tokens, width), BF), ((tokens, 2 * hidden), BF)]
        + [((rows, width), F32)]
        + [((rows, width), BF)] * (n - 1),
        [*parts, gu, wgu, wdown],
        flops=2 * tokens * width * 3 * hidden,
    )


def weight_grads(here, pairs, n, direct, ties=()):
    width = pairs[0][0].shape[1]
    columns = sum(right.shape[1] for left, right in pairs)
    flat = [a for pair in pairs for a in pair]
    direct = direct and n <= DIRECT_MOST
    blocks = n if direct else 1
    rows = width // blocks

    def body(*refs):
        here_ref = refs[0]
        outs = refs[1 + len(flat) :]
        for d in range(blocks):
            start = 0
            for k in range(len(pairs)):
                left, right = refs[1 + 2 * k], refs[2 + 2 * k]
                wide = right.shape[1]
                if direct:
                    at = pl.multiple_of(lax.rem(here_ref[0] + d, n) * rows, rows)
                    piece = left[:, pl.ds(at, rows)]
                else:
                    piece = left[...]
                outs[d][:, start : start + wide] = mm_tn(piece, right[...]).astype(outs[d].dtype)
                start += wide

    return kernel_call(
        "weight_grads",
        body,
        [((rows, columns), F32 if direct and d == 0 else BF) for d in range(blocks)],
        [here, *flat],
        flops=2 * pairs[0][0].shape[0] * width * columns,
        ties=ties,
    )


def mixer_grad_in(me, parts, wout, wao, gate, y, act, hd, tok, o2, q_own):
    n = len(parts)
    rows, width = parts[0].shape
    tokens, inner = y.shape
    early = 96

    def body(*refs):
        me_ref = refs[0]
        wout_ref, wao_ref, gate_ref, y_ref, act_ref, hd_ref, tok_ref, o2_ref = refs[1 + n : 9 + n]
        q_ref, nat_ref, dy_ref, dgate_ref, pack_ref, da_ref, delta_ref = refs[9 + n :]
        ordered(me_ref, refs[1 : 1 + n], nat_ref)
        mb = nat_ref[...]
        d_gated = mm_nt(mb, wout_ref[...])
        gate_raw = gate_ref[...]
        sg = sigmoid(gate_raw)
        dy = d_gated * gate_raw * sg
        dy_ref[...] = dy
        dgate_ref[...] = (
            d_gated * y_ref[...] * sg * (1.0 + gate_raw * (1.0 - sg))
        ).astype(BF)
        cum = hd_ref[2]
        decay_in = jnp.exp(cum) * tok_ref[:, 4:5]
        pack_ref[:inner, :] = mm_tn(
            dy * expand(decay_in, inner), act_ref[:, inner + NS :]
        ).astype(BF)
        pack_ref[inner : inner + 16, :] = decay_rows(decay_in[tokens - 1 :, :])
        pack_ref[inner + 16 :, :] = q_ref[:early, :]
        da_ref[tokens + 16 :, :] = q_ref[early:, :]
        d_attn = mm_nt(mb, wao_ref[...])
        da_ref[:tokens, :] = d_attn.astype(BF)
        delta = jnp.sum(value_rows(d_attn) * o2_ref[...], axis=1, keepdims=True)
        delta_ref[...] = jnp.broadcast_to(delta, (2 * tokens, 128))
        lane = iota((tokens, 128), 1)
        table = jnp.zeros((tokens, 128), F32)
        columns = [
            o2_ref[:tokens, 0:1], o2_ref[tokens:, 0:1], delta[:tokens], delta[tokens:]
        ]
        for k in range(4):
            table = jnp.where((lane == k) | (lane == k + 4), columns[k], table)
        table = table.T[:8]
        high = table.astype(BF).astype(F32)
        table = jnp.where(iota(table.shape, 0) < 4, high, table - high)
        da_ref[tokens : tokens + 16, :] = jnp.concatenate(
            [table[:, 128 * k : 128 * (k + 1)] for k in range(tokens // 128)], axis=0
        ).astype(BF)

    return kernel_call(
        "mixer_grad_in",
        body,
        [
            ((tokens, width), BF),
            ((tokens, inner), F32),
            ((tokens, inner), BF),
            ((inner + 16 + early, NS), BF),
            ((tokens + 16 + tokens - early, 128), BF),
            ((2 * tokens, 128), F32),
        ],
        [me, *parts, wout, wao, gate, y, act, hd, tok, o2, q_own],
        flops=2 * tokens * width * 512,
    )


def attend_back(
    here, every, states_back, every_back, delta, o2, q_own, segc, segrel, seglater, blocks,
    cos_q, sin_q, cos_kv, sin_kv, inner,
):
    n = every.shape[0]
    tokens = segc.shape[0]
    rows = 2 * tokens

    def body(
        here_ref, all_ref, state_ref, back_ref, delta_ref, lse_ref, q_ref, segc_ref, segr_ref, segl_ref, nb_ref,
        cq_ref, sq_ref, ck_ref, sk_ref, dq_ref, dkv_ref,
    ):
        arrive(all_ref, state_ref, back_ref, segr_ref, segl_ref)
        here_at = here_ref[0]
        q = query_rows(q_ref[...])
        da = value_rows(back_ref[here_at, :tokens, :]).astype(BF)
        lse_col = lse_ref[:, 0:1]
        delta_col = delta_ref[:, 0:1]
        seg_own = segc_ref[...]
        seg_two = jnp.concatenate([seg_own] * 2, axis=0)

        def step(d, dq):
            kv = all_ref[here_at - d]
            allowed = allowed_pair(seg_two, segr_ref[d], tokens, d)
            scores = mm_nt(q, kv) * score_scale
            probs = jnp.exp(jnp.where(allowed, scores - lse_col, neg_big))
            d_scores = probs * (mm_nt(da, kv) - delta_col)
            return dq + mm(d_scores, kv)

        dq = lax.fori_loop(0, nb_ref[0], step, jnp.zeros((rows, 128), F32)) * score_scale
        lane = iota((tokens, 128), 1)
        flat = jnp.where(lane < HEAD_SIZE, dq[:tokens], pltpu.roll(dq[tokens:], HEAD_SIZE, 1))
        dq_ref[...] = (flat * cq_ref[...] - halves_swapped(flat) * sq_ref[...]).astype(BF)
        kv_own = all_ref[here_at]

        def back_step(d, dkv):
            j = here_at + d
            q_there = query_rows(
                jnp.concatenate(
                    [state_ref[j, inner + 16 :, :], back_ref[j, tokens + 16 :, :]], axis=0
                )
            )
            da_there = value_rows(back_ref[j, :tokens, :]).astype(BF)
            table = back_ref[j, tokens : tokens + 16, :].astype(F32)
            row = iota((tokens, tokens), 0)
            column = iota((tokens, tokens), 1)
            allowed = (seg_own == segl_ref[d]) & (row <= column + tokens * d)
            d_key = jnp.zeros((tokens, 128), F32)
            d_value = jnp.zeros((tokens, 128), F32)
            for k in range(2):

                def line(r):
                    return jnp.concatenate(
                        [
                            table[8 * i + r : 8 * i + r + 1] + table[8 * i + r + 4 : 8 * i + r + 5]
                            for i in range(tokens // 128)
                        ],
                        axis=1,
                    )

                mine = slice(k * tokens, (k + 1) * tokens)
                scores = mm_nt(kv_own, q_there[mine]) * score_scale
                probs = jnp.exp(jnp.where(allowed, scores - line(k), neg_big))
                d_scores = probs * (mm_nt(kv_own, da_there[mine]) - line(2 + k))
                d_key = d_key + mm(d_scores, q_there[mine])
                d_value = d_value + mm(probs, da_there[mine])
            return dkv + (d_key * score_scale + d_value)

        dkv = lax.fori_loop(0, nb_ref[1], back_step, jnp.zeros((tokens, 128), F32))
        dkv_ref[...] = (dkv * ck_ref[...] - halves_swapped(dkv) * sk_ref[...]).astype(BF)

    return kernel_call(
        "attend_back",
        body,
        [((tokens, 128), BF), ((tokens, 128), BF)],
        [
            here, every, states_back, every_back, delta, o2, q_own, segc, segrel, seglater, blocks,
            cos_q, sin_q, cos_kv, sin_kv,
        ],
        flops=2 * rows * tokens * 128 * 7 * n,
    )


def mixer_grad(here, every_back, state_in, dy, act, slope, pad, hd, tok, segc, segrel, hp, conv_w):
    tokens, inner = dy.shape
    mix = act.shape[1]

    def body(*refs):
        (
            here_ref, back_ref, state_ref, dy_ref, act_ref, slope_ref, pad_ref, hd_ref, tok_ref, segc_ref, segr_ref,
            hp_ref, cw_ref, dmix_ref, tail_ref, edge_ref, ddt_ref, gconv_ref, ghead_ref,
            dconv_ref, dpad_ref, dxs_ref,
        ) = refs
        later = fold_states(back_ref, inner, here_ref[0], True)
        state = state_ref[...]
        tk = tok_ref[...]
        act_all = act_ref[...]
        x = act_all[:, :inner]
        b_mat = act_all[:, inner : inner + NS]
        c_mat = act_all[:, inner + NS :]
        dy_all = dy_ref[...]
        r, dt, cum = hd_ref[0], hd_ref[1], hd_ref[2]
        cum_t = cum.T
        last = cum[tokens - 1 :, :]
        to_last = jnp.where(tk[:, 5:6] > 0.5, jnp.exp(last - cum), 0.0)
        decay_in = jnp.exp(cum) * tk[:, 4:5]
        dt_wide = expand(dt, inner)
        last_wide = expand(to_last, inner)
        in_wide = expand(decay_in, inner)
        xs = x * dt_wide
        allowed = allowed_pair(segc_ref[...], segr_ref[0], tokens, 0)
        both = mm_nt(c_mat, b_mat)
        lane = iota((tokens, 128), 1)
        lane_row = iota((128, tokens), 0)
        d_both = jnp.zeros((tokens, tokens), F32)
        d_cum = jnp.zeros((tokens, 128), F32)
        d_cum_t = jnp.zeros((128, tokens), F32)
        for p in range(inner // 128):
            cols = slice(128 * p, 128 * (p + 1))
            xs_pair = xs[:, cols].astype(BF)
            dy_pair = dy_all[:, cols]
            pieces = []
            for k in range(2):
                h = 2 * p + k
                decay = within_decay(cum, cum_t, h, allowed)
                weight = decay * both
                mine = (lane >= HEAD_SIZE) if k else (lane < HEAD_SIZE)
                d_weight = mm_nt(jnp.where(mine, dy_pair, 0.0), xs_pair)
                d_both = d_both + d_weight * decay
                flow = d_weight * weight
                d_cum = d_cum + jnp.where(lane == h, jnp.sum(flow, axis=1, keepdims=True), 0.0)
                d_cum_t = d_cum_t + jnp.where(
                    lane_row == h, jnp.sum(flow, axis=0, keepdims=True), 0.0
                )
                pieces.append(mm_tn(weight, dy_pair))
            dxs_ref[:, cols] = jnp.where(lane < HEAD_SIZE, pieces[0], pieces[1])
        from_state = mm_nt(b_mat, later)
        d_xs = dxs_ref[...] + from_state * last_wide
        dy_in = dy_all * in_wide
        inflow = mm_nt(c_mat, state)
        d_c = mm(d_both, b_mat) + mm(dy_in, state)
        d_b = mm_tn(d_both, c_mat) + mm(xs * last_wide, later)
        carried = head_sum(from_state * xs * last_wide)
        d_cum = d_cum - d_cum_t.T + head_sum(dy_in * inflow) - carried
        row_sum = jnp.sum(later * state, axis=1, keepdims=True)
        pick = (iota((inner, 128), 0) // HEAD_SIZE == iota((inner, 128), 1)).astype(F32)
        d_decay = jnp.sum(row_sum * pick, axis=0, keepdims=True)
        d_last = jnp.sum(carried, axis=0, keepdims=True) + decay_in[tokens - 1 :, :] * d_decay
        d_cum = d_cum + jnp.where(iota((tokens, 128), 0) == tokens - 1, d_last, 0.0)
        upper = (iota((tokens, tokens), 0) <= iota((tokens, tokens), 1)).astype(F32)
        d_log = mm_hi(upper, d_cum)
        rate = jnp.exp(hp_ref[1:2, :])
        d_dt = head_sum(d_xs * x) - rate * d_log
        d_r = d_dt * sigmoid(r)
        ddt_ref[...] = d_r.astype(BF)
        g_bias = jnp.sum(d_r, axis=0, keepdims=True)
        g_log = -jnp.sum(d_log * dt, axis=0, keepdims=True) * rate
        g_skip = jnp.sum(head_sum(dy_all * x), axis=0, keepdims=True)
        row8 = iota((8, 128), 0)
        ghead_ref[...] = jnp.where(
            row8 == 0, g_bias, jnp.where(row8 == 1, g_log, jnp.where(row8 == 2, g_skip, 0.0))
        )
        skip = expand(hp_ref[...], inner)[2:3, :]
        dconv_ref[:, :inner] = (dy_all * skip + d_xs * dt_wide) * slope_ref[:, :inner]
        dconv_ref[:, inner : inner + NS] = d_b * slope_ref[:, inner : inner + NS]
        dconv_ref[:, inner + NS :] = d_c * slope_ref[:, inner + NS :]
        dpad_ref[...] = jnp.zeros((tokens + 16, mix), F32)
        gconv_ref[...] = jnp.zeros((8, mix), F32)
        dconv = dconv_ref[...]
        gconv_ref[KC : KC + 1, :] = jnp.sum(dconv, axis=0, keepdims=True)
        for j in range(KC):
            at = 16 - (KC - 1) + j
            used = dconv * tk[:, j : j + 1]
            gconv_ref[j : j + 1, :] = jnp.sum(
                used * pad_ref[at : at + tokens, :], axis=0, keepdims=True
            )
            dpad_ref[at : at + tokens, :] = (
                dpad_ref[at : at + tokens, :] + used * cw_ref[j : j + 1, :]
            )
        dmix_ref[...] = dpad_ref[16:, :].astype(BF)
        tail_ref[...] = dpad_ref[tokens:, :]
        edge_ref[...] = dpad_ref[8:16, :]

    return kernel_call(
        "mixer_grad",
        body,
        [
            ((tokens, mix), BF),
            ((16, mix), F32),
            ((8, mix), F32),
            ((tokens, 128), BF),
            ((8, mix), F32),
            ((8, 128), F32),
        ],
        [here, every_back, state_in, dy, act, slope, pad, hd, tok, segc, segrel, hp, conv_w],
        scratch=[
            pltpu.VMEM((tokens, mix), F32),
            pltpu.VMEM((tokens + 16, mix), F32),
            pltpu.VMEM((tokens, inner), F32),
        ],
        flops=2 * tokens * tokens * 128 * 24,
    )


def grads_out(
    me, dgate, dmix, tail, next_edge, ddt, dq, dkv, wzx, wbc, wdt, wq, kvw, wa_count
):
    tokens, inner = dgate.shape
    mix = dmix.shape[1]
    width = wzx[0].shape[1]
    rows = tokens // wa_count

    def body(
        me_ref, dgate_ref, dmix_ref, tail_ref, edge_ref, ddt_ref, dq_ref, dkv_ref,
        wzx_ref, wbc_ref, wdt_ref, wq_ref, kvw_ref, dx_ref, dbc_ref, *rest,
    ):
        blocks, full_ref = rest[:-1], rest[-1]
        ends = tail_ref[...] + jnp.concatenate([jnp.zeros((8, mix), F32), edge_ref[...]], axis=0)
        for ref, cols in ((dx_ref, slice(0, inner)), (dbc_ref, slice(inner, mix))):
            ref[: tokens - 16, :] = dmix_ref[: tokens - 16, cols]
            ref[tokens - 16 :, :] = ends[:, cols].astype(BF)
        full_ref[...] = (
            mm_nt(ddt_ref[...], wdt_ref[...])
            + mm_nt(dq_ref[...], wq_ref[...])
            + mm_nt(dkv_ref[...], kvw_ref[...])
            + mm_nt(dbc_ref[...], wbc_ref[...])
            + mm_nt(dgate_ref[...], wzx_ref[:, :inner])
            + mm_nt(dx_ref[...], wzx_ref[:, inner:])
        )
        rotated(me_ref, full_ref, blocks)

    return kernel_call(
        "grads_out",
        body,
        [((tokens, inner), BF), ((tokens, 2 * NS), BF), ((rows, width), F32)]
        + [((rows, width), BF)] * (wa_count - 1),
        [me, dgate, dmix, tail, next_edge, ddt, dq, dkv, wzx, wbc, wdt, wq, kvw],
        scratch=[pltpu.VMEM((tokens, width), F32)],
        flops=2 * tokens * width * (mix + 768),
    )


def all_rows(me, parts):
    n = len(parts)
    rows, width = parts[0].shape

    def body(*refs):
        for d in range(n):
            at = pl.multiple_of(lax.rem(refs[0][0] + n - d, n) * rows, rows)
            refs[-1][pl.ds(at, rows), :] = refs[1 + d][...].astype(F32)

    return kernel_call("all_rows", body, [((n * rows, width), F32)], [me, *parts])[0]


def held_back(arrays, ties):
    count = len(arrays)

    def body(*refs):
        pass

    return pl.pallas_call(
        body,
        in_specs=[pl.BlockSpec(memory_space=pl.ANY)] * (count + len(ties)),
        out_specs=[pl.BlockSpec(memory_space=pl.ANY)] * count,
        out_shape=[jax.ShapeDtypeStruct(a.shape, a.dtype) for a in arrays],
        input_output_aliases={i: i for i in range(count)},
        name="held_back",
    )(*arrays, *ties)


def pack_small(gains, convs, heads, inner, ties):
    width = gains[0].shape[1]
    mix = convs[0].shape[1]
    pieces = [(g, 0, 0, width) for g in range(len(gains))]
    at = len(gains)
    pieces += [(at + k, j, inner, mix) for k in range(len(convs)) for j in range(KC + 1)]
    pieces += [(at + k, j, 0, inner) for k in range(len(convs)) for j in range(KC + 1)]
    at += len(convs)
    pieces += [(at + k, j, 0, 128) for k in range(len(heads)) for j in range(8)]
    total = sum((end - start) // 128 for _, _, start, end in pieces)

    def body(*refs):
        row = 0
        for source, line, start, end in pieces:
            for c in range(start, end, 128):
                refs[-1][row : row + 1, :] = refs[source][line : line + 1, c : c + 128]
                row += 1

    return kernel_call(
        "pack_small", body, [((total, 128), F32)], [*gains, *convs, *heads], ties=ties
    )[0]


def per_device(
    x_in,
    d_out,
    segment_ids,
    norm_gains,
    w_zx,
    w_bc,
    w_dt,
    conv_x,
    conv_bc,
    dt_bias,
    a_log,
    d_skip,
    w_out,
    w_q,
    key_value_weight,
    w_ao,
    w_gu,
    w_down,
):
    seq_count = lax.axis_size("seq")
    wa_count = lax.axis_size("wa")
    tokens, width = x_in.shape
    rows = tokens // wa_count
    seq_here = lax.axis_index("seq")
    wa_here = lax.axis_index("wa")
    start_row = seq_here * tokens
    inner = w_zx.shape[3]
    heads = w_dt.shape[2]
    hidden = w_gu.shape[3]
    query_local = w_q.shape[2] // HEAD_SIZE
    group = QUERY_HEADS // KEY_VALUE_HEADS
    kv_head = wa_here * query_local // group
    me = wa_here.astype(jnp.int32).reshape(1)
    here = seq_here.astype(jnp.int32).reshape(1)

    seg_blocks = segment_ids.reshape(seq_count, tokens)
    seg_here = lax.dynamic_slice_in_dim(segment_ids, start_row, tokens)
    seg_padded = jnp.concatenate([jnp.full((KC - 1,), -1, jnp.int32), segment_ids])
    seg_edge = lax.dynamic_slice_in_dim(seg_padded, start_row, KC - 1)
    seg_full = jnp.concatenate([seg_edge, seg_here])
    steps = jnp.arange(seq_count, dtype=jnp.int32)
    segrel = jnp.where(
        (steps <= seq_here)[:, None], seg_blocks[(seq_here - steps) % seq_count], -1
    )
    seglater = jnp.where(
        (steps + seq_here < seq_count)[:, None], seg_blocks[(seq_here + steps) % seq_count], -1
    )
    blocks_used = jnp.stack(
        [
            1 + jnp.sum((segrel[1:, tokens - 1] == seg_here[0]).astype(jnp.int32)),
            1 + jnp.sum((seglater[1:, 0] == seg_here[tokens - 1]).astype(jnp.int32)),
        ]
    ).astype(jnp.int32)
    segrel = segrel[:, None, :]
    seglater = seglater[:, None, :]
    segc = seg_here[:, None]
    columns = [(seg_full[j : j + tokens] == seg_here).astype(F32) for j in range(KC)]
    columns.append((seg_here == seg_edge[KC - 2]).astype(F32))
    columns.append((seg_here == seg_here[tokens - 1]).astype(F32))
    tok = jnp.pad(jnp.stack(columns, axis=1), ((0, 0), (0, 128 - len(columns))))
    half = HEAD_SIZE // 2
    frequency = jnp.exp(jnp.arange(half, dtype=F32) * (-math.log(theta) / half))
    positions = (start_row + jnp.arange(tokens, dtype=jnp.int32)).astype(F32)
    angles = positions[:, None] * frequency[None, :]
    cosine, sine = jnp.cos(angles), jnp.sin(angles)
    cos_q = jnp.concatenate([cosine] * 4, axis=1)
    sin_q = jnp.concatenate([-sine, sine, -sine, sine], axis=1)
    ones = jnp.ones((tokens, HEAD_SIZE), F32)
    cos_kv = jnp.concatenate([cosine, cosine, ones], axis=1)
    sin_kv = jnp.concatenate([-sine, sine, 0.0 * ones], axis=1)

    wzx_all = w_zx.reshape(LAYER_COUNT, width, 2 * inner)
    wgu_all = w_gu.reshape(LAYER_COUNT, width, 2 * hidden)
    wdt_all = jnp.pad(w_dt, ((0, 0), (0, 0), (0, 128 - heads)))
    kvw_all = lax.dynamic_slice_in_dim(
        key_value_weight, kv_head * HEAD_SIZE, HEAD_SIZE, axis=3
    ).reshape(LAYER_COUNT, width, 2 * HEAD_SIZE)
    conv_all = jnp.pad(
        jnp.concatenate([conv_x, conv_bc], axis=2), ((0, 0), (0, 8 - (KC + 1)), (0, 0))
    )
    hp_all = jnp.pad(
        jnp.stack([dt_bias, a_log, d_skip], axis=1), ((0, 0), (0, 5), (0, 128 - heads))
    )

    def own_rows(array):
        return lax.dynamic_slice_in_dim(array, wa_here * rows, rows)

    h = own_rows(x_in)
    normed = norm_first(h, norm_gains[0, 0][None, :])
    saved = []
    for layer in range(LAYER_COUNT):
        wzx, wbc, wdt, wq = [(a, layer) for a in (wzx_all, w_bc, wdt_all, w_q)]
        kvw, conv_w, hp = [(a, layer) for a in (kvw_all, conv_all, hp_all)]
        wout, wao, wgu, wdown = [(a, layer) for a in (w_out, w_ao, wgu_all, w_down)]
        normed_parts = gather_wa(normed)
        edge = jnp.zeros((16, width), BF)
        for d, part in enumerate(normed_parts):
            edge = jnp.where((wa_here + wa_count - d) % wa_count == wa_count - 1, part[rows - 16 :], edge)
        edge = lax.ppermute(edge, "seq", [(i, i + 1) for i in range(seq_count - 1)])
        nat, gate, u, r_raw, kv, q_own = project(
            me, normed_parts, wzx, wbc, wdt, wq, kvw, cos_q, sin_q, cos_kv, sin_kv
        )
        every = gather_seq(kv)
        pad, act, slope, hd, pack = mixer_front(
            edge, u, r_raw, wzx, wbc, conv_w, hp, tok
        )
        states = gather_seq(pack)
        y_local = mixer_within(act, hd, segc, segrel, hp, inner)
        o2, flat = attend(here, every, q_own, segc, segrel, blocks_used)
        state_in, y, gated, *parts = mixer_out(
            me, here, states, y_local, act, hd, tok, gate, flat, wout, wao, wa_count
        )
        mixed, normed_two = norm_step(scatter_wa(parts), h, norm_gains[layer, 1][None, :])
        n2, gu, act_ff, *parts = feed_forward(gather_wa(normed_two), wgu, wdown)
        saved.append(
            (h, nat, every, q_own, gate, pad, act, slope, hd, o2, flat, state_in, y, gated,
             mixed, n2, gu, act_ff)
        )
        if layer + 1 < LAYER_COUNT:
            h, normed = norm_step(scatter_wa(parts), mixed, norm_gains[layer + 1, 0][None, :])

    last_parts = parts
    last_mixed = mixed

    grad = own_rows(d_out)
    grad_parts = [
        lax.dynamic_slice_in_dim(d_out, (wa_here + wa_count - d) % wa_count * rows, rows).astype(BF)
        for d in range(wa_count)
    ]
    sums = [None] * LAYER_COUNT
    small = [None] * LAYER_COUNT
    for layer in reversed(range(LAYER_COUNT)):
        wzx, wbc, wdt, wq = [(a, layer) for a in (wzx_all, w_bc, wdt_all, w_q)]
        kvw, conv_w, hp = [(a, layer) for a in (kvw_all, conv_all, hp_all)]
        wout, wao, wgu, wdown = [(a, layer) for a in (w_out, w_ao, wgu_all, w_down)]
        (h_in, nat, every, q_own, gate, pad, act, slope, hd, o2, flat, state_in, y, gated,
         mixed, n2, gu, act_ff) = saved[layer]
        gb, dgu, *parts = feed_back(grad_parts, gu, wgu, wdown)
        parts = scatter_wa(parts)
        sum_ff = scatter_rows(
            weight_grads(here, [(gb, act_ff), (n2, dgu)], seq_count, False, [parts[1]])
        )
        d_mixed, mixed_b, gain_two = norm_back(
            parts, mixed, norm_gains[layer, 1][None, :], grad
        )
        mixed_parts = gather_wa(mixed_b)
        mb, dy, dgate, pack, da, delta = mixer_grad_in(
            me, mixed_parts, wout, wao, gate, y, act, hd, tok, o2, q_own
        )
        states_back = gather_seq(pack)
        every_back = gather_seq(da)
        dq, dkv = attend_back(
            here, every, states_back, every_back, delta, o2, q_own, segc, segrel, seglater,
            blocks_used, cos_q, sin_q, cos_kv, sin_kv, inner,
        )
        if layer == LAYER_COUNT - 1:
            out_parts = scatter_wa(held_back(last_parts, [delta]))
            h = norm_step(out_parts, last_mixed, norm_gains[layer, 0][None, :], [dq])[0]
        dmix, tail, edge_grad, ddt, gconv, ghead = mixer_grad(
            here, states_back, state_in, dy, act, slope, pad, hd, tok, segc, segrel, hp, conv_w
        )
        next_edge = lax.ppermute(
            edge_grad, "seq", [(i + 1, i) for i in range(seq_count - 1)]
        )
        dx, dbc, *parts = grads_out(
            me, dgate, dmix, tail, next_edge, ddt, dq, dkv, wzx, wbc, wdt, wq, kvw, wa_count
        )
        parts = scatter_wa(parts)
        mix_pairs = [(mb, gated), (mb, flat), (nat, dgate), (nat, dq)]
        if layer:
            sum_mix = scatter_rows(
                weight_grads(here, mix_pairs, seq_count, False, [parts[1]])
            )
        else:
            sum_mix = scatter_rows(weight_grads(here, mix_pairs, seq_count, False))
            sum_every = scatter_rows(
                weight_grads(here, [(nat, dbc), (nat, dkv)], seq_count, True)
            )
            sum_in = scatter_rows(weight_grads(here, [(nat, dx), (nat, ddt)], seq_count, True))
        grad, grad_b, gain_one = norm_back(
            parts, h_in, norm_gains[layer, 0][None, :], d_mixed
        )
        grad_parts = gather_wa(grad_b)
        if layer:
            joint = scatter_rows(
                weight_grads(
                    here, [(nat, dbc), (nat, dkv), (nat, dx), (nat, ddt)], seq_count, False,
                    [grad_parts[1]],
                )
            )
            ends = 2 * NS + 128
            sum_every, sum_in = joint[:, :ends], joint[:, ends:]
            x_parts = gather_wa(held_back([h.astype(BF)], [grad_parts[-1]])[0])
        sums[layer] = (sum_ff, sum_mix, sum_in, sum_every)
        small[layer] = (gain_one, gain_two, gconv, ghead)
    x_out = all_rows(me, x_parts)
    d_x = all_rows(me, grad_parts)

    mix = inner + 2 * NS
    local = pack_small(
        [small[layer][k] for layer in range(LAYER_COUNT) for k in (0, 1)],
        [small[layer][2] for layer in range(LAYER_COUNT)],
        [small[layer][3] for layer in range(LAYER_COUNT)],
        inner,
        [grad_parts[1]],
    )
    local = jnp.sum(gather_seq(local), axis=0)
    gain_rows = 2 * LAYER_COUNT * width // 128
    shared_rows = gain_rows + LAYER_COUNT * (KC + 1) * 2 * NS // 128
    shared = sum(gather_wa(local[:shared_rows]))
    gain_sum = shared[:gain_rows].reshape(LAYER_COUNT, 2, width)
    g_conv_bc = shared[gain_rows:].reshape(LAYER_COUNT, KC + 1, 2 * NS)
    local = local[shared_rows:]
    conv_rows = LAYER_COUNT * (KC + 1) * (inner // 128)
    g_conv_x = local[:conv_rows].reshape(LAYER_COUNT, KC + 1, inner)
    head_part = local[conv_rows:].reshape(LAYER_COUNT, 8, 128)

    every = jnp.stack([s[3] for s in sums]).astype(BF)
    every_parts = gather_wa(every)
    g_bc = sum(part[:, :, : 2 * NS].astype(F32) for part in every_parts)
    kv_columns = []
    for head in range(KEY_VALUE_HEADS):
        total = 0.0
        for d, part in enumerate(every_parts):
            source = (wa_here + wa_count - d) % wa_count * query_local // group
            total = total + jnp.where(source == head, part[:, :, 2 * NS :].astype(F32), 0.0)
        kv_columns.append(total.reshape(total.shape[0], total.shape[1], 2, HEAD_SIZE))
    g_kv = jnp.concatenate(kv_columns, axis=3)

    block = sums[0][0].shape[0]

    def stacked(pick):
        return jnp.stack([pick(s) for s in sums])

    g_down = stacked(lambda s: s[0][:, :hidden].T)
    g_gu = stacked(lambda s: s[0][:, hidden:].reshape(block, 2, hidden))
    ends = inner + 128
    g_out = stacked(lambda s: s[1][:, :inner].T)
    g_ao = stacked(lambda s: s[1][:, inner:ends].T)
    g_zx = stacked(
        lambda s: jnp.stack([s[1][:, ends : ends + inner], s[2][:, :inner]], axis=1)
    )
    g_q = stacked(lambda s: s[1][:, ends + inner :])
    g_dt = stacked(lambda s: s[2][:, inner : inner + heads])
    return (
        x_out,
        d_x,
        gain_sum[:, 0],
        gain_sum[:, 1],
        g_zx,
        g_bc,
        g_dt,
        g_conv_x,
        g_conv_bc,
        head_part[:, 0, :heads],
        head_part[:, 1, :heads],
        head_part[:, 2, :heads],
        g_out,
        g_q,
        g_kv,
        g_ao,
        g_gu,
        g_down,
    )


def solution(mesh):
    return jax.shard_map(
        per_device,
        mesh=mesh,
        in_specs=(
            P("seq", None),
            P("seq", None),
            P(),
            P(),
            P(None, None, None, "wa"),
            P(),
            P(None, None, "wa"),
            P(None, None, "wa"),
            P(),
            P(None, "wa"),
            P(None, "wa"),
            P(None, "wa"),
            P(None, "wa", None),
            P(None, None, "wa"),
            P(),
            P(None, "wa", None),
            P(None, None, None, "wa"),
            P(None, "wa", None),
        ),
        out_specs=(
            P("seq", None),
            P("seq", None),
            P(),
            P(),
            P(None, "seq", None, "wa"),
            P(None, "seq", None),
            P(None, "seq", "wa"),
            P(None, None, "wa"),
            P(),
            P(None, "wa"),
            P(None, "wa"),
            P(None, "wa"),
            P(None, "wa", "seq"),
            P(None, "seq", "wa"),
            P(None, "seq", None, None),
            P(None, "wa", "seq"),
            P(None, "seq", None, "wa"),
            P(None, "wa", "seq"),
        ),
        check_vma=False,
    )
```

time: 675 us -> 598 us (0.89)
  the two profiles are of different devices: /device:TPU:19 before, /device:TPU:0 now
where the time goes in v2:
time: 598 us; the launch traced here: 587 us
  starting transfers between devices  125 us (21%)
  waiting for transfers between devices  122 us (20%)
  blocking collectives  112 us (19%)
  local copies, waits for them, and re-layouts  106 us (18%)
  Pallas kernels  82.5 us (14%)
  other arithmetic  21.2 us (4%)
  between operations  18.4 us (3%)
    all_gather x9, blocking collectives, gather_seq(): return lax.all_gather(block, 'seq')  112 us
    pallas_call x41, Pallas kernels, kernel_call(): pl.pallas_call(whole, grid=(1,), in_specs=in_specs, out_specs=[pl.BlockSp...  82.5 us
    unnamed x503, local copies, waits for them, and re-layouts  71.8 us
    ppermute x33, waiting for transfers between devices, gather_wa(): lax.ppermute(block, 'wa', [(i, (i + d) % n) for i in range(n)])  58.1 us
    ppermute x33, starting transfers between devices, gather_wa(): lax.ppermute(block, 'wa', [(i, (i + d) % n) for i in range(n)])  54.8 us
    ppermute x24, waiting for transfers between devices, scatter_wa(): lax.ppermute(blocks[n - d], 'wa', [(i, (i + d) % n) for i in range(n)])  48.5 us
    ppermute x24, starting transfers between devices, scatter_wa(): lax.ppermute(blocks[n - d], 'wa', [(i, (i + d) % n) for i in range(n)])  44.1 us
    ppermute x14, starting transfers between devices, scatter_rows(): lax.ppermute(blocks[d], 'seq', [(i, (i + d) % n) for i in range(n)])  19.1 us
  transfers between devices with their start and end apart: 80, of which 31 were waited for; matrix products, arithmetic and copies ran while one was open for 10% of the time, Pallas kernels for 6%

profile of v2, /device:TPU:0, one launch (start us, length us, event | category | flops | bytes accessed | tf_op | source)
XLA Modules:
  0.0 587.4 jit_solution(10863031876202370896)
XLA Ops:
  9.8 5.1 collective-permute-start
  33.1 8.3 %reshape.246.refs_9_.refs_3_.refs_8_ = bf16[2,1024,768]{2,1,0:T(8,128)(2,1)} reshape(bf16[2,1024,2,384]{3,2,1,0:T(2,128)(2,1)} %param.22) | data formatting | bytes 6291456 | tf_op jit(solution)/shard_map/reshape | solution.py:1036
  50.8 9.9 %all-gather.1 = bf16[2048,128]{1,0:T(8,128)(2,1)S(1)} all-gather(bf16[256,128]{1,0:T(8,128)(2,1)S(1)} %get-tuple-element.168), channel_id=3, replica_groups=mesh['seq'=8,'wa'=4] {'seq'}, dimensions={0}, use_global_device_ids=true | all-gather | bytes 589824 | tf_op jit(solution)/shard_map/all_gather | solution.py:61
  71.2 13.8 %all-gather = bf16[3200,128]{1,0:T(8,128)(2,1)S(1)} all-gather(bf16[400,128]{1,0:T(8,128)(2,1)S(1)} %get-tuple-element.164), channel_id=2, replica_groups=mesh['seq'=8,'wa'=4] {'seq'}, dimensions={0}, use_global_device_ids=true | all-gather | bytes 921600 | tf_op jit(solution)/shard_map/all_gather | solution.py:61
  96.7 5.2 collective-permute-done.5.refs_2_
  109.1 7.7 %reshape.248.refs_4_.refs_5_ = bf16[2,1024,1024]{2,1,0:T(8,128)(2,1)} reshape(bf16[2,1024,2,512]{3,2,1,0:T(2,128)(2,1)} %param.34) | data formatting | bytes 8388608 | tf_op jit(solution)/shard_map/reshape | solution.py:1037
  131.8 4.4 collective-permute-done.11.refs_2_
  136.5 4.4 collective-permute-start.13
  144.9 8.2 %collective-permute-done.14.refs_3_ = bf16[64,1024]{1,0:T(8,128)(2,1)S(1)} collective-permute-done((bf16[64,1024]{1,0:T(8,128)(2,1)S(1)}, bf16[64,1024]{1,0:T(8,128)(2,1)S(1)}, u32[]{:S(2)}, u32[]{:S(2)}) %collective-permute-start.14) | collective-permute-done | bytes 131104 | tf_op jit(solution)/shard_map/ppermute | solution.py:81
  156.7 9.7 %all-gather.3 = bf16[2048,128]{1,0:T(8,128)(2,1)S(1)} all-gather(bf16[256,128]{1,0:T(8,128)(2,1)S(1)} %get-tuple-element.188), channel_id=5, replica_groups=mesh['seq'=8,'wa'=4] {'seq'}, dimensions={0}, use_global_device_ids=true | all-gather | bytes 589824 | tf_op jit(solution)/shard_map/all_gather | solution.py:61
  175.2 13.9 %all-gather.2 = bf16[3200,128]{1,0:T(8,128)(2,1)S(1)} all-gather(bf16[400,128]{1,0:T(8,128)(2,1)S(1)} %get-tuple-element.184), channel_id=4, replica_groups=mesh['seq'=8,'wa'=4] {'seq'}, dimensions={0}, use_global_device_ids=true | all-gather | bytes 921600 | tf_op jit(solution)/shard_map/all_gather | solution.py:61
  200.8 4.7 collective-permute-done.18.refs_2_
  215.5 4.4 collective-permute-done.21.refs_2_
  225.5 5.1 feed_back.2
  239.5 4.4 collective-permute-done.24.refs_2_
  253.3 4.4 collective-permute-done.27.refs_3_
  261.4 10.9 %all-gather.4 = bf16[3968,128]{1,0:T(8,128)(2,1)S(1)} all-gather(bf16[496,128]{1,0:T(8,128)(2,1)S(1)} %get-tuple-element.215), channel_id=6, replica_groups=mesh['seq'=8,'wa'=4] {'seq'}, dimensions={0}, use_global_device_ids=true | all-gather | bytes 1142784 | tf_op jit(solution)/shard_map/all_gather | solution.py:61
  272.2 6.3 %mixer_grad.2 = (bf16[256,640]{1,0:T(8,128)(2,1)S(1)}, f32[16,640]{1,0:T(8,128)S(1)}, f32[8,640]{1,0:T(8,128)S(1)}, bf16[256,128]{1,0:T(8,128)(2,1)S(1)}, f32[8,640]{1,0:T(8,128)S(1)}, /*index=5*/f32[8,128]{1,0:T(8,128)S(1)}) custom-call(s32[1]{0:T(128)} %bitcast.1.refs_0_.refs_1_, bf16[8,496,128]{2,1,0:T(8,128)(2,1)S(1)} %bitcast.107, ...), custom_call_target="tpu_custom_call" | custom-call | flops 402653184 | bytes 4649988 | tf_op jit(solution)/shard_map/mixer_grad/pallas_call | solution.py:120
  279.9 12.3 %all-gather.5 = bf16[3456,128]{1,0:T(8,128)(2,1)S(1)} all-gather(bf16[432,128]{1,0:T(8,128)(2,1)S(1)} %get-tuple-element.216), channel_id=7, replica_groups=mesh['seq'=8,'wa'=4] {'seq'}, dimensions={0}, use_global_device_ids=true | all-gather | bytes 995328 | tf_op jit(solution)/shard_map/all_gather | solution.py:61
  305.4 6.3 %collective-permute-done.34.refs_2_ = bf16[64,1024]{1,0:T(8,128)(2,1)S(1)} collective-permute-done((bf16[64,1024]{1,0:T(8,128)(2,1)S(1)}, bf16[64,1024]{1,0:T(8,128)(2,1)S(1)}, u32[]{:S(2)}, u32[]{:S(2)}) %collective-permute-start.34) | collective-permute-done | bytes 131104 | tf_op jit(solution)/shard_map/ppermute | solution.py:88
  315.9 5.6 collective-permute-done.40.refs_1_.refs_9_
  339.6 5.0 collective-permute-done.41.refs_2_
  347.8 4.8 feed_back.3
  358.1 4.5 collective-permute-done.42.refs_1_.refs_5_
  375.1 4.7 collective-permute-done.46.refs_3_
  382.8 15.1 %all-gather.7 = bf16[3456,128]{1,0:T(8,128)(2,1)S(1)} all-gather(bf16[432,128]{1,0:T(8,128)(2,1)S(1)} %get-tuple-element.254), channel_id=9, replica_groups=mesh['seq'=8,'wa'=4] {'seq'}, dimensions={0}, use_global_device_ids=true | all-gather | bytes 995328 | tf_op jit(solution)/shard_map/all_gather | solution.py:61
  397.9 11.2 %all-gather.6 = bf16[3968,128]{1,0:T(8,128)(2,1)S(1)} all-gather(bf16[496,128]{1,0:T(8,128)(2,1)S(1)} %get-tuple-element.245), channel_id=8, replica_groups=mesh['seq'=8,'wa'=4] {'seq'}, dimensions={0}, use_global_device_ids=true | all-gather | bytes 1142784 | tf_op jit(solution)/shard_map/all_gather | solution.py:61
  421.5 7.0 %collective-permute-start.29 = (bf16[64,1024]{1,0:T(8,128)(2,1)}, bf16[64,1024]{1,0:T(8,128)(2,1)S(1)}, u32[]{:S(2)}, u32[]{:S(2)}) collective-permute-start(bf16[64,1024]{1,0:T(8,128)(2,1)} %get-tuple-element.212), channel_id=1, source_target_pairs={{0,1},{1,2},{2,3},{3,0},{4,5},{5,6},{6,7},{7,4},{8,9},{9,10},{10,1... | collective-permute-start | bytes 393224 | tf_op jit(solution)/shard_map/ppermute | solution.py:88
  440.2 6.7 %mixer_grad.3 = (bf16[256,640]{1,0:T(8,128)(2,1)S(1)}, f32[16,640]{1,0:T(8,128)S(1)}, f32[8,640]{1,0:T(8,128)}, bf16[256,128]{1,0:T(8,128)(2,1)S(1)}, f32[8,640]{1,0:T(8,128)S(1)}, /*index=5*/f32[8,128]{1,0:T(8,128)S(1)}) custom-call(s32[1]{0:T(128)} %bitcast.1.refs_0_.refs_1_, bf16[8,496,128]{2,1,0:T(8,128)(2,1)S(1)} %bitcast.106, ...), custom_call_target="tpu_custom_call" | custom-call | flops 402653184 | bytes 4649988 | tf_op jit(solution)/shard_map/mixer_grad/pallas_call | solution.py:120
  511.2 15.4 %all-gather.9 = f32[8,98,128]{2,1,0:T(8,128)S(1)} all-gather(f32[1,98,128]{2,1,0:T(8,128)S(1)} %bitcast.117), channel_id=10, replica_groups=mesh['seq'=8,'wa'=4] {'seq'}, dimensions={0}, use_global_device_ids=true | all-gather | bytes 451584 | tf_op jit(solution)/shard_map/all_gather | solution.py:61
  545.9 6.7 %collective-permute-done.73 = bf16[2,128,384]{2,1,0:T(8,128)(2,1)S(1)} collective-permute-done((bf16[2,128,384]{2,1,0:T(8,128)(2,1)S(1)}, bf16[2,128,384]{2,1,0:T(8,128)(2,1)S(1)}, u32[]{:S(2)}, u32[]{:S(2)}) %collective-permute-start.73) | collective-permute-done | bytes 196640 | tf_op jit(solution)/shard_map/ppermute | solution.py:81
  563.4 12.9 %reduce-scatter.12.cloned.1.call-done = bf16[128,1536]{1,0:T(8,128)(2,1)} async-done(((bf16[1024,1536]{1,0:T(8,128)(2,1)}), bf16[128,1536]{1,0:T(8,128)(2,1)}) %reduce-scatter.12.cloned.1.call-update) | async-done | bytes 393232 | tf_op jit(solution)/shard_map/reduce_scatter | solution.py:75
  (787 shorter events, 319.9 us)
Async XLA Ops:
  7.2 528.0 %reduce-scatter.10.cloned.1.call-start = ((), (), s32[]{:S(2)}) async-start(), calls=%async_computation.7 | async-start | bytes 2064384 | tf_op jit(solution)/shard_map/reduce_scatter | solution.py:75
  9.8 37.3 %collective-permute-start = (bf16[64,1024]{1,0:T(8,128)(2,1)S(1)}, bf16[64,1024]{1,0:T(8,128)(2,1)S(1)}, u32[]{:S(2)}, u32[]{:S(2)}) collective-permute-start(bf16[64,1024]{1,0:T(8,128)(2,1)S(1)} %norm_first.1.refs_1_), channel_id=1, source_target_pairs={{0,3},{1,0},{2,1},{3,2},{4,7},{5,4},{6,5},{7,6},{8,11},{9,8},{10,9... | collective-permute-start | bytes 393224 | tf_op jit(solution)/shard_map/ppermute | solution.py:81
  14.9 32.2 %collective-permute-start.1 = (bf16[64,1024]{1,0:T(8,128)(2,1)S(1)}, bf16[64,1024]{1,0:T(8,128)(2,1)S(1)}, u32[]{:S(2)}, u32[]{:S(2)}) collective-permute-start(bf16[64,1024]{1,0:T(8,128)(2,1)S(1)} %norm_first.1.refs_1_), channel_id=1, source_target_pairs={{0,2},{1,3},{2,0},{3,1},{4,6},{5,7},{6,4},{7,5},{8,10},{9,11},{10,... | collective-permute-start | bytes 393224 | tf_op jit(solution)/shard_map/ppermute | solution.py:81
  14.9 32.2 %collective-permute-start.2 = (bf16[64,1024]{1,0:T(8,128)(2,1)S(1)}, bf16[64,1024]{1,0:T(8,128)(2,1)}, u32[]{:S(2)}, u32[]{:S(2)}) collective-permute-start(bf16[64,1024]{1,0:T(8,128)(2,1)S(1)} %norm_first.1.refs_1_), channel_id=1, source_target_pairs={{0,1},{1,2},{2,3},{3,0},{4,5},{5,6},{6,7},{7,4},{8,9},{9,10},{10,1... | collective-permute-start | bytes 393224 | tf_op jit(solution)/shard_map/ppermute | solution.py:81
  103.4 13.4 %collective-permute-start.7 = (bf16[64,1024]{1,0:T(8,128)(2,1)}, bf16[64,1024]{1,0:T(8,128)(2,1)}, u32[]{:S(2)}, u32[]{:S(2)}) collective-permute-start(bf16[64,1024]{1,0:T(8,128)(2,1)} %get-tuple-element.175.refs_0_), channel_id=1, source_target_pairs={{0,1},{1,2},{2,3},{3,0},{4,5},{5,6},{6,7},{7,4},{8,9},{9,10},{10,1... | collective-permute-start | bytes 393224 | tf_op jit(solution)/shard_map/ppermute | solution.py:81
  140.9 12.2 %collective-permute-start.14 = (bf16[64,1024]{1,0:T(8,128)(2,1)S(1)}, bf16[64,1024]{1,0:T(8,128)(2,1)S(1)}, u32[]{:S(2)}, u32[]{:S(2)}) collective-permute-start(bf16[64,1024]{1,0:T(8,128)(2,1)S(1)} %get-tuple-element.181.refs_1_), channel_id=1, source_target_pairs={{0,2},{1,3},{2,0},{3,1},{4,6},{5,7},{6,4},{7,5},{8,10},{9,11},{10,... | collective-permute-start | bytes 393224 | tf_op jit(solution)/shard_map/ppermute | solution.py:81
  141.3 11.8 %collective-permute-start.15 = (bf16[64,1024]{1,0:T(8,128)(2,1)S(1)}, bf16[64,1024]{1,0:T(8,128)(2,1)S(1)}, u32[]{:S(2)}, u32[]{:S(2)}) collective-permute-start(bf16[64,1024]{1,0:T(8,128)(2,1)S(1)} %get-tuple-element.181.refs_1_), channel_id=1, source_target_pairs={{0,1},{1,2},{2,3},{3,0},{4,5},{5,6},{6,7},{7,4},{8,9},{9,10},{10,1... | collective-permute-start | bytes 393224 | tf_op jit(solution)/shard_map/ppermute | solution.py:81
  192.6 12.9 %collective-permute-start.18 = (bf16[64,1024]{1,0:T(8,128)(2,1)S(1)}, bf16[64,1024]{1,0:T(8,128)(2,1)S(1)}, u32[]{:S(2)}, u32[]{:S(2)}) collective-permute-start(bf16[64,1024]{1,0:T(8,128)(2,1)S(1)} %get-tuple-element.193), channel_id=1, source_target_pairs={{0,2},{1,3},{2,0},{3,1},{4,6},{5,7},{6,4},{7,5},{8,10},{9,11},{10,... | collective-permute-start | bytes 393224 | tf_op jit(solution)/shard_map/ppermute | solution.py:88
  193.9 11.7 %collective-permute-start.19 = (bf16[64,1024]{1,0:T(8,128)(2,1)S(1)}, bf16[64,1024]{1,0:T(8,128)(2,1)S(1)}, u32[]{:S(2)}, u32[]{:S(2)}) collective-permute-start(bf16[64,1024]{1,0:T(8,128)(2,1)S(1)} %get-tuple-element.194), channel_id=1, source_target_pairs={{0,3},{1,0},{2,1},{3,2},{4,7},{5,4},{6,5},{7,6},{8,11},{9,8},{10,9... | collective-permute-start | bytes 393224 | tf_op jit(solution)/shard_map/ppermute | solution.py:88
  278.6 16.5 %collective-permute-start.32 = (f32[8,640]{1,0:T(8,128)S(1)}, f32[8,640]{1,0:T(8,128)S(1)}, u32[]{:S(2)}, u32[]{:S(2)}) collective-permute-start(f32[8,640]{1,0:T(8,128)S(1)} %get-tuple-element.226), channel_id=1, source_target_pairs={{4,0},{8,4},{12,8},{16,12},{20,16},{24,20},{28,24},{5,1},{9,5},{13... | collective-permute-start | bytes 61448 | tf_op jit(solution)/shard_map/ppermute | solution.py:1126
  324.4 230.3 %reduce-scatter.8.cloned.1.call-start = ((), (), s32[]{:S(2)}) async-start(), calls=%async_computation.6 | async-start | bytes 2359296 | tf_op jit(solution)/shard_map/reduce_scatter | solution.py:75
  333.3 222.4 %reduce-scatter.6.cloned.1.call-start = ((), (), s32[]{:S(2)}) async-start(), calls=%async_computation.5 | async-start | bytes 2359296 | tf_op jit(solution)/shard_map/reduce_scatter | solution.py:75
  333.6 11.0 %collective-permute-start.41 = (bf16[64,1024]{1,0:T(8,128)(2,1)}, bf16[64,1024]{1,0:T(8,128)(2,1)S(1)}, u32[]{:S(2)}, u32[]{:S(2)}) collective-permute-start(bf16[64,1024]{1,0:T(8,128)(2,1)} %copy-done.167), channel_id=1, source_target_pairs={{0,2},{1,3},{2,0},{3,1},{4,6},{5,7},{6,4},{7,5},{8,10},{9,11},{10,... | collective-permute-start | bytes 393224 | tf_op jit(solution)/shard_map/ppermute | solution.py:81
  354.3 11.8 %collective-permute-start.43 = (bf16[64,1024]{1,0:T(8,128)(2,1)S(1)}, bf16[64,1024]{1,0:T(8,128)(2,1)S(1)}, u32[]{:S(2)}, u32[]{:S(2)}) collective-permute-start(bf16[64,1024]{1,0:T(8,128)(2,1)S(1)} %get-tuple-element.238), channel_id=1, source_target_pairs={{0,2},{1,3},{2,0},{3,1},{4,6},{5,7},{6,4},{7,5},{8,10},{9,11},{10,... | collective-permute-start | bytes 393224 | tf_op jit(solution)/shard_map/ppermute | solution.py:88
  415.6 145.3 %reduce-scatter.14.cloned.1.call-start = ((), (), s32[]{:S(2)}) async-start(), calls=%async_computation.9 | async-start | bytes 3538944 | tf_op jit(solution)/shard_map/reduce_scatter | solution.py:75
  421.4 154.8 %reduce-scatter.12.cloned.1.call-start = ((), (), s32[]{:S(2)}) async-start(), calls=%async_computation.8 | async-start | bytes 3538944 | tf_op jit(solution)/shard_map/reduce_scatter | solution.py:75
  421.5 26.7 %collective-permute-start.29 = (bf16[64,1024]{1,0:T(8,128)(2,1)}, bf16[64,1024]{1,0:T(8,128)(2,1)S(1)}, u32[]{:S(2)}, u32[]{:S(2)}) collective-permute-start(bf16[64,1024]{1,0:T(8,128)(2,1)} %get-tuple-element.212), channel_id=1, source_target_pairs={{0,1},{1,2},{2,3},{3,0},{4,5},{5,6},{6,7},{7,4},{8,9},{9,10},{10,1... | collective-permute-start | bytes 393224 | tf_op jit(solution)/shard_map/ppermute | solution.py:88
  428.5 19.7 %collective-permute-start.30 = (bf16[64,1024]{1,0:T(8,128)(2,1)}, bf16[64,1024]{1,0:T(8,128)(2,1)S(1)}, u32[]{:S(2)}, u32[]{:S(2)}) collective-permute-start(bf16[64,1024]{1,0:T(8,128)(2,1)} %get-tuple-element.213), channel_id=1, source_target_pairs={{0,2},{1,3},{2,0},{3,1},{4,6},{5,7},{6,4},{7,5},{8,10},{9,11},{10,... | collective-permute-start | bytes 393224 | tf_op jit(solution)/shard_map/ppermute | solution.py:88
  430.5 17.7 %collective-permute-start.31 = (bf16[64,1024]{1,0:T(8,128)(2,1)}, bf16[64,1024]{1,0:T(8,128)(2,1)S(1)}, u32[]{:S(2)}, u32[]{:S(2)}) collective-permute-start(bf16[64,1024]{1,0:T(8,128)(2,1)} %get-tuple-element.214), channel_id=1, source_target_pairs={{0,3},{1,0},{2,1},{3,2},{4,7},{5,4},{6,5},{7,6},{8,11},{9,8},{10,9... | collective-permute-start | bytes 393224 | tf_op jit(solution)/shard_map/ppermute | solution.py:88
  452.3 18.9 %collective-permute-start.37 = (bf16[64,1024]{1,0:T(8,128)(2,1)}, bf16[64,1024]{1,0:T(8,128)(2,1)S(1)}, u32[]{:S(2)}, u32[]{:S(2)}) collective-permute-start(bf16[64,1024]{1,0:T(8,128)(2,1)} %held_back.3.refs_1_), channel_id=1, source_target_pairs={{0,1},{1,2},{2,3},{3,0},{4,5},{5,6},{6,7},{7,4},{8,9},{9,10},{10,1... | collective-permute-start | bytes 393224 | tf_op jit(solution)/shard_map/ppermute | solution.py:81
  453.9 17.9 %collective-permute-start.38 = (bf16[64,1024]{1,0:T(8,128)(2,1)}, bf16[64,1024]{1,0:T(8,128)(2,1)S(1)}, u32[]{:S(2)}, u32[]{:S(2)}) collective-permute-start(bf16[64,1024]{1,0:T(8,128)(2,1)} %held_back.3.refs_1_), channel_id=1, source_target_pairs={{0,2},{1,3},{2,0},{3,1},{4,6},{5,7},{6,4},{7,5},{8,10},{9,11},{10,... | collective-permute-start | bytes 393224 | tf_op jit(solution)/shard_map/ppermute | solution.py:81
  454.8 19.3 %collective-permute-start.39 = (bf16[64,1024]{1,0:T(8,128)(2,1)}, bf16[64,1024]{1,0:T(8,128)(2,1)S(1)}, u32[]{:S(2)}, u32[]{:S(2)}) collective-permute-start(bf16[64,1024]{1,0:T(8,128)(2,1)} %held_back.3.refs_1_), channel_id=1, source_target_pairs={{0,3},{1,0},{2,1},{3,2},{4,7},{5,4},{6,5},{7,6},{8,11},{9,8},{10,9... | collective-permute-start | bytes 393224 | tf_op jit(solution)/shard_map/ppermute | solution.py:81
  479.8 15.0 %collective-permute-start.58 = (bf16[128,512]{1,0:T(8,128)(2,1)}, bf16[128,512]{1,0:T(8,128)(2,1)}, u32[]{:S(2)}, u32[]{:S(2)}) collective-permute-start(bf16[128,512]{1,0:T(8,128)(2,1)} %get-tuple-element.277), channel_id=1, source_target_pairs={{0,4},{4,8},{8,12},{12,16},{16,20},{20,24},{24,28},{28,0},{1,5},{5... | collective-permute-start | bytes 393224 | tf_op jit(solution)/shard_map/ppermute | solution.py:68
  479.9 16.6 %collective-permute-start.59 = (bf16[128,512]{1,0:T(8,128)(2,1)}, bf16[128,512]{1,0:T(8,128)(2,1)}, u32[]{:S(2)}, u32[]{:S(2)}) collective-permute-start(bf16[128,512]{1,0:T(8,128)(2,1)} %get-tuple-element.278), channel_id=1, source_target_pairs={{0,8},{4,12},{8,16},{12,20},{16,24},{20,28},{24,0},{28,4},{1,9},{5... | collective-permute-start | bytes 393224 | tf_op jit(solution)/shard_map/ppermute | solution.py:68
  481.1 16.2 %collective-permute-start.49 = (bf16[64,1024]{1,0:T(8,128)(2,1)}, bf16[64,1024]{1,0:T(8,128)(2,1)S(1)}, u32[]{:S(2)}, u32[]{:S(2)}) collective-permute-start(bf16[64,1024]{1,0:T(8,128)(2,1)} %get-tuple-element.259), channel_id=1, source_target_pairs={{0,1},{1,2},{2,3},{3,0},{4,5},{5,6},{6,7},{7,4},{8,9},{9,10},{10,1... | collective-permute-start | bytes 393224 | tf_op jit(solution)/shard_map/ppermute | solution.py:88
  481.4 16.2 %collective-permute-start.50 = (bf16[64,1024]{1,0:T(8,128)(2,1)}, bf16[64,1024]{1,0:T(8,128)(2,1)S(1)}, u32[]{:S(2)}, u32[]{:S(2)}) collective-permute-start(bf16[64,1024]{1,0:T(8,128)(2,1)} %get-tuple-element.260), channel_id=1, source_target_pairs={{0,2},{1,3},{2,0},{3,1},{4,6},{5,7},{6,4},{7,5},{8,10},{9,11},{10,... | collective-permute-start | bytes 393224 | tf_op jit(solution)/shard_map/ppermute | solution.py:88
  483.4 16.4 %collective-permute-start.51 = (bf16[64,1024]{1,0:T(8,128)(2,1)}, bf16[64,1024]{1,0:T(8,128)(2,1)S(1)}, u32[]{:S(2)}, u32[]{:S(2)}) collective-permute-start(bf16[64,1024]{1,0:T(8,128)(2,1)} %get-tuple-element.261), channel_id=1, source_target_pairs={{0,3},{1,0},{2,1},{3,2},{4,7},{5,4},{6,5},{7,6},{8,11},{9,8},{10,9... | collective-permute-start | bytes 393224 | tf_op jit(solution)/shard_map/ppermute | solution.py:88
  497.6 11.9 %collective-permute-start.63 = (bf16[128,512]{1,0:T(8,128)(2,1)S(1)}, bf16[128,512]{1,0:T(8,128)(2,1)S(1)}, u32[]{:S(2)}, u32[]{:S(2)}) collective-permute-start(bf16[128,512]{1,0:T(8,128)(2,1)S(1)} %get-tuple-element.282), channel_id=1, source_target_pairs={{0,24},{4,28},{8,0},{12,4},{16,8},{20,12},{24,16},{28,20},{1,25},{... | collective-permute-start | bytes 393224 | tf_op jit(solution)/shard_map/ppermute | solution.py:68
  505.5 26.7 %collective-permute-start.53 = (bf16[64,1024]{1,0:T(8,128)(2,1)S(1)}, bf16[64,1024]{1,0:T(8,128)(2,1)S(1)}, u32[]{:S(2)}, u32[]{:S(2)}) collective-permute-start(bf16[64,1024]{1,0:T(8,128)(2,1)S(1)} %get-tuple-element.263.refs_1_), channel_id=1, source_target_pairs={{0,2},{1,3},{2,0},{3,1},{4,6},{5,7},{6,4},{7,5},{8,10},{9,11},{10,... | collective-permute-start | bytes 393224 | tf_op jit(solution)/shard_map/ppermute | solution.py:81
  507.9 24.3 %collective-permute-start.54 = (bf16[64,1024]{1,0:T(8,128)(2,1)S(1)}, bf16[64,1024]{1,0:T(8,128)(2,1)S(1)}, u32[]{:S(2)}, u32[]{:S(2)}) collective-permute-start(bf16[64,1024]{1,0:T(8,128)(2,1)S(1)} %get-tuple-element.263.refs_1_), channel_id=1, source_target_pairs={{0,3},{1,0},{2,1},{3,2},{4,7},{5,4},{6,5},{7,6},{8,11},{9,8},{10,9... | collective-permute-start | bytes 393224 | tf_op jit(solution)/shard_map/ppermute | solution.py:81
  537.9 14.8 %collective-permute-start.73 = (bf16[2,128,384]{2,1,0:T(8,128)(2,1)S(1)}, bf16[2,128,384]{2,1,0:T(8,128)(2,1)S(1)}, u32[]{:S(2)}, u32[]{:S(2)}) collective-permute-start(bf16[2,128,384]{2,1,0:T(8,128)(2,1)S(1)} %pad_maximum_fusion.5), channel_id=1, source_target_pairs={{0,2},{1,3},{2,0},{3,1},{4,6},{5,7},{6,4},{7,5},{8,10},{9,11},{10,... | collective-permute-start | bytes 589832 | tf_op jit(solution)/shard_map/ppermute | solution.py:81
  540.2 12.5 %collective-permute-start.74 = (bf16[2,128,384]{2,1,0:T(8,128)(2,1)S(1)}, bf16[2,128,384]{2,1,0:T(8,128)(2,1)S(1)}, u32[]{:S(2)}, u32[]{:S(2)}) collective-permute-start(bf16[2,128,384]{2,1,0:T(8,128)(2,1)S(1)} %pad_maximum_fusion.5), channel_id=1, source_target_pairs={{0,3},{1,0},{2,1},{3,2},{4,7},{5,4},{6,5},{7,6},{8,11},{9,8},{10,9... | collective-permute-start | bytes 589832 | tf_op jit(solution)/shard_map/ppermute | solution.py:81
  (293 other events, 3753.0 us)
Sparse Core Ops, SparseCore 0:
  324.5 40.1 reduce-scatter.9
  367.9 44.2 reduce-scatter.7
  415.8 49.3 reduce-scatter.5
  468.4 57.9 reduce-scatter.13
  530.0 46.1 reduce-scatter.11

commit v3 on v2

--- a/solution.py
+++ b/solution.py
@@ -72,7 +72,7 @@
         for part in got:
             total = total + part.astype(F32)
         return total
-    return lax.psum_scatter(blocks[0], "seq", scatter_dimension=0, tiled=True).astype(F32)
+    return lax.psum_scatter(blocks[0], "seq", scatter_dimension=0, tiled=True)
 
 
 def gather_wa(block):
@@ -228,7 +228,7 @@
     )
 
 
-def norm_back(parts, hidden, gain, grad):
+def norm_back(parts, hidden, gain, grad, ties):
     rows, width = hidden.shape
     n = len(parts)
 
@@ -253,6 +253,7 @@
         body,
         [((rows, width), F32), ((rows, width), BF), ((1, width), F32)],
         [*parts, hidden, gain, grad],
+        ties=ties,
     )
 
 
@@ -277,7 +278,7 @@
         q_ref[...] = (q * cq_ref[...] + halves_swapped(q) * sq_ref[...]).astype(BF)
         r_ref[...] = mm(x, wdt_ref[...])
         u_ref[:, inner:] = mm(x, wbc_ref[...])
-        gate_ref[...] = mm(x, wzx_ref[:, :inner])
+        gate_ref[...] = mm(x, wzx_ref[:, :inner]).astype(BF)
         u_ref[:, :inner] = mm(x, wzx_ref[:, inner:])
 
     return kernel_call(
@@ -285,7 +286,7 @@
         body,
         [
             ((tokens, width), BF),
-            ((tokens, inner), F32),
+            ((tokens, inner), BF),
             ((tokens, mix), F32),
             ((tokens, 128), F32),
             ((tokens, 128), BF),
@@ -296,27 +297,31 @@
     )
 
 
+def convolved(pad_ref, cw_ref, tk, tokens):
+    mix = pad_ref.shape[1]
+    conv = jnp.broadcast_to(cw_ref[KC : KC + 1, :], (tokens, mix))
+    for j in range(KC):
+        at = 16 - (KC - 1) + j
+        conv = conv + cw_ref[j : j + 1, :] * pad_ref[at : at + tokens, :] * tk[:, j : j + 1]
+    return conv
+
+
 def mixer_front(edge, u, r_raw, wzx, wbc, conv_w, hp, tok):
     tokens, mix = u.shape
     inner = mix - 2 * NS
 
     def body(
         edge_ref, u_ref, r_ref, wzx_ref, wbc_ref, cw_ref, hp_ref, tok_ref,
-        pad_ref, act_ref, slope_ref, hd_ref, pack_ref,
+        pad_ref, act_ref, hd_ref, pack_ref,
     ):
         e = edge_ref[...]
         pad_ref[:16, :inner] = mm(e, wzx_ref[:, inner:])
         pad_ref[:16, inner:] = mm(e, wbc_ref[...])
         pad_ref[16:, :] = u_ref[...]
         tk = tok_ref[...]
-        conv = jnp.broadcast_to(cw_ref[KC : KC + 1, :], (tokens, mix))
-        for j in range(KC):
-            shifted = pad_ref[16 - (KC - 1) + j : 16 - (KC - 1) + j + tokens, :]
-            conv = conv + cw_ref[j : j + 1, :] * shifted * tk[:, j : j + 1]
-        sg = sigmoid(conv)
-        act = conv * sg
-        act_ref[...] = act
-        slope_ref[...] = sg * (1.0 + conv * (1.0 - sg))
+        conv = convolved(pad_ref, cw_ref, tk, tokens)
+        act = conv * sigmoid(conv)
+        act_ref[...] = act.astype(BF)
         r = r_ref[...] + hp_ref[0:1, :]
         dt = jnp.maximum(r, 0.0) + jnp.log1p(jnp.exp(-jnp.abs(r)))
         log_decay = -dt * jnp.exp(hp_ref[1:2, :])
@@ -336,8 +341,7 @@
         body,
         [
             ((tokens + 16, mix), F32),
-            ((tokens, mix), F32),
-            ((tokens, mix), F32),
+            ((tokens, mix), BF),
             ((3, tokens, 128), F32),
             ((inner + 16, NS), BF),
         ],
@@ -386,7 +390,7 @@
 
     def body(act_ref, hd_ref, segc_ref, segr_ref, hp_ref, y_ref):
         lane = iota((tokens, 128), 1)
-        act_all = act_ref[...]
+        act_all = act_ref[...].astype(F32)
         b_mat = act_all[:, inner : inner + NS]
         c_mat = act_all[:, inner + NS :]
         both = mm_nt(c_mat, b_mat)
@@ -486,8 +490,8 @@
         state_ref[...] = state
         decay_in = jnp.exp(hd_ref[2]) * tok_ref[:, 4:5]
         y = y_ref[...] + mm_nt(act_ref[:, inner + NS :], state) * expand(decay_in, inner)
-        yy_ref[...] = y
-        gate_raw = gate_ref[...]
+        yy_ref[...] = y.astype(BF)
+        gate_raw = gate_ref[...].astype(F32)
         gated = (y * gate_raw * sigmoid(gate_raw)).astype(BF)
         gated_ref[...] = gated
         full_ref[...] = mm(gated, wout_ref[...]) + mm(flat_ref[...], wao_ref[...])
@@ -496,7 +500,7 @@
     return kernel_call(
         "mixer_out",
         body,
-        [((inner, NS), F32), ((tokens, inner), F32), ((tokens, inner), BF)]
+        [((inner, NS), F32), ((tokens, inner), BF), ((tokens, inner), BF)]
         + [((rows, width), F32)]
         + [((rows, width), BF)] * (wa_count - 1),
         [me, here, states, y_local, act, hd, tok, gate, flat, wout, wao],
@@ -519,8 +523,8 @@
         x = n_ref[...]
         gate = mm(x, wgu_ref[:, :hidden])
         up = mm(x, wgu_ref[:, hidden:])
-        gu_ref[:, :hidden] = gate
-        gu_ref[:, hidden:] = up
+        gu_ref[:, :hidden] = gate.astype(BF)
+        gu_ref[:, hidden:] = up.astype(BF)
         act = (gate * sigmoid(gate) * up).astype(BF)
         act_ref[...] = act
         for d in range(n):
@@ -531,7 +535,7 @@
     return kernel_call(
         "feed_forward",
         body,
-        [((tokens, width), BF), ((tokens, 2 * hidden), F32), ((tokens, hidden), BF)]
+        [((tokens, width), BF), ((tokens, 2 * hidden), BF), ((tokens, hidden), BF)]
         + [((rows, width), F32)]
         + [((rows, width), BF)] * (n - 1),
         [*parts, wgu, wdown],
@@ -551,8 +555,8 @@
         for d in range(n):
             gb_ref[d * rows : (d + 1) * rows, :] = refs[d][...]
         d_act = mm_nt(gb_ref[...], wdown_ref[...])
-        gate = gu_ref[:, :hidden]
-        up = gu_ref[:, hidden:]
+        gate = gu_ref[:, :hidden].astype(F32)
+        up = gu_ref[:, hidden:].astype(F32)
         sg = sigmoid(gate)
         dgu_ref[:, :hidden] = (d_act * up * sg * (1.0 + gate * (1.0 - sg))).astype(BF)
         dgu_ref[:, hidden:] = (d_act * gate * sg).astype(BF)
@@ -572,38 +576,53 @@
     )
 
 
-def weight_grads(here, pairs, n, direct, ties=()):
-    width = pairs[0][0].shape[1]
-    columns = sum(right.shape[1] for left, right in pairs)
-    flat = [a for pair in pairs for a in pair]
-    direct = direct and n <= DIRECT_MOST
-    blocks = n if direct else 1
-    rows = width // blocks
+def weight_grads(here, groups, n, ties=()):
+    width = groups[0][0][0][0].shape[1]
+    flat = [a for pairs, _ in groups for pair in pairs for a in pair]
+    plan, shapes = [], []
+    for pairs, direct in groups:
+        blocks = n if direct and n <= DIRECT_MOST else 1
+        columns = sum(right.shape[1] for _, right in pairs)
+        plan.append((len(pairs), blocks))
+        shapes += [
+            ((width // blocks, columns), F32 if blocks > 1 and d == 0 else BF)
+            for d in range(blocks)
+        ]
 
     def body(*refs):
         here_ref = refs[0]
-        outs = refs[1 + len(flat) :]
-        for d in range(blocks):
-            start = 0
-            for k in range(len(pairs)):
-                left, right = refs[1 + 2 * k], refs[2 + 2 * k]
-                wide = right.shape[1]
-                if direct:
-                    at = pl.multiple_of(lax.rem(here_ref[0] + d, n) * rows, rows)
-                    piece = left[:, pl.ds(at, rows)]
-                else:
-                    piece = left[...]
-                outs[d][:, start : start + wide] = mm_tn(piece, right[...]).astype(outs[d].dtype)
-                start += wide
-
-    return kernel_call(
+        source, out = 1, 1 + len(flat)
+        for count, blocks in plan:
+            for d in range(blocks):
+                rows = width // blocks
+                start = 0
+                for k in range(count):
+                    left, right = refs[source + 2 * k], refs[source + 2 * k + 1]
+                    if blocks > 1:
+                        at = pl.multiple_of(lax.rem(here_ref[0] + d, n) * rows, rows)
+                        piece = left[:, pl.ds(at, rows)]
+                    else:
+                        piece = left[...]
+                    wide = right.shape[1]
+                    target = refs[out + d]
+                    target[:, start : start + wide] = mm_tn(piece, right[...]).astype(target.dtype)
+                    start += wide
+            source += 2 * count
+            out += blocks
+
+    got = kernel_call(
         "weight_grads",
         body,
-        [((rows, columns), F32 if direct and d == 0 else BF) for d in range(blocks)],
+        shapes,
         [here, *flat],
-        flops=2 * pairs[0][0].shape[0] * width * columns,
+        flops=2 * flat[0].shape[0] * width * sum(a.shape[1] for a in flat[1::2]),
         ties=ties,
     )
+    out = []
+    for _, blocks in plan:
+        out.append(got[:blocks])
+        got = got[blocks:]
+    return out
 
 
 def mixer_grad_in(me, parts, wout, wao, gate, y, act, hd, tok, o2, q_own):
@@ -619,12 +638,12 @@
         ordered(me_ref, refs[1 : 1 + n], nat_ref)
         mb = nat_ref[...]
         d_gated = mm_nt(mb, wout_ref[...])
-        gate_raw = gate_ref[...]
+        gate_raw = gate_ref[...].astype(F32)
         sg = sigmoid(gate_raw)
         dy = d_gated * gate_raw * sg
-        dy_ref[...] = dy
+        dy_ref[...] = dy.astype(BF)
         dgate_ref[...] = (
-            d_gated * y_ref[...] * sg * (1.0 + gate_raw * (1.0 - sg))
+            d_gated * y_ref[...].astype(F32) * sg * (1.0 + gate_raw * (1.0 - sg))
         ).astype(BF)
         cum = hd_ref[2]
         decay_in = jnp.exp(cum) * tok_ref[:, 4:5]
@@ -657,7 +676,7 @@
         body,
         [
             ((tokens, width), BF),
-            ((tokens, inner), F32),
+            ((tokens, inner), BF),
             ((tokens, inner), BF),
             ((inner + 16 + early, NS), BF),
             ((tokens + 16 + tokens - early, 128), BF),
@@ -670,7 +689,7 @@
 
 def attend_back(
     here, every, states_back, every_back, delta, o2, q_own, segc, segrel, seglater, blocks,
-    cos_q, sin_q, cos_kv, sin_kv, inner,
+    cos_q, sin_q, cos_kv, sin_kv, inner, ties,
 ):
     n = every.shape[0]
     tokens = segc.shape[0]
@@ -748,27 +767,31 @@
             cos_q, sin_q, cos_kv, sin_kv,
         ],
         flops=2 * rows * tokens * 128 * 7 * n,
-    )
-
-
-def mixer_grad(here, every_back, state_in, dy, act, slope, pad, hd, tok, segc, segrel, hp, conv_w):
+        ties=ties,
+    )
+
+
+def mixer_grad(here, every_back, state_in, dy, pad, hd, tok, segc, segrel, hp, conv_w):
     tokens, inner = dy.shape
-    mix = act.shape[1]
+    mix = pad.shape[1]
 
     def body(*refs):
         (
-            here_ref, back_ref, state_ref, dy_ref, act_ref, slope_ref, pad_ref, hd_ref, tok_ref, segc_ref, segr_ref,
+            here_ref, back_ref, state_ref, dy_ref, pad_ref, hd_ref, tok_ref, segc_ref, segr_ref,
             hp_ref, cw_ref, dmix_ref, tail_ref, edge_ref, ddt_ref, gconv_ref, ghead_ref,
-            dconv_ref, dpad_ref, dxs_ref,
+            dconv_ref, dpad_ref, dxs_ref, slope_ref,
         ) = refs
         later = fold_states(back_ref, inner, here_ref[0], True)
         state = state_ref[...]
         tk = tok_ref[...]
-        act_all = act_ref[...]
+        conv = convolved(pad_ref, cw_ref, tk, tokens)
+        sg = sigmoid(conv)
+        slope_ref[...] = sg * (1.0 + conv * (1.0 - sg))
+        act_all = conv * sg
         x = act_all[:, :inner]
         b_mat = act_all[:, inner : inner + NS]
         c_mat = act_all[:, inner + NS :]
-        dy_all = dy_ref[...]
+        dy_all = dy_ref[...].astype(F32)
         r, dt, cum = hd_ref[0], hd_ref[1], hd_ref[2]
         cum_t = cum.T
         last = cum[tokens - 1 :, :]
@@ -862,18 +885,19 @@
             ((8, mix), F32),
             ((8, 128), F32),
         ],
-        [here, every_back, state_in, dy, act, slope, pad, hd, tok, segc, segrel, hp, conv_w],
+        [here, every_back, state_in, dy, pad, hd, tok, segc, segrel, hp, conv_w],
         scratch=[
             pltpu.VMEM((tokens, mix), F32),
             pltpu.VMEM((tokens + 16, mix), F32),
             pltpu.VMEM((tokens, inner), F32),
+            pltpu.VMEM((tokens, mix), F32),
         ],
         flops=2 * tokens * tokens * 128 * 24,
     )
 
 
 def grads_out(
-    me, dgate, dmix, tail, next_edge, ddt, dq, dkv, wzx, wbc, wdt, wq, kvw, wa_count
+    me, dgate, dmix, tail, next_edge, ddt, dq, dkv, wzx, wbc, wdt, wq, kvw, wa_count, ties
 ):
     tokens, inner = dgate.shape
     mix = dmix.shape[1]
@@ -907,6 +931,7 @@
         [me, dgate, dmix, tail, next_edge, ddt, dq, dkv, wzx, wbc, wdt, wq, kvw],
         scratch=[pltpu.VMEM((tokens, width), F32)],
         flops=2 * tokens * width * (mix + 768),
+        ties=ties,
     )
 
 
@@ -1018,20 +1043,20 @@
     segrel = segrel[:, None, :]
     seglater = seglater[:, None, :]
     segc = seg_here[:, None]
-    columns = [(seg_full[j : j + tokens] == seg_here).astype(F32) for j in range(KC)]
-    columns.append((seg_here == seg_edge[KC - 2]).astype(F32))
-    columns.append((seg_here == seg_here[tokens - 1]).astype(F32))
-    tok = jnp.pad(jnp.stack(columns, axis=1), ((0, 0), (0, 128 - len(columns))))
+    lane = iota((tokens, 128), 1)
+    tok = jnp.zeros((tokens, 128), F32)
+    conditions = [seg_full[j : j + tokens] == seg_here for j in range(KC)]
+    conditions.append(seg_here == seg_edge[KC - 2])
+    conditions.append(seg_here == seg_here[tokens - 1])
+    for k, condition in enumerate(conditions):
+        tok = jnp.where((lane == k) & condition[:, None], 1.0, tok)
     half = HEAD_SIZE // 2
-    frequency = jnp.exp(jnp.arange(half, dtype=F32) * (-math.log(theta) / half))
-    positions = (start_row + jnp.arange(tokens, dtype=jnp.int32)).astype(F32)
-    angles = positions[:, None] * frequency[None, :]
-    cosine, sine = jnp.cos(angles), jnp.sin(angles)
-    cos_q = jnp.concatenate([cosine] * 4, axis=1)
-    sin_q = jnp.concatenate([-sine, sine, -sine, sine], axis=1)
-    ones = jnp.ones((tokens, HEAD_SIZE), F32)
-    cos_kv = jnp.concatenate([cosine, cosine, ones], axis=1)
-    sin_kv = jnp.concatenate([-sine, sine, 0.0 * ones], axis=1)
+    frequency = jnp.exp((lane % half).astype(F32) * (-math.log(theta) / half))
+    angles = (start_row + iota((tokens, 128), 0)).astype(F32) * frequency
+    cos_q = jnp.cos(angles)
+    sin_q = jnp.where(lane % HEAD_SIZE < half, -1.0, 1.0) * jnp.sin(angles)
+    cos_kv = jnp.where(lane < HEAD_SIZE, cos_q, 1.0)
+    sin_kv = jnp.where(lane < HEAD_SIZE, sin_q, 0.0)
 
     wzx_all = w_zx.reshape(LAYER_COUNT, width, 2 * inner)
     wgu_all = w_gu.reshape(LAYER_COUNT, width, 2 * hidden)
@@ -1065,7 +1090,7 @@
             me, normed_parts, wzx, wbc, wdt, wq, kvw, cos_q, sin_q, cos_kv, sin_kv
         )
         every = gather_seq(kv)
-        pad, act, slope, hd, pack = mixer_front(
+        pad, act, hd, pack = mixer_front(
             edge, u, r_raw, wzx, wbc, conv_w, hp, tok
         )
         states = gather_seq(pack)
@@ -1077,7 +1102,7 @@
         mixed, normed_two = norm_step(scatter_wa(parts), h, norm_gains[layer, 1][None, :])
         n2, gu, act_ff, *parts = feed_forward(gather_wa(normed_two), wgu, wdown)
         saved.append(
-            (h, nat, every, q_own, gate, pad, act, slope, hd, o2, flat, state_in, y, gated,
+            (h, nat, every, q_own, gate, pad, act, hd, o2, flat, state_in, y, gated,
              mixed, n2, gu, act_ff)
         )
         if layer + 1 < LAYER_COUNT:
@@ -1097,15 +1122,17 @@
         wzx, wbc, wdt, wq = [(a, layer) for a in (wzx_all, w_bc, wdt_all, w_q)]
         kvw, conv_w, hp = [(a, layer) for a in (kvw_all, conv_all, hp_all)]
         wout, wao, wgu, wdown = [(a, layer) for a in (w_out, w_ao, wgu_all, w_down)]
-        (h_in, nat, every, q_own, gate, pad, act, slope, hd, o2, flat, state_in, y, gated,
+        (h_in, nat, every, q_own, gate, pad, act, hd, o2, flat, state_in, y, gated,
          mixed, n2, gu, act_ff) = saved[layer]
         gb, dgu, *parts = feed_back(grad_parts, gu, wgu, wdown)
         parts = scatter_wa(parts)
-        sum_ff = scatter_rows(
-            weight_grads(here, [(gb, act_ff), (n2, dgu)], seq_count, False, [parts[1]])
-        )
+        ff_pairs = [(gb, act_ff), (n2, dgu)]
+        grad_ties = []
+        if not layer:
+            early = weight_grads(here, [(ff_pairs, False)], seq_count)[0]
+            grad_ties = list(early)
         d_mixed, mixed_b, gain_two = norm_back(
-            parts, mixed, norm_gains[layer, 1][None, :], grad
+            parts, mixed, norm_gains[layer, 1][None, :], grad, grad_ties
         )
         mixed_parts = gather_wa(mixed_b)
         mb, dy, dgate, pack, da, delta = mixer_grad_in(
@@ -1113,50 +1140,61 @@
         )
         states_back = gather_seq(pack)
         every_back = gather_seq(da)
+        mix_pairs = [(mb, gated), (mb, flat), (nat, dgate)]
+        if layer == LAYER_COUNT - 1:
+            out_parts = scatter_wa(held_back(last_parts, [delta]))
+            out_ties = out_parts[1:]
+        if not layer:
+            early = held_back(list(early), [joint, every_back])
+            out_ties = list(early)
+            sum_ff = scatter_rows(early)
         dq, dkv = attend_back(
             here, every, states_back, every_back, delta, o2, q_own, segc, segrel, seglater,
-            blocks_used, cos_q, sin_q, cos_kv, sin_kv, inner,
-        )
-        if layer == LAYER_COUNT - 1:
-            out_parts = scatter_wa(held_back(last_parts, [delta]))
-            h = norm_step(out_parts, last_mixed, norm_gains[layer, 0][None, :], [dq])[0]
+            blocks_used, cos_q, sin_q, cos_kv, sin_kv, inner, out_ties,
+        )
         dmix, tail, edge_grad, ddt, gconv, ghead = mixer_grad(
-            here, states_back, state_in, dy, act, slope, pad, hd, tok, segc, segrel, hp, conv_w
+            here, states_back, state_in, dy, pad, hd, tok, segc, segrel, hp, conv_w
         )
         next_edge = lax.ppermute(
             edge_grad, "seq", [(i + 1, i) for i in range(seq_count - 1)]
         )
         dx, dbc, *parts = grads_out(
-            me, dgate, dmix, tail, next_edge, ddt, dq, dkv, wzx, wbc, wdt, wq, kvw, wa_count
+            me, dgate, dmix, tail, next_edge, ddt, dq, dkv, wzx, wbc, wdt, wq, kvw, wa_count, []
         )
         parts = scatter_wa(parts)
-        mix_pairs = [(mb, gated), (mb, flat), (nat, dgate), (nat, dq)]
+        every_pairs = [(nat, dbc), (nat, dkv)]
+        in_pairs = [(nat, dx), (nat, dq), (nat, ddt)]
         if layer:
-            sum_mix = scatter_rows(
-                weight_grads(here, mix_pairs, seq_count, False, [parts[1]])
-            )
+            joint = weight_grads(
+                here, [(ff_pairs + mix_pairs + every_pairs + in_pairs, False)], seq_count
+            )[0]
+            back_ties = list(joint)
+            joint = scatter_rows(joint)
+            cuts = [3 * hidden, 2 * inner + 128, 2 * NS + 128, inner + 256]
+            ends = [sum(cuts[: k + 1]) for k in range(4)]
+            sum_ff, sum_mix, sum_every, sum_in = [
+                joint[:, end - size : end] for end, size in zip(ends, cuts)
+            ]
+            h = norm_step(out_parts, last_mixed, norm_gains[layer, 0][None, :], [parts[1]])[0]
         else:
-            sum_mix = scatter_rows(weight_grads(here, mix_pairs, seq_count, False))
-            sum_every = scatter_rows(
-                weight_grads(here, [(nat, dbc), (nat, dkv)], seq_count, True)
-            )
-            sum_in = scatter_rows(weight_grads(here, [(nat, dx), (nat, ddt)], seq_count, True))
+            joint = weight_grads(
+                here, [(every_pairs + mix_pairs + in_pairs, False)], seq_count
+            )[0]
+            back_ties = list(joint)
+            joint = scatter_rows(joint)
+            cuts = [2 * NS + 128, 2 * inner + 128, inner + 256]
+            ends = [sum(cuts[: k + 1]) for k in range(3)]
+            sum_every, sum_mix, sum_in = [
+                joint[:, end - size : end] for end, size in zip(ends, cuts)
+            ]
         grad, grad_b, gain_one = norm_back(
-            parts, h_in, norm_gains[layer, 0][None, :], d_mixed
+            parts, h_in, norm_gains[layer, 0][None, :], d_mixed, back_ties
         )
         grad_parts = gather_wa(grad_b)
-        if layer:
-            joint = scatter_rows(
-                weight_grads(
-                    here, [(nat, dbc), (nat, dkv), (nat, dx), (nat, ddt)], seq_count, False,
-                    [grad_parts[1]],
-                )
-            )
-            ends = 2 * NS + 128
-            sum_every, sum_in = joint[:, :ends], joint[:, ends:]
-            x_parts = gather_wa(held_back([h.astype(BF)], [grad_parts[-1]])[0])
         sums[layer] = (sum_ff, sum_mix, sum_in, sum_every)
         small[layer] = (gain_one, gain_two, gconv, ghead)
+    x_parts = gather_wa(held_back([h.astype(BF)], [grad_parts[-1]])[0])
+    shared_late = gather_wa(held_back([sums[1][3]], [x_parts[-1]])[0])
     x_out = all_rows(me, x_parts)
     d_x = all_rows(me, grad_parts)
 
@@ -1166,7 +1204,7 @@
         [small[layer][2] for layer in range(LAYER_COUNT)],
         [small[layer][3] for layer in range(LAYER_COUNT)],
         inner,
-        [grad_parts[1]],
+        [grad_parts[-1]],
     )
     local = jnp.sum(gather_seq(local), axis=0)
     gain_rows = 2 * LAYER_COUNT * width // 128
@@ -1179,8 +1217,9 @@
     g_conv_x = local[:conv_rows].reshape(LAYER_COUNT, KC + 1, inner)
     head_part = local[conv_rows:].reshape(LAYER_COUNT, 8, 128)
 
-    every = jnp.stack([s[3] for s in sums]).astype(BF)
-    every_parts = gather_wa(every)
+    every_parts = [
+        jnp.stack(pair) for pair in zip(gather_wa(sums[0][3]), shared_late)
+    ]
     g_bc = sum(part[:, :, : 2 * NS].astype(F32) for part in every_parts)
     kv_columns = []
     for head in range(KEY_VALUE_HEADS):
@@ -1194,7 +1233,7 @@
     block = sums[0][0].shape[0]
 
     def stacked(pick):
-        return jnp.stack([pick(s) for s in sums])
+        return jnp.stack([pick(s).astype(F32) for s in sums])
 
     g_down = stacked(lambda s: s[0][:, :hidden].T)
     g_gu = stacked(lambda s: s[0][:, hidden:].reshape(block, 2, hidden))
@@ -1202,10 +1241,12 @@
     g_out = stacked(lambda s: s[1][:, :inner].T)
     g_ao = stacked(lambda s: s[1][:, inner:ends].T)
     g_zx = stacked(
-        lambda s: jnp.stack([s[1][:, ends : ends + inner], s[2][:, :inner]], axis=1)
-    )
-    g_q = stacked(lambda s: s[1][:, ends + inner :])
-    g_dt = stacked(lambda s: s[2][:, inner : inner + heads])
+        lambda s: jnp.stack(
+            [s[1][:, ends : ends + inner].astype(F32), s[2][:, :inner].astype(F32)], axis=1
+        )
+    )
+    g_q = stacked(lambda s: s[2][:, inner:ends])
+    g_dt = stacked(lambda s: s[2][:, ends : ends + heads])
     return (
         x_out,
         d_x,

time: 598 us -> 540 us (0.903)
  waiting for transfers between devices: 122 us -> 103 us
  local copies, waits for them, and re-layouts: 106 us -> 90.2 us
  starting transfers between devices: 125 us -> 114 us
  other arithmetic: 21.2 us -> 12.2 us
    ppermute x14 -> x0, starting transfers between devices: 19.1 us -> none  [scatter_rows(): lax.ppermute(blocks[d], 'seq', [(i, (i + d) % n) for i in range(n)])]
    unnamed x503 -> x449, local copies, waits for them, and re-layouts: 71.8 us -> 53.6 us
    reduce_scatter x5 -> x3, waiting for transfers between devices: 12.9 us -> 0.01 us  [scatter_rows(): return lax.psum_scatter(blocks[0], 'seq', scatter_dimension=0, tiled=True)]
    ppermute x33 -> x36, starting transfers between devices: 54.8 us -> 66.4 us  [gather_wa(): lax.ppermute(block, 'wa', [(i, (i + d) % n) for i in range(n)])]
    ppermute x33 -> x36, waiting for transfers between devices: 58.1 us -> 49.5 us  [gather_wa(): lax.ppermute(block, 'wa', [(i, (i + d) % n) for i in range(n)])]
    pallas_call x41 -> x37, Pallas kernels: 82.5 us -> 84.4 us  [kernel_call(): pl.pallas_call(whole, grid=(1,), in_specs=in_specs, out_specs=[pl.BlockSp...]
  transfers between devices with their start and end apart: 80 -> 67, of which waited for: 31 -> 26; matrix products, arithmetic and copies ran while one was open for 10% -> 10% of each run, Pallas kernels for 6% -> 9%
where the time goes in v3:
time: 540 us; the launch traced here: 530 us
  starting transfers between devices  114 us (21%)
  blocking collectives  108 us (20%)
  waiting for transfers between devices  103 us (19%)
  local copies, waits for them, and re-layouts  90.2 us (17%)
  Pallas kernels  84.4 us (16%)
  between operations  18.4 us (3%)
  other arithmetic  12.2 us (2%)
    all_gather x9, blocking collectives, gather_seq(): return lax.all_gather(block, 'seq')  108 us
    pallas_call x37, Pallas kernels, kernel_call(): pl.pallas_call(whole, grid=(1,), in_specs=in_specs, out_specs=[pl.BlockSp...  84.4 us
    ppermute x36, starting transfers between devices, gather_wa(): lax.ppermute(block, 'wa', [(i, (i + d) % n) for i in range(n)])  66.4 us
    ppermute x24, waiting for transfers between devices, scatter_wa(): lax.ppermute(blocks[n - d], 'wa', [(i, (i + d) % n) for i in range(n)])  53.8 us
    unnamed x449, local copies, waits for them, and re-layouts  53.6 us
    ppermute x36, waiting for transfers between devices, gather_wa(): lax.ppermute(block, 'wa', [(i, (i + d) % n) for i in range(n)])  49.5 us
    ppermute x24, starting transfers between devices, scatter_wa(): lax.ppermute(blocks[n - d], 'wa', [(i, (i + d) % n) for i in range(n)])  41.7 us
  transfers between devices with their start and end apart: 67, of which 26 were waited for; matrix products, arithmetic and copies ran while one was open for 10% of the time, Pallas kernels for 9%

profile of v3, /device:TPU:0, one launch (start us, length us, event | category | flops | bytes accessed | tf_op | source)
XLA Modules:
  0.0 530.4 jit_solution(6095705164542996751)
XLA Ops:
  31.5 8.2 %reshape.267.refs_9_.refs_3_.refs_8_ = bf16[2,1024,768]{2,1,0:T(8,128)(2,1)} reshape(bf16[2,1024,2,384]{3,2,1,0:T(2,128)(2,1)} %param.22) | data formatting | bytes 6291456 | tf_op jit(solution)/shard_map/reshape | solution.py:1061
  46.2 10.9 %all-gather.1 = bf16[2048,128]{1,0:T(8,128)(2,1)S(1)} all-gather(bf16[256,128]{1,0:T(8,128)(2,1)S(1)} %get-tuple-element.150), channel_id=3, replica_groups=mesh['seq'=8,'wa'=4] {'seq'}, dimensions={0}, use_global_device_ids=true | all-gather | bytes 589824 | tf_op jit(solution)/shard_map/all_gather | solution.py:61
  62.3 14.1 %all-gather = bf16[3200,128]{1,0:T(8,128)(2,1)S(1)} all-gather(bf16[400,128]{1,0:T(8,128)(2,1)S(1)} %get-tuple-element.146), channel_id=2, replica_groups=mesh['seq'=8,'wa'=4] {'seq'}, dimensions={0}, use_global_device_ids=true | all-gather | bytes 921600 | tf_op jit(solution)/shard_map/all_gather | solution.py:61
  83.2 4.4 collective-permute-done.4.refs_1_
  87.6 5.2 collective-permute-done.5.refs_2_
  99.6 7.7 %reshape.269.refs_4_.refs_5_ = bf16[2,1024,1024]{2,1,0:T(8,128)(2,1)} reshape(bf16[2,1024,2,512]{3,2,1,0:T(2,128)(2,1)} %param.34) | data formatting | bytes 8388608 | tf_op jit(solution)/shard_map/reshape | solution.py:1062
  119.7 4.5 collective-permute-done.11.refs_2_
  142.9 10.7 %all-gather.3 = bf16[2048,128]{1,0:T(8,128)(2,1)S(1)} all-gather(bf16[256,128]{1,0:T(8,128)(2,1)S(1)} %get-tuple-element.170), channel_id=5, replica_groups=mesh['seq'=8,'wa'=4] {'seq'}, dimensions={0}, use_global_device_ids=true | all-gather | bytes 589824 | tf_op jit(solution)/shard_map/all_gather | solution.py:61
  159.4 14.4 %all-gather.2 = bf16[3200,128]{1,0:T(8,128)(2,1)S(1)} all-gather(bf16[400,128]{1,0:T(8,128)(2,1)S(1)} %get-tuple-element.166), channel_id=4, replica_groups=mesh['seq'=8,'wa'=4] {'seq'}, dimensions={0}, use_global_device_ids=true | all-gather | bytes 921600 | tf_op jit(solution)/shard_map/all_gather | solution.py:61
  186.0 5.4 %collective-permute-done.18.refs_2_ = bf16[64,1024]{1,0:T(8,128)(2,1)S(1)} collective-permute-done((bf16[64,1024]{1,0:T(8,128)(2,1)S(1)}, bf16[64,1024]{1,0:T(8,128)(2,1)S(1)}, u32[]{:S(2)}, u32[]{:S(2)}) %collective-permute-start.18) | collective-permute-done | bytes 131104 | tf_op jit(solution)/shard_map/ppermute | solution.py:88
  201.9 4.9 collective-permute-done.21.refs_2_
  212.4 4.9 feed_back.2
  226.0 4.5 collective-permute-done.24.refs_2_
  256.1 11.2 %all-gather.4 = bf16[3968,128]{1,0:T(8,128)(2,1)S(1)} all-gather(bf16[496,128]{1,0:T(8,128)(2,1)} %copy-done.159), channel_id=6, replica_groups=mesh['seq'=8,'wa'=4] {'seq'}, dimensions={0}, use_global_device_ids=true | all-gather | bytes 1142784 | tf_op jit(solution)/shard_map/all_gather | solution.py:61
  272.9 6.5 %mixer_grad.2 = (bf16[256,640]{1,0:T(8,128)(2,1)S(1)}, f32[16,640]{1,0:T(8,128)S(1)}, f32[8,640]{1,0:T(8,128)S(1)}, bf16[256,128]{1,0:T(8,128)(2,1)S(1)}, f32[8,640]{1,0:T(8,128)S(1)}, /*index=5*/f32[8,128]{1,0:T(8,128)S(1)}) custom-call(s32[1]{0:T(128)} %bitcast.1.refs_0_.refs_1_, bf16[8,496,128]{2,1,0:T(8,128)(2,1)S(1)} %bitcast.105, ...), custom_call_target="tpu_custom_call" | custom-call | flops 402653184 | bytes 3142660 | tf_op jit(solution)/shard_map/mixer_grad/pallas_call | solution.py:120
  280.8 11.9 %all-gather.5 = bf16[3456,128]{1,0:T(8,128)(2,1)S(1)} all-gather(bf16[432,128]{1,0:T(8,128)(2,1)S(1)} %copy-done.162), channel_id=7, replica_groups=mesh['seq'=8,'wa'=4] {'seq'}, dimensions={0}, use_global_device_ids=true | all-gather | bytes 995328 | tf_op jit(solution)/shard_map/all_gather | solution.py:61
  292.9 5.6 %attend_back.2 = (bf16[256,128]{1,0:T(8,128)(2,1)S(1)}, bf16[256,128]{1,0:T(8,128)(2,1)S(1)}) custom-call(s32[1]{0:T(128)} %bitcast.1.refs_0_.refs_1_, bf16[8,256,128]{2,1,0:T(8,128)(2,1)S(1)} %bitcast.117, bf16[8,496,128]{2,1,0:T(8,128)(2,1)S(1)} %bitcast.106, bf16[8,432,128]{2,1,0:T(8,128)(2,1)S(1)} %bitcast.113, f32[512,128]{1,0:T(8,128)S(1)} %copy-done.131, ...), custom_call_target="tpu_custom_call" | custom-call | flops 1879048192 | bytes 3687436 | tf_op jit(solution)/shard_map/attend_back/pallas_call | solution.py:120
  304.3 5.4 %weight_grads.3.refs_7_ = bf16[1024,3456]{1,0:T(8,128)(2,1)} custom-call(s32[1]{0:T(128)} %bitcast.1.refs_0_.refs_1_, bf16[256,1024]{1,0:T(8,128)(2,1)S(1)} %copy-done.103, bf16[256,512]{1,0:T(8,128)(2,1)S(1)} %copy-done.129, bf16[256,1024]{1,0:T(8,128)(2,1)S(1)} %copy-done.101, bf16[256,1024]{1,0:T(8,128)(2,1)S(1)} %copy-done.105, ...), custom_call_target="tpu_custom_call" | custom-call | flops 1811939328 | bytes 14090244 | tf_op jit(solution)/shard_map/weight_grads/pallas_call | solution.py:120
  313.8 4.6 collective-permute-done.33.refs_6_.refs_1_
  318.4 5.0 collective-permute-done.34.refs_2_
  332.1 4.8 collective-permute-done.37.refs_2_
  336.9 4.8 feed_back.3
  351.2 4.4 collective-permute-done.40.refs_2_
  364.4 4.5 collective-permute-done.43.refs_3_
  373.3 10.8 %all-gather.7 = bf16[3456,128]{1,0:T(8,128)(2,1)} all-gather(bf16[432,128]{1,0:T(8,128)(2,1)S(1)} %get-tuple-element.247), channel_id=9, replica_groups=mesh['seq'=8,'wa'=4] {'seq'}, dimensions={0}, use_global_device_ids=true | all-gather | bytes 995328 | tf_op jit(solution)/shard_map/all_gather | solution.py:61
  384.2 11.4 %all-gather.6 = bf16[3968,128]{1,0:T(8,128)(2,1)S(1)} all-gather(bf16[496,128]{1,0:T(8,128)(2,1)} %copy-done.160), channel_id=8, replica_groups=mesh['seq'=8,'wa'=4] {'seq'}, dimensions={0}, use_global_device_ids=true | all-gather | bytes 1142784 | tf_op jit(solution)/shard_map/all_gather | solution.py:61
  396.5 6.6 %mixer_grad.3 = (bf16[256,640]{1,0:T(8,128)(2,1)S(1)}, f32[16,640]{1,0:T(8,128)S(1)}, f32[8,640]{1,0:T(8,128)S(1)}, bf16[256,128]{1,0:T(8,128)(2,1)S(1)}, f32[8,640]{1,0:T(8,128)S(1)}, /*index=5*/f32[8,128]{1,0:T(8,128)S(1)}) custom-call(s32[1]{0:T(128)} %bitcast.1.refs_0_.refs_1_, bf16[8,496,128]{2,1,0:T(8,128)(2,1)S(1)} %bitcast.107, ...), custom_call_target="tpu_custom_call" | custom-call | flops 402653184 | bytes 3142660 | tf_op jit(solution)/shard_map/mixer_grad/pallas_call | solution.py:120
  415.6 5.6 %attend_back.3 = (bf16[256,128]{1,0:T(8,128)(2,1)S(1)}, bf16[256,128]{1,0:T(8,128)(2,1)S(1)}) custom-call(s32[1]{0:T(128)} %bitcast.1.refs_0_.refs_1_, bf16[8,256,128]{2,1,0:T(8,128)(2,1)S(1)} %bitcast.115, bf16[8,496,128]{2,1,0:T(8,128)(2,1)S(1)} %bitcast.108, bf16[8,432,128]{2,1,0:T(8,128)(2,1)S(1)} %bitcast.110, f32[512,128]{1,0:T(8,128)S(1)} %copy-done.195, ...), custom_call_target="tpu_custom_call" | custom-call | flops 1879048192 | bytes 3687436 | tf_op jit(solution)/shard_map/attend_back/pallas_call | solution.py:120
  440.5 5.5 %collective-permute-done.47.refs_2_ = bf16[64,1024]{1,0:T(8,128)(2,1)S(1)} collective-permute-done((bf16[64,1024]{1,0:T(8,128)(2,1)S(1)}, bf16[64,1024]{1,0:T(8,128)(2,1)S(1)}, u32[]{:S(2)}, u32[]{:S(2)}) %collective-permute-start.47) | collective-permute-done | bytes 131104 | tf_op jit(solution)/shard_map/ppermute | solution.py:88
  456.8 12.4 %all-gather.9 = f32[8,98,128]{2,1,0:T(8,128)S(1)} all-gather(f32[1,98,128]{2,1,0:T(8,128)S(1)} %bitcast.118), channel_id=10, replica_groups=mesh['seq'=8,'wa'=4] {'seq'}, dimensions={0}, use_global_device_ids=true | all-gather | bytes 451584 | tf_op jit(solution)/shard_map/all_gather | solution.py:61
  486.5 5.8 %collective-permute-done.52.refs_4_.refs_1_ = bf16[64,1024]{1,0:T(8,128)(2,1)S(1)} collective-permute-done((bf16[64,1024]{1,0:T(8,128)(2,1)}, bf16[64,1024]{1,0:T(8,128)(2,1)S(1)}, u32[]{:S(2)}, u32[]{:S(2)}) %collective-permute-start.52) | collective-permute-done | bytes 131104 | tf_op jit(solution)/shard_map/ppermute | solution.py:81
  516.3 5.1 collective-permute-done.58
  (692 shorter events, 280.1 us)
Async XLA Ops:
  7.2 376.8 %reduce-scatter.4.cloned.1.call-start = ((), (), s32[]{:S(2)}) async-start(), calls=%async_computation.3 | async-start | bytes 7962624 | tf_op jit(solution)/shard_map/reduce_scatter | solution.py:75
  9.8 31.3 %collective-permute-start.2 = (bf16[64,1024]{1,0:T(8,128)(2,1)S(1)}, bf16[64,1024]{1,0:T(8,128)(2,1)S(1)}, u32[]{:S(2)}, u32[]{:S(2)}) collective-permute-start(bf16[64,1024]{1,0:T(8,128)(2,1)S(1)} %norm_first.1.refs_1_), channel_id=1, source_target_pairs={{0,1},{1,2},{2,3},{3,0},{4,5},{5,6},{6,7},{7,4},{8,9},{9,10},{10,1... | collective-permute-start | bytes 393224 | tf_op jit(solution)/shard_map/ppermute | solution.py:81
  12.9 28.2 %collective-permute-start.1 = (bf16[64,1024]{1,0:T(8,128)(2,1)S(1)}, bf16[64,1024]{1,0:T(8,128)(2,1)}, u32[]{:S(2)}, u32[]{:S(2)}) collective-permute-start(bf16[64,1024]{1,0:T(8,128)(2,1)S(1)} %norm_first.1.refs_1_), channel_id=1, source_target_pairs={{0,2},{1,3},{2,0},{3,1},{4,6},{5,7},{6,4},{7,5},{8,10},{9,11},{10,... | collective-permute-start | bytes 393224 | tf_op jit(solution)/shard_map/ppermute | solution.py:81
  15.5 25.7 %collective-permute-start = (bf16[64,1024]{1,0:T(8,128)(2,1)S(1)}, bf16[64,1024]{1,0:T(8,128)(2,1)}, u32[]{:S(2)}, u32[]{:S(2)}) collective-permute-start(bf16[64,1024]{1,0:T(8,128)(2,1)S(1)} %norm_first.1.refs_1_), channel_id=1, source_target_pairs={{0,3},{1,0},{2,1},{3,2},{4,7},{5,4},{6,5},{7,6},{8,11},{9,8},{10,9... | collective-permute-start | bytes 393224 | tf_op jit(solution)/shard_map/ppermute | solution.py:81
  42.0 16.7 %collective-permute-start.3 = (bf16[16,1024]{1,0:T(8,128)(2,1)S(1)}, bf16[16,1024]{1,0:T(8,128)(2,1)S(1)}, u32[]{:S(2)}, u32[]{:S(2)}) collective-permute-start(bf16[16,1024]{1,0:T(8,128)(2,1)S(1)} %fusion.15), channel_id=1, source_target_pairs={{0,4},{4,8},{8,12},{12,16},{16,20},{20,24},{24,28},{1,5},{5,9},{9,... | collective-permute-start | bytes 98312 | tf_op jit(solution)/shard_map/ppermute | solution.py:1088
  80.1 12.7 %collective-permute-start.5 = (bf16[64,1024]{1,0:T(8,128)(2,1)S(1)}, bf16[64,1024]{1,0:T(8,128)(2,1)S(1)}, u32[]{:S(2)}, u32[]{:S(2)}) collective-permute-start(bf16[64,1024]{1,0:T(8,128)(2,1)S(1)} %get-tuple-element.155), channel_id=1, source_target_pairs={{0,2},{1,3},{2,0},{3,1},{4,6},{5,7},{6,4},{7,5},{8,10},{9,11},{10,... | collective-permute-start | bytes 393224 | tf_op jit(solution)/shard_map/ppermute | solution.py:88
  80.4 12.4 %collective-permute-start.6 = (bf16[64,1024]{1,0:T(8,128)(2,1)S(1)}, bf16[64,1024]{1,0:T(8,128)(2,1)S(1)}, u32[]{:S(2)}, u32[]{:S(2)}) collective-permute-start(bf16[64,1024]{1,0:T(8,128)(2,1)S(1)} %get-tuple-element.156), channel_id=1, source_target_pairs={{0,3},{1,0},{2,1},{3,2},{4,7},{5,4},{6,5},{7,6},{8,11},{9,8},{10,9... | collective-permute-start | bytes 393224 | tf_op jit(solution)/shard_map/ppermute | solution.py:88
  94.3 13.0 %collective-permute-start.7 = (bf16[64,1024]{1,0:T(8,128)(2,1)}, bf16[64,1024]{1,0:T(8,128)(2,1)}, u32[]{:S(2)}, u32[]{:S(2)}) collective-permute-start(bf16[64,1024]{1,0:T(8,128)(2,1)} %get-tuple-element.157.refs_0_), channel_id=1, source_target_pairs={{0,1},{1,2},{2,3},{3,0},{4,5},{5,6},{6,7},{7,4},{8,9},{9,10},{10,1... | collective-permute-start | bytes 393224 | tf_op jit(solution)/shard_map/ppermute | solution.py:81
  138.1 17.7 %collective-permute-start.16 = (bf16[16,1024]{1,0:T(8,128)(2,1)S(1)}, bf16[16,1024]{1,0:T(8,128)(2,1)S(1)}, u32[]{:S(2)}, u32[]{:S(2)}) collective-permute-start(bf16[16,1024]{1,0:T(8,128)(2,1)S(1)} %fusion.12), channel_id=1, source_target_pairs={{0,4},{4,8},{8,12},{12,16},{16,20},{20,24},{24,28},{1,5},{5,9},{9,... | collective-permute-start | bytes 98312 | tf_op jit(solution)/shard_map/ppermute | solution.py:1088
  180.7 10.7 %collective-permute-start.18 = (bf16[64,1024]{1,0:T(8,128)(2,1)S(1)}, bf16[64,1024]{1,0:T(8,128)(2,1)S(1)}, u32[]{:S(2)}, u32[]{:S(2)}) collective-permute-start(bf16[64,1024]{1,0:T(8,128)(2,1)S(1)} %get-tuple-element.175), channel_id=1, source_target_pairs={{0,2},{1,3},{2,0},{3,1},{4,6},{5,7},{6,4},{7,5},{8,10},{9,11},{10,... | collective-permute-start | bytes 393224 | tf_op jit(solution)/shard_map/ppermute | solution.py:88
  196.3 10.6 %collective-permute-start.21 = (bf16[64,1024]{1,0:T(8,128)(2,1)}, bf16[64,1024]{1,0:T(8,128)(2,1)}, u32[]{:S(2)}, u32[]{:S(2)}) collective-permute-start(bf16[64,1024]{1,0:T(8,128)(2,1)} %get-tuple-element.178.refs_0_), channel_id=1, source_target_pairs={{0,2},{1,3},{2,0},{3,1},{4,6},{5,7},{6,4},{7,5},{8,10},{9,11},{10,... | collective-permute-start | bytes 393224 | tf_op jit(solution)/shard_map/ppermute | solution.py:81
  250.3 42.4 %collective-permute-start.29 = (bf16[64,1024]{1,0:T(8,128)(2,1)}, bf16[64,1024]{1,0:T(8,128)(2,1)S(1)}, u32[]{:S(2)}, u32[]{:S(2)}) collective-permute-start(bf16[64,1024]{1,0:T(8,128)(2,1)} %get-tuple-element.194), channel_id=1, source_target_pairs={{0,1},{1,2},{2,3},{3,0},{4,5},{5,6},{6,7},{7,4},{8,9},{9,10},{10,1... | collective-permute-start | bytes 393224 | tf_op jit(solution)/shard_map/ppermute | solution.py:88
  253.6 39.1 %collective-permute-start.30 = (bf16[64,1024]{1,0:T(8,128)(2,1)}, bf16[64,1024]{1,0:T(8,128)(2,1)S(1)}, u32[]{:S(2)}, u32[]{:S(2)}) collective-permute-start(bf16[64,1024]{1,0:T(8,128)(2,1)} %get-tuple-element.195), channel_id=1, source_target_pairs={{0,2},{1,3},{2,0},{3,1},{4,6},{5,7},{6,4},{7,5},{8,10},{9,11},{10,... | collective-permute-start | bytes 393224 | tf_op jit(solution)/shard_map/ppermute | solution.py:88
  255.2 37.5 %collective-permute-start.31 = (bf16[64,1024]{1,0:T(8,128)(2,1)}, bf16[64,1024]{1,0:T(8,128)(2,1)S(1)}, u32[]{:S(2)}, u32[]{:S(2)}) collective-permute-start(bf16[64,1024]{1,0:T(8,128)(2,1)} %get-tuple-element.196), channel_id=1, source_target_pairs={{0,3},{1,0},{2,1},{3,2},{4,7},{5,4},{6,5},{7,6},{8,11},{9,8},{10,9... | collective-permute-start | bytes 393224 | tf_op jit(solution)/shard_map/ppermute | solution.py:88
  279.4 19.1 %collective-permute-start.32 = (f32[8,640]{1,0:T(8,128)S(1)}, f32[8,640]{1,0:T(8,128)S(1)}, u32[]{:S(2)}, u32[]{:S(2)}) collective-permute-start(f32[8,640]{1,0:T(8,128)S(1)} %get-tuple-element.204), channel_id=1, source_target_pairs={{4,0},{8,4},{12,8},{16,12},{20,16},{24,20},{28,24},{5,1},{9,5},{13... | collective-permute-start | bytes 61448 | tf_op jit(solution)/shard_map/ppermute | solution.py:1158
  309.8 189.8 %reduce-scatter.8.cloned.1.call-start = ((), (), s32[]{:S(2)}) async-start(), calls=%async_computation.5 | async-start | bytes 3538944 | tf_op jit(solution)/shard_map/reduce_scatter | solution.py:75
  311.1 12.3 %collective-permute-start.34 = (bf16[64,1024]{1,0:T(8,128)(2,1)}, bf16[64,1024]{1,0:T(8,128)(2,1)S(1)}, u32[]{:S(2)}, u32[]{:S(2)}) collective-permute-start(bf16[64,1024]{1,0:T(8,128)(2,1)} %copy-done.200), channel_id=1, source_target_pairs={{0,2},{1,3},{2,0},{3,1},{4,6},{5,7},{6,4},{7,5},{8,10},{9,11},{10,... | collective-permute-start | bytes 393224 | tf_op jit(solution)/shard_map/ppermute | solution.py:88
  312.5 11.0 %collective-permute-start.35 = (bf16[64,1024]{1,0:T(8,128)(2,1)S(1)}, bf16[64,1024]{1,0:T(8,128)(2,1)S(1)}, u32[]{:S(2)}, u32[]{:S(2)}) collective-permute-start(bf16[64,1024]{1,0:T(8,128)(2,1)S(1)} %copy-done.199), channel_id=1, source_target_pairs={{0,3},{1,0},{2,1},{3,2},{4,7},{5,4},{6,5},{7,6},{8,11},{9,8},{10,9... | collective-permute-start | bytes 393224 | tf_op jit(solution)/shard_map/ppermute | solution.py:88
  345.1 10.5 %collective-permute-start.40 = (bf16[64,1024]{1,0:T(8,128)(2,1)S(1)}, bf16[64,1024]{1,0:T(8,128)(2,1)S(1)}, u32[]{:S(2)}, u32[]{:S(2)}) collective-permute-start(bf16[64,1024]{1,0:T(8,128)(2,1)S(1)} %get-tuple-element.228), channel_id=1, source_target_pairs={{0,2},{1,3},{2,0},{3,1},{4,6},{5,7},{6,4},{7,5},{8,10},{9,11},{10,... | collective-permute-start | bytes 393224 | tf_op jit(solution)/shard_map/ppermute | solution.py:88
  384.1 120.2 %reduce-scatter.6.cloned.1.call-start = ((), (), s32[]{:S(2)}) async-start(), calls=%async_computation.4 | async-start | bytes 4423680 | tf_op jit(solution)/shard_map/reduce_scatter | solution.py:75
  404.3 16.9 %collective-permute-start.45 = (f32[8,640]{1,0:T(8,128)S(1)}, f32[8,640]{1,0:T(8,128)S(1)}, u32[]{:S(2)}, u32[]{:S(2)}) collective-permute-start(f32[8,640]{1,0:T(8,128)S(1)} %get-tuple-element.245), channel_id=1, source_target_pairs={{4,0},{8,4},{12,8},{16,12},{20,16},{24,20},{28,24},{5,1},{9,5},{13... | collective-permute-start | bytes 61448 | tf_op jit(solution)/shard_map/ppermute | solution.py:1158
  434.7 11.3 %collective-permute-start.47 = (bf16[64,1024]{1,0:T(8,128)(2,1)S(1)}, bf16[64,1024]{1,0:T(8,128)(2,1)S(1)}, u32[]{:S(2)}, u32[]{:S(2)}) collective-permute-start(bf16[64,1024]{1,0:T(8,128)(2,1)S(1)} %get-tuple-element.253), channel_id=1, source_target_pairs={{0,2},{1,3},{2,0},{3,1},{4,6},{5,7},{6,4},{7,5},{8,10},{9,11},{10,... | collective-permute-start | bytes 393224 | tf_op jit(solution)/shard_map/ppermute | solution.py:88
  453.2 25.5 %collective-permute-start.53 = (bf16[64,1024]{1,0:T(8,128)(2,1)S(1)}, bf16[64,1024]{1,0:T(8,128)(2,1)S(1)}, u32[]{:S(2)}, u32[]{:S(2)}) collective-permute-start(bf16[64,1024]{1,0:T(8,128)(2,1)S(1)} %get-tuple-element.261.refs_1_), channel_id=1, source_target_pairs={{0,1},{1,2},{2,3},{3,0},{4,5},{5,6},{6,7},{7,4},{8,9},{9,10},{10,1... | collective-permute-start | bytes 393224 | tf_op jit(solution)/shard_map/ppermute | solution.py:81
  453.2 25.5 %collective-permute-start.54 = (bf16[64,1024]{1,0:T(8,128)(2,1)S(1)}, bf16[64,1024]{1,0:T(8,128)(2,1)S(1)}, u32[]{:S(2)}, u32[]{:S(2)}) collective-permute-start(bf16[64,1024]{1,0:T(8,128)(2,1)S(1)} %get-tuple-element.261.refs_1_), channel_id=1, source_target_pairs={{0,2},{1,3},{2,0},{3,1},{4,6},{5,7},{6,4},{7,5},{8,10},{9,11},{10,... | collective-permute-start | bytes 393224 | tf_op jit(solution)/shard_map/ppermute | solution.py:81
  469.3 15.2 %collective-permute-start.57 = (f32[52,128]{1,0:T(8,128)S(1)}, f32[52,128]{1,0:T(8,128)S(1)}, u32[]{:S(2)}, u32[]{:S(2)}) collective-permute-start(f32[52,128]{1,0:T(8,128)S(1)} %slice.271), channel_id=1, source_target_pairs={{0,3},{1,0},{2,1},{3,2},{4,7},{5,4},{6,5},{7,6},{8,11},{9,8},{10,9... | collective-permute-start | bytes 79880 | tf_op jit(solution)/shard_map/ppermute | solution.py:81
  473.6 10.9 %collective-permute-start.56 = (f32[52,128]{1,0:T(8,128)S(1)}, f32[52,128]{1,0:T(8,128)S(1)}, u32[]{:S(2)}, u32[]{:S(2)}) collective-permute-start(f32[52,128]{1,0:T(8,128)S(1)} %slice.271), channel_id=1, source_target_pairs={{0,2},{1,3},{2,0},{3,1},{4,6},{5,7},{6,4},{7,5},{8,10},{9,11},{10,... | collective-permute-start | bytes 79880 | tf_op jit(solution)/shard_map/ppermute | solution.py:81
  478.7 18.0 %collective-permute-start.50 = (bf16[64,1024]{1,0:T(8,128)(2,1)}, bf16[64,1024]{1,0:T(8,128)(2,1)S(1)}, u32[]{:S(2)}, u32[]{:S(2)}) collective-permute-start(bf16[64,1024]{1,0:T(8,128)(2,1)} %held_back.6.refs_1_), channel_id=1, source_target_pairs={{0,1},{1,2},{2,3},{3,0},{4,5},{5,6},{6,7},{7,4},{8,9},{9,10},{10,1... | collective-permute-start | bytes 393224 | tf_op jit(solution)/shard_map/ppermute | solution.py:81
  478.7 18.0 %collective-permute-start.51 = (bf16[64,1024]{1,0:T(8,128)(2,1)}, bf16[64,1024]{1,0:T(8,128)(2,1)S(1)}, u32[]{:S(2)}, u32[]{:S(2)}) collective-permute-start(bf16[64,1024]{1,0:T(8,128)(2,1)} %held_back.6.refs_1_), channel_id=1, source_target_pairs={{0,2},{1,3},{2,0},{3,1},{4,6},{5,7},{6,4},{7,5},{8,10},{9,11},{10,... | collective-permute-start | bytes 393224 | tf_op jit(solution)/shard_map/ppermute | solution.py:81
  492.9 22.1 %collective-permute-start.63 = (bf16[128,384]{1,0:T(8,128)(2,1)}, bf16[128,384]{1,0:T(8,128)(2,1)S(1)}, u32[]{:S(2)}, u32[]{:S(2)}) collective-permute-start(bf16[128,384]{1,0:T(8,128)(2,1)} %held_back.7), channel_id=1, source_target_pairs={{0,3},{1,0},{2,1},{3,2},{4,7},{5,4},{6,5},{7,6},{8,11},{9,8},{10,9... | collective-permute-start | bytes 294920 | tf_op jit(solution)/shard_map/ppermute | solution.py:81
  493.0 23.3 %collective-permute-start.61 = (bf16[128,384]{1,0:T(8,128)(2,1)}, bf16[128,384]{1,0:T(8,128)(2,1)S(1)}, u32[]{:S(2)}, u32[]{:S(2)}) collective-permute-start(bf16[128,384]{1,0:T(8,128)(2,1)} %held_back.7), channel_id=1, source_target_pairs={{0,2},{1,3},{2,0},{3,1},{4,6},{5,7},{6,4},{7,5},{8,10},{9,11},{10,... | collective-permute-start | bytes 294920 | tf_op jit(solution)/shard_map/ppermute | solution.py:81
  496.7 19.5 %collective-permute-start.59 = (bf16[128,384]{1,0:T(8,128)(2,1)}, bf16[128,384]{1,0:T(8,128)(2,1)S(1)}, u32[]{:S(2)}, u32[]{:S(2)}) collective-permute-start(bf16[128,384]{1,0:T(8,128)(2,1)} %held_back.7), channel_id=1, source_target_pairs={{0,1},{1,2},{2,3},{3,0},{4,5},{5,6},{6,7},{7,4},{8,9},{9,10},{10,1... | collective-permute-start | bytes 294920 | tf_op jit(solution)/shard_map/ppermute | solution.py:81
  505.5 10.7 %collective-permute-start.62 = (bf16[128,384]{1,0:T(8,128)(2,1)S(1)}, bf16[128,384]{1,0:T(8,128)(2,1)S(1)}, u32[]{:S(2)}, u32[]{:S(2)}) collective-permute-start(bf16[128,384]{1,0:T(8,128)(2,1)S(1)} %get-tuple-element.340), channel_id=1, source_target_pairs={{0,3},{1,0},{2,1},{3,2},{4,7},{5,4},{6,5},{7,6},{8,11},{9,8},{10,9... | collective-permute-start | bytes 294920 | tf_op jit(solution)/shard_map/ppermute | solution.py:81
  (254 other events, 3310.1 us)
Sparse Core Ops, SparseCore 0:
  309.9 64.7 reduce-scatter.3
  384.2 47.8 reduce-scatter.7
  435.7 51.7 reduce-scatter.5

commit v4 on v3

--- a/solution.py
+++ b/solution.py
@@ -579,7 +579,7 @@
 def weight_grads(here, groups, n, ties=()):
     width = groups[0][0][0][0].shape[1]
     flat = [a for pairs, _ in groups for pair in pairs for a in pair]
-    plan, shapes = [], []
+    plan, shapes = [], [((8, 128), F32)]
     for pairs, direct in groups:
         blocks = n if direct and n <= DIRECT_MOST else 1
         columns = sum(right.shape[1] for _, right in pairs)
@@ -591,7 +591,8 @@
 
     def body(*refs):
         here_ref = refs[0]
-        source, out = 1, 1 + len(flat)
+        source, out = 1, 2 + len(flat)
+        refs[1 + len(flat)][...] = jnp.zeros((8, 128), F32)
         for count, blocks in plan:
             for d in range(blocks):
                 rows = width // blocks
@@ -618,11 +619,12 @@
         flops=2 * flat[0].shape[0] * width * sum(a.shape[1] for a in flat[1::2]),
         ties=ties,
     )
+    token, got = got[0], got[1:]
     out = []
     for _, blocks in plan:
         out.append(got[:blocks])
         got = got[blocks:]
-    return out
+    return out, token
 
 
 def mixer_grad_in(me, parts, wout, wao, gate, y, act, hd, tok, o2, q_own):
@@ -1129,8 +1131,8 @@
         ff_pairs = [(gb, act_ff), (n2, dgu)]
         grad_ties = []
         if not layer:
-            early = weight_grads(here, [(ff_pairs, False)], seq_count)[0]
-            grad_ties = list(early)
+            (early,), token = weight_grads(here, [(ff_pairs, False)], seq_count)
+            grad_ties = [token]
         d_mixed, mixed_b, gain_two = norm_back(
             parts, mixed, norm_gains[layer, 1][None, :], grad, grad_ties
         )
@@ -1165,10 +1167,10 @@
         every_pairs = [(nat, dbc), (nat, dkv)]
         in_pairs = [(nat, dx), (nat, dq), (nat, ddt)]
         if layer:
-            joint = weight_grads(
+            (joint,), token = weight_grads(
                 here, [(ff_pairs + mix_pairs + every_pairs + in_pairs, False)], seq_count
-            )[0]
-            back_ties = list(joint)
+            )
+            back_ties = [token]
             joint = scatter_rows(joint)
             cuts = [3 * hidden, 2 * inner + 128, 2 * NS + 128, inner + 256]
             ends = [sum(cuts[: k + 1]) for k in range(4)]
@@ -1177,10 +1179,10 @@
             ]
             h = norm_step(out_parts, last_mixed, norm_gains[layer, 0][None, :], [parts[1]])[0]
         else:
-            joint = weight_grads(
+            (joint,), token = weight_grads(
                 here, [(every_pairs + mix_pairs + in_pairs, False)], seq_count
-            )[0]
-            back_ties = list(joint)
+            )
+            back_ties = [token]
             joint = scatter_rows(joint)
             cuts = [2 * NS + 128, 2 * inner + 128, inner + 256]
             ends = [sum(cuts[: k + 1]) for k in range(3)]
@@ -1193,8 +1195,8 @@
         grad_parts = gather_wa(grad_b)
         sums[layer] = (sum_ff, sum_mix, sum_in, sum_every)
         small[layer] = (gain_one, gain_two, gconv, ghead)
-    x_parts = gather_wa(held_back([h.astype(BF)], [grad_parts[-1]])[0])
-    shared_late = gather_wa(held_back([sums[1][3]], [x_parts[-1]])[0])
+    x_parts = gather_wa(held_back([h.astype(BF)], grad_parts[1:])[0])
+    shared_late = gather_wa(held_back([sums[1][3]], x_parts[1:])[0])
     x_out = all_rows(me, x_parts)
     d_x = all_rows(me, grad_parts)
 
@@ -1204,7 +1206,7 @@
         [small[layer][2] for layer in range(LAYER_COUNT)],
         [small[layer][3] for layer in range(LAYER_COUNT)],
         inner,
-        [grad_parts[-1]],
+        grad_parts[1:],
     )
     local = jnp.sum(gather_seq(local), axis=0)
     gain_rows = 2 * LAYER_COUNT * width // 128

time: 540 us -> 548 us (1.015)
  local copies, waits for them, and re-layouts: 90.2 us -> 100 us
    unnamed x449 -> x481, local copies, waits for them, and re-layouts: 53.6 us -> 65.3 us
  transfers between devices with their start and end apart: 67 -> 67, of which waited for: 26 -> 28; matrix products, arithmetic and copies ran while one was open for 10% -> 10% of each run, Pallas kernels for 9% -> 9%
where the time goes in v4:
time: 548 us; the launch traced here: 538 us
  starting transfers between devices  114 us (21%)
  blocking collectives  105 us (19%)
  waiting for transfers between devices  104 us (19%)
  local copies, waits for them, and re-layouts  100 us (18%)
  Pallas kernels  83.4 us (15%)
  between operations  18.4 us (3%)
  other arithmetic  12.7 us (2%)
    all_gather x9, blocking collectives, gather_seq(): return lax.all_gather(block, 'seq')  105 us
    pallas_call x37, Pallas kernels, kernel_call(): pl.pallas_call(whole, grid=(1,), in_specs=in_specs, out_specs=[pl.BlockSp...  83.4 us
    ppermute x36, starting transfers between devices, gather_wa(): lax.ppermute(block, 'wa', [(i, (i + d) % n) for i in range(n)])  66.9 us
    unnamed x481, local copies, waits for them, and re-layouts  65.3 us
    ppermute x24, waiting for transfers between devices, scatter_wa(): lax.ppermute(blocks[n - d], 'wa', [(i, (i + d) % n) for i in range(n)])  53.7 us
    ppermute x36, waiting for transfers between devices, gather_wa(): lax.ppermute(block, 'wa', [(i, (i + d) % n) for i in range(n)])  50 us
    ppermute x24, starting transfers between devices, scatter_wa(): lax.ppermute(blocks[n - d], 'wa', [(i, (i + d) % n) for i in range(n)])  41.7 us
  transfers between devices with their start and end apart: 67, of which 28 were waited for; matrix products, arithmetic and copies ran while one was open for 10% of the time, Pallas kernels for 9%

profile of v4, /device:TPU:0, one launch (start us, length us, event | category | flops | bytes accessed | tf_op | source)
XLA Modules:
  0.0 538.0 jit_solution(1036490401921382270)
XLA Ops:
  32.0 8.2 %reshape.267.refs_9_.refs_3_.refs_8_ = bf16[2,1024,768]{2,1,0:T(8,128)(2,1)} reshape(bf16[2,1024,2,384]{3,2,1,0:T(2,128)(2,1)} %param.22) | data formatting | bytes 6291456 | tf_op jit(solution)/shard_map/reshape | solution.py:1063
  48.3 10.9 %all-gather.1 = bf16[2048,128]{1,0:T(8,128)(2,1)S(1)} all-gather(bf16[256,128]{1,0:T(8,128)(2,1)S(1)} %get-tuple-element.156), channel_id=3, replica_groups=mesh['seq'=8,'wa'=4] {'seq'}, dimensions={0}, use_global_device_ids=true | all-gather | bytes 589824 | tf_op jit(solution)/shard_map/all_gather | solution.py:61
  64.4 14.3 %all-gather = bf16[3200,128]{1,0:T(8,128)(2,1)S(1)} all-gather(bf16[400,128]{1,0:T(8,128)(2,1)S(1)} %get-tuple-element.152), channel_id=2, replica_groups=mesh['seq'=8,'wa'=4] {'seq'}, dimensions={0}, use_global_device_ids=true | all-gather | bytes 921600 | tf_op jit(solution)/shard_map/all_gather | solution.py:61
  84.9 4.4 collective-permute-done.4.refs_1_
  89.3 5.2 collective-permute-done.5.refs_2_
  101.2 7.7 %reshape.269.refs_4_.refs_5_ = bf16[2,1024,1024]{2,1,0:T(8,128)(2,1)} reshape(bf16[2,1024,2,512]{3,2,1,0:T(2,128)(2,1)} %param.34) | data formatting | bytes 8388608 | tf_op jit(solution)/shard_map/reshape | solution.py:1064
  121.4 4.5 collective-permute-done.11.refs_2_
  144.7 9.7 %all-gather.3 = bf16[2048,128]{1,0:T(8,128)(2,1)S(1)} all-gather(bf16[256,128]{1,0:T(8,128)(2,1)S(1)} %get-tuple-element.176), channel_id=5, replica_groups=mesh['seq'=8,'wa'=4] {'seq'}, dimensions={0}, use_global_device_ids=true | all-gather | bytes 589824 | tf_op jit(solution)/shard_map/all_gather | solution.py:61
  160.3 14.9 %all-gather.2 = bf16[3200,128]{1,0:T(8,128)(2,1)S(1)} all-gather(bf16[400,128]{1,0:T(8,128)(2,1)S(1)} %get-tuple-element.172), channel_id=4, replica_groups=mesh['seq'=8,'wa'=4] {'seq'}, dimensions={0}, use_global_device_ids=true | all-gather | bytes 921600 | tf_op jit(solution)/shard_map/all_gather | solution.py:61
  186.2 5.4 %collective-permute-done.18.refs_2_ = bf16[64,1024]{1,0:T(8,128)(2,1)S(1)} collective-permute-done((bf16[64,1024]{1,0:T(8,128)(2,1)S(1)}, bf16[64,1024]{1,0:T(8,128)(2,1)S(1)}, u32[]{:S(2)}, u32[]{:S(2)}) %collective-permute-start.18) | collective-permute-done | bytes 131104 | tf_op jit(solution)/shard_map/ppermute | solution.py:88
  202.2 4.9 collective-permute-done.21.refs_2_
  213.3 4.9 feed_back.2
  226.9 4.5 collective-permute-done.24.refs_2_
  240.8 4.4 collective-permute-done.27.refs_3_
  256.9 11.1 %all-gather.4 = bf16[3968,128]{1,0:T(8,128)(2,1)S(1)} all-gather(bf16[496,128]{1,0:T(8,128)(2,1)} %copy-done.168), channel_id=6, replica_groups=mesh['seq'=8,'wa'=4] {'seq'}, dimensions={0}, use_global_device_ids=true | all-gather | bytes 1142784 | tf_op jit(solution)/shard_map/all_gather | solution.py:61
  273.7 6.6 %mixer_grad.2 = (bf16[256,640]{1,0:T(8,128)(2,1)S(1)}, f32[16,640]{1,0:T(8,128)S(1)}, f32[8,640]{1,0:T(8,128)S(1)}, bf16[256,128]{1,0:T(8,128)(2,1)S(1)}, f32[8,640]{1,0:T(8,128)S(1)}, /*index=5*/f32[8,128]{1,0:T(8,128)S(1)}) custom-call(s32[1]{0:T(128)} %bitcast.1.refs_0_.refs_1_, bf16[8,496,128]{2,1,0:T(8,128)(2,1)S(1)} %bitcast.105, ...), custom_call_target="tpu_custom_call" | custom-call | flops 402653184 | bytes 3142660 | tf_op jit(solution)/shard_map/mixer_grad/pallas_call | solution.py:120
  282.2 11.9 %all-gather.5 = bf16[3456,128]{1,0:T(8,128)(2,1)S(1)} all-gather(bf16[432,128]{1,0:T(8,128)(2,1)S(1)} %copy-done.171), channel_id=7, replica_groups=mesh['seq'=8,'wa'=4] {'seq'}, dimensions={0}, use_global_device_ids=true | all-gather | bytes 995328 | tf_op jit(solution)/shard_map/all_gather | solution.py:61
  294.3 5.0 attend_back.2
  303.2 5.4 %weight_grads.3 = (f32[8,128]{1,0:T(8,128)S(1)}, bf16[1024,3456]{1,0:T(8,128)(2,1)}) custom-call(s32[1]{0:T(128)} %bitcast.1.refs_0_.refs_1_, bf16[256,1024]{1,0:T(8,128)(2,1)S(1)} %copy-done.118, bf16[256,512]{1,0:T(8,128)(2,1)S(1)} %copy-done.132, bf16[256,1024]{1,0:T(8,128)(2,1)S(1)} %copy-done.116, bf16[256,1024]{1,0:T(8,128)(2,1)S(1)} %copy-done.120, ...), custom_call_target="tpu_custom_call" | custom-call | flops 1811939328 | bytes 14094340 | tf_op jit(solution)/shard_map/weight_grads/pallas_call | solution.py:120
  313.3 4.6 collective-permute-done.33.refs_6_.refs_1_
  317.9 5.1 collective-permute-done.34.refs_2_
  335.8 4.8 collective-permute-done.37.refs_2_
  341.6 4.8 feed_back.3
  370.5 4.6 collective-permute-done.43.refs_3_
  379.6 10.7 %all-gather.7 = bf16[3456,128]{1,0:T(8,128)(2,1)} all-gather(bf16[432,128]{1,0:T(8,128)(2,1)S(1)} %get-tuple-element.255), channel_id=9, replica_groups=mesh['seq'=8,'wa'=4] {'seq'}, dimensions={0}, use_global_device_ids=true | all-gather | bytes 995328 | tf_op jit(solution)/shard_map/all_gather | solution.py:61
  390.4 11.4 %all-gather.6 = bf16[3968,128]{1,0:T(8,128)(2,1)S(1)} all-gather(bf16[496,128]{1,0:T(8,128)(2,1)} %copy-done.169), channel_id=8, replica_groups=mesh['seq'=8,'wa'=4] {'seq'}, dimensions={0}, use_global_device_ids=true | all-gather | bytes 1142784 | tf_op jit(solution)/shard_map/all_gather | solution.py:61
  402.9 6.7 %mixer_grad.3 = (bf16[256,640]{1,0:T(8,128)(2,1)S(1)}, f32[16,640]{1,0:T(8,128)S(1)}, f32[8,640]{1,0:T(8,128)S(1)}, bf16[256,128]{1,0:T(8,128)(2,1)S(1)}, f32[8,640]{1,0:T(8,128)S(1)}, /*index=5*/f32[8,128]{1,0:T(8,128)S(1)}) custom-call(s32[1]{0:T(128)} %bitcast.1.refs_0_.refs_1_, bf16[8,496,128]{2,1,0:T(8,128)(2,1)S(1)} %bitcast.107, ...), custom_call_target="tpu_custom_call" | custom-call | flops 402653184 | bytes 3142660 | tf_op jit(solution)/shard_map/mixer_grad/pallas_call | solution.py:120
  422.1 5.0 attend_back.3
  445.5 5.7 %collective-permute-done.47.refs_2_ = bf16[64,1024]{1,0:T(8,128)(2,1)S(1)} collective-permute-done((bf16[64,1024]{1,0:T(8,128)(2,1)S(1)}, bf16[64,1024]{1,0:T(8,128)(2,1)S(1)}, u32[]{:S(2)}, u32[]{:S(2)}) %collective-permute-start.47) | collective-permute-done | bytes 131104 | tf_op jit(solution)/shard_map/ppermute | solution.py:88
  460.4 4.8 collective-permute-done.50.refs_2_.refs_3_.refs_9_
  474.7 9.8 %all-gather.9 = f32[8,98,128]{2,1,0:T(8,128)S(1)} all-gather(f32[1,98,128]{2,1,0:T(8,128)S(1)} %bitcast.118), channel_id=10, replica_groups=mesh['seq'=8,'wa'=4] {'seq'}, dimensions={0}, use_global_device_ids=true | all-gather | bytes 451584 | tf_op jit(solution)/shard_map/all_gather | solution.py:61
  523.3 5.8 %collective-permute-done.58 = bf16[128,384]{1,0:T(8,128)(2,1)S(1)} collective-permute-done((bf16[128,384]{1,0:T(8,128)(2,1)S(1)}, bf16[128,384]{1,0:T(8,128)(2,1)S(1)}, u32[]{:S(2)}, u32[]{:S(2)}) %collective-permute-start.58) | collective-permute-done | bytes 98336 | tf_op jit(solution)/shard_map/ppermute | solution.py:81
  (724 shorter events, 291.8 us)
Async XLA Ops:
  7.2 383.1 %reduce-scatter.4.cloned.1.call-start = ((), (), s32[]{:S(2)}) async-start(), calls=%async_computation.3 | async-start | bytes 7962624 | tf_op jit(solution)/shard_map/reduce_scatter | solution.py:75
  9.8 31.8 %collective-permute-start.2 = (bf16[64,1024]{1,0:T(8,128)(2,1)S(1)}, bf16[64,1024]{1,0:T(8,128)(2,1)S(1)}, u32[]{:S(2)}, u32[]{:S(2)}) collective-permute-start(bf16[64,1024]{1,0:T(8,128)(2,1)S(1)} %norm_first.1.refs_1_), channel_id=1, source_target_pairs={{0,1},{1,2},{2,3},{3,0},{4,5},{5,6},{6,7},{7,4},{8,9},{9,10},{10,1... | collective-permute-start | bytes 393224 | tf_op jit(solution)/shard_map/ppermute | solution.py:81
  12.9 28.7 %collective-permute-start.1 = (bf16[64,1024]{1,0:T(8,128)(2,1)S(1)}, bf16[64,1024]{1,0:T(8,128)(2,1)}, u32[]{:S(2)}, u32[]{:S(2)}) collective-permute-start(bf16[64,1024]{1,0:T(8,128)(2,1)S(1)} %norm_first.1.refs_1_), channel_id=1, source_target_pairs={{0,2},{1,3},{2,0},{3,1},{4,6},{5,7},{6,4},{7,5},{8,10},{9,11},{10,... | collective-permute-start | bytes 393224 | tf_op jit(solution)/shard_map/ppermute | solution.py:81
  15.5 26.2 %collective-permute-start = (bf16[64,1024]{1,0:T(8,128)(2,1)S(1)}, bf16[64,1024]{1,0:T(8,128)(2,1)}, u32[]{:S(2)}, u32[]{:S(2)}) collective-permute-start(bf16[64,1024]{1,0:T(8,128)(2,1)S(1)} %norm_first.1.refs_1_), channel_id=1, source_target_pairs={{0,3},{1,0},{2,1},{3,2},{4,7},{5,4},{6,5},{7,6},{8,11},{9,8},{10,9... | collective-permute-start | bytes 393224 | tf_op jit(solution)/shard_map/ppermute | solution.py:81
  43.2 17.6 %collective-permute-start.3 = (bf16[16,1024]{1,0:T(8,128)(2,1)S(1)}, bf16[16,1024]{1,0:T(8,128)(2,1)S(1)}, u32[]{:S(2)}, u32[]{:S(2)}) collective-permute-start(bf16[16,1024]{1,0:T(8,128)(2,1)S(1)} %fusion.15), channel_id=1, source_target_pairs={{0,4},{4,8},{8,12},{12,16},{16,20},{20,24},{24,28},{1,5},{5,9},{9,... | collective-permute-start | bytes 98312 | tf_op jit(solution)/shard_map/ppermute | solution.py:1090
  81.7 12.7 %collective-permute-start.5 = (bf16[64,1024]{1,0:T(8,128)(2,1)S(1)}, bf16[64,1024]{1,0:T(8,128)(2,1)S(1)}, u32[]{:S(2)}, u32[]{:S(2)}) collective-permute-start(bf16[64,1024]{1,0:T(8,128)(2,1)S(1)} %get-tuple-element.161), channel_id=1, source_target_pairs={{0,2},{1,3},{2,0},{3,1},{4,6},{5,7},{6,4},{7,5},{8,10},{9,11},{10,... | collective-permute-start | bytes 393224 | tf_op jit(solution)/shard_map/ppermute | solution.py:88
  82.0 12.4 %collective-permute-start.6 = (bf16[64,1024]{1,0:T(8,128)(2,1)S(1)}, bf16[64,1024]{1,0:T(8,128)(2,1)S(1)}, u32[]{:S(2)}, u32[]{:S(2)}) collective-permute-start(bf16[64,1024]{1,0:T(8,128)(2,1)S(1)} %get-tuple-element.162), channel_id=1, source_target_pairs={{0,3},{1,0},{2,1},{3,2},{4,7},{5,4},{6,5},{7,6},{8,11},{9,8},{10,9... | collective-permute-start | bytes 393224 | tf_op jit(solution)/shard_map/ppermute | solution.py:88
  96.0 13.1 %collective-permute-start.7 = (bf16[64,1024]{1,0:T(8,128)(2,1)}, bf16[64,1024]{1,0:T(8,128)(2,1)}, u32[]{:S(2)}, u32[]{:S(2)}) collective-permute-start(bf16[64,1024]{1,0:T(8,128)(2,1)} %get-tuple-element.163.refs_0_), channel_id=1, source_target_pairs={{0,1},{1,2},{2,3},{3,0},{4,5},{5,6},{6,7},{7,4},{8,9},{9,10},{10,1... | collective-permute-start | bytes 393224 | tf_op jit(solution)/shard_map/ppermute | solution.py:81
  98.8 10.3 %collective-permute-start.8 = (bf16[64,1024]{1,0:T(8,128)(2,1)}, bf16[64,1024]{1,0:T(8,128)(2,1)}, u32[]{:S(2)}, u32[]{:S(2)}) collective-permute-start(bf16[64,1024]{1,0:T(8,128)(2,1)} %get-tuple-element.163.refs_0_), channel_id=1, source_target_pairs={{0,2},{1,3},{2,0},{3,1},{4,6},{5,7},{6,4},{7,5},{8,10},{9,11},{10,... | collective-permute-start | bytes 393224 | tf_op jit(solution)/shard_map/ppermute | solution.py:81
  129.5 10.3 %collective-permute-start.14 = (bf16[64,1024]{1,0:T(8,128)(2,1)S(1)}, bf16[64,1024]{1,0:T(8,128)(2,1)S(1)}, u32[]{:S(2)}, u32[]{:S(2)}) collective-permute-start(bf16[64,1024]{1,0:T(8,128)(2,1)S(1)} %get-tuple-element.169.refs_1_), channel_id=1, source_target_pairs={{0,2},{1,3},{2,0},{3,1},{4,6},{5,7},{6,4},{7,5},{8,10},{9,11},{10,... | collective-permute-start | bytes 393224 | tf_op jit(solution)/shard_map/ppermute | solution.py:81
  139.9 16.1 %collective-permute-start.16 = (bf16[16,1024]{1,0:T(8,128)(2,1)S(1)}, bf16[16,1024]{1,0:T(8,128)(2,1)S(1)}, u32[]{:S(2)}, u32[]{:S(2)}) collective-permute-start(bf16[16,1024]{1,0:T(8,128)(2,1)S(1)} %fusion.12), channel_id=1, source_target_pairs={{0,4},{4,8},{8,12},{12,16},{16,20},{20,24},{24,28},{1,5},{5,9},{9,... | collective-permute-start | bytes 98312 | tf_op jit(solution)/shard_map/ppermute | solution.py:1090
  180.9 10.7 %collective-permute-start.18 = (bf16[64,1024]{1,0:T(8,128)(2,1)S(1)}, bf16[64,1024]{1,0:T(8,128)(2,1)S(1)}, u32[]{:S(2)}, u32[]{:S(2)}) collective-permute-start(bf16[64,1024]{1,0:T(8,128)(2,1)S(1)} %get-tuple-element.181), channel_id=1, source_target_pairs={{0,2},{1,3},{2,0},{3,1},{4,6},{5,7},{6,4},{7,5},{8,10},{9,11},{10,... | collective-permute-start | bytes 393224 | tf_op jit(solution)/shard_map/ppermute | solution.py:88
  196.5 10.5 %collective-permute-start.21 = (bf16[64,1024]{1,0:T(8,128)(2,1)}, bf16[64,1024]{1,0:T(8,128)(2,1)}, u32[]{:S(2)}, u32[]{:S(2)}) collective-permute-start(bf16[64,1024]{1,0:T(8,128)(2,1)} %get-tuple-element.184.refs_0_), channel_id=1, source_target_pairs={{0,2},{1,3},{2,0},{3,1},{4,6},{5,7},{6,4},{7,5},{8,10},{9,11},{10,... | collective-permute-start | bytes 393224 | tf_op jit(solution)/shard_map/ppermute | solution.py:81
  235.0 10.2 %collective-permute-start.27 = (bf16[64,1024]{1,0:T(8,128)(2,1)S(1)}, bf16[64,1024]{1,0:T(8,128)(2,1)S(1)}, u32[]{:S(2)}, u32[]{:S(2)}) collective-permute-start(bf16[64,1024]{1,0:T(8,128)(2,1)S(1)} %get-tuple-element.195.refs_1_), channel_id=1, source_target_pairs={{0,2},{1,3},{2,0},{3,1},{4,6},{5,7},{6,4},{7,5},{8,10},{9,11},{10,... | collective-permute-start | bytes 393224 | tf_op jit(solution)/shard_map/ppermute | solution.py:81
  251.2 43.0 %collective-permute-start.29 = (bf16[64,1024]{1,0:T(8,128)(2,1)}, bf16[64,1024]{1,0:T(8,128)(2,1)S(1)}, u32[]{:S(2)}, u32[]{:S(2)}) collective-permute-start(bf16[64,1024]{1,0:T(8,128)(2,1)} %get-tuple-element.200), channel_id=1, source_target_pairs={{0,1},{1,2},{2,3},{3,0},{4,5},{5,6},{6,7},{7,4},{8,9},{9,10},{10,1... | collective-permute-start | bytes 393224 | tf_op jit(solution)/shard_map/ppermute | solution.py:88
  254.5 39.6 %collective-permute-start.30 = (bf16[64,1024]{1,0:T(8,128)(2,1)}, bf16[64,1024]{1,0:T(8,128)(2,1)S(1)}, u32[]{:S(2)}, u32[]{:S(2)}) collective-permute-start(bf16[64,1024]{1,0:T(8,128)(2,1)} %get-tuple-element.201), channel_id=1, source_target_pairs={{0,2},{1,3},{2,0},{3,1},{4,6},{5,7},{6,4},{7,5},{8,10},{9,11},{10,... | collective-permute-start | bytes 393224 | tf_op jit(solution)/shard_map/ppermute | solution.py:88
  256.0 38.1 %collective-permute-start.31 = (bf16[64,1024]{1,0:T(8,128)(2,1)}, bf16[64,1024]{1,0:T(8,128)(2,1)S(1)}, u32[]{:S(2)}, u32[]{:S(2)}) collective-permute-start(bf16[64,1024]{1,0:T(8,128)(2,1)} %get-tuple-element.202), channel_id=1, source_target_pairs={{0,3},{1,0},{2,1},{3,2},{4,7},{5,4},{6,5},{7,6},{8,11},{9,8},{10,9... | collective-permute-start | bytes 393224 | tf_op jit(solution)/shard_map/ppermute | solution.py:88
  280.9 18.5 %collective-permute-start.32 = (f32[8,640]{1,0:T(8,128)S(1)}, f32[8,640]{1,0:T(8,128)S(1)}, u32[]{:S(2)}, u32[]{:S(2)}) collective-permute-start(f32[8,640]{1,0:T(8,128)S(1)} %get-tuple-element.210), channel_id=1, source_target_pairs={{4,0},{8,4},{12,8},{16,12},{20,16},{24,20},{28,24},{5,1},{9,5},{13... | collective-permute-start | bytes 61448 | tf_op jit(solution)/shard_map/ppermute | solution.py:1160
  309.3 197.3 %reduce-scatter.8.cloned.1.call-start = ((), (), s32[]{:S(2)}) async-start(), calls=%async_computation.5 | async-start | bytes 3538944 | tf_op jit(solution)/shard_map/reduce_scatter | solution.py:75
  310.6 12.4 %collective-permute-start.34 = (bf16[64,1024]{1,0:T(8,128)(2,1)}, bf16[64,1024]{1,0:T(8,128)(2,1)S(1)}, u32[]{:S(2)}, u32[]{:S(2)}) collective-permute-start(bf16[64,1024]{1,0:T(8,128)(2,1)} %copy-done.212), channel_id=1, source_target_pairs={{0,2},{1,3},{2,0},{3,1},{4,6},{5,7},{6,4},{7,5},{8,10},{9,11},{10,... | collective-permute-start | bytes 393224 | tf_op jit(solution)/shard_map/ppermute | solution.py:88
  312.0 11.0 %collective-permute-start.35 = (bf16[64,1024]{1,0:T(8,128)(2,1)}, bf16[64,1024]{1,0:T(8,128)(2,1)S(1)}, u32[]{:S(2)}, u32[]{:S(2)}) collective-permute-start(bf16[64,1024]{1,0:T(8,128)(2,1)} %copy-done.211), channel_id=1, source_target_pairs={{0,3},{1,0},{2,1},{3,2},{4,7},{5,4},{6,5},{7,6},{8,11},{9,8},{10,9... | collective-permute-start | bytes 393224 | tf_op jit(solution)/shard_map/ppermute | solution.py:88
  349.8 10.4 %collective-permute-start.40 = (bf16[64,1024]{1,0:T(8,128)(2,1)S(1)}, bf16[64,1024]{1,0:T(8,128)(2,1)S(1)}, u32[]{:S(2)}, u32[]{:S(2)}) collective-permute-start(bf16[64,1024]{1,0:T(8,128)(2,1)S(1)} %get-tuple-element.235), channel_id=1, source_target_pairs={{0,2},{1,3},{2,0},{3,1},{4,6},{5,7},{6,4},{7,5},{8,10},{9,11},{10,... | collective-permute-start | bytes 393224 | tf_op jit(solution)/shard_map/ppermute | solution.py:88
  390.3 121.1 %reduce-scatter.6.cloned.1.call-start = ((), (), s32[]{:S(2)}) async-start(), calls=%async_computation.4 | async-start | bytes 4423680 | tf_op jit(solution)/shard_map/reduce_scatter | solution.py:75
  410.8 16.3 %collective-permute-start.45 = (f32[8,640]{1,0:T(8,128)S(1)}, f32[8,640]{1,0:T(8,128)S(1)}, u32[]{:S(2)}, u32[]{:S(2)}) collective-permute-start(f32[8,640]{1,0:T(8,128)S(1)} %get-tuple-element.253), channel_id=1, source_target_pairs={{4,0},{8,4},{12,8},{16,12},{20,16},{24,20},{28,24},{5,1},{9,5},{13... | collective-permute-start | bytes 61448 | tf_op jit(solution)/shard_map/ppermute | solution.py:1160
  439.8 11.4 %collective-permute-start.47 = (bf16[64,1024]{1,0:T(8,128)(2,1)S(1)}, bf16[64,1024]{1,0:T(8,128)(2,1)S(1)}, u32[]{:S(2)}, u32[]{:S(2)}) collective-permute-start(bf16[64,1024]{1,0:T(8,128)(2,1)S(1)} %get-tuple-element.263), channel_id=1, source_target_pairs={{0,2},{1,3},{2,0},{3,1},{4,6},{5,7},{6,4},{7,5},{8,10},{9,11},{10,... | collective-permute-start | bytes 393224 | tf_op jit(solution)/shard_map/ppermute | solution.py:88
  466.5 30.4 %collective-permute-start.52 = (bf16[64,1024]{1,0:T(8,128)(2,1)}, bf16[64,1024]{1,0:T(8,128)(2,1)S(1)}, u32[]{:S(2)}, u32[]{:S(2)}) collective-permute-start(bf16[64,1024]{1,0:T(8,128)(2,1)} %held_back.6.refs_1_), channel_id=1, source_target_pairs={{0,1},{1,2},{2,3},{3,0},{4,5},{5,6},{6,7},{7,4},{8,9},{9,10},{10,1... | collective-permute-start | bytes 393224 | tf_op jit(solution)/shard_map/ppermute | solution.py:81
  469.1 27.7 %collective-permute-start.53 = (bf16[64,1024]{1,0:T(8,128)(2,1)}, bf16[64,1024]{1,0:T(8,128)(2,1)S(1)}, u32[]{:S(2)}, u32[]{:S(2)}) collective-permute-start(bf16[64,1024]{1,0:T(8,128)(2,1)} %held_back.6.refs_1_), channel_id=1, source_target_pairs={{0,2},{1,3},{2,0},{3,1},{4,6},{5,7},{6,4},{7,5},{8,10},{9,11},{10,... | collective-permute-start | bytes 393224 | tf_op jit(solution)/shard_map/ppermute | solution.py:81
  484.8 10.2 %collective-permute-start.56 = (f32[52,128]{1,0:T(8,128)S(1)}, f32[52,128]{1,0:T(8,128)S(1)}, u32[]{:S(2)}, u32[]{:S(2)}) collective-permute-start(f32[52,128]{1,0:T(8,128)S(1)} %slice.271), channel_id=1, source_target_pairs={{0,2},{1,3},{2,0},{3,1},{4,6},{5,7},{6,4},{7,5},{8,10},{9,11},{10,... | collective-permute-start | bytes 79880 | tf_op jit(solution)/shard_map/ppermute | solution.py:81
  498.1 24.5 %collective-permute-start.63 = (bf16[128,384]{1,0:T(8,128)(2,1)}, bf16[128,384]{1,0:T(8,128)(2,1)S(1)}, u32[]{:S(2)}, u32[]{:S(2)}) collective-permute-start(bf16[128,384]{1,0:T(8,128)(2,1)} %held_back.7), channel_id=1, source_target_pairs={{0,3},{1,0},{2,1},{3,2},{4,7},{5,4},{6,5},{7,6},{8,11},{9,8},{10,9... | collective-permute-start | bytes 294920 | tf_op jit(solution)/shard_map/ppermute | solution.py:81
  502.3 20.9 %collective-permute-start.61 = (bf16[128,384]{1,0:T(8,128)(2,1)}, bf16[128,384]{1,0:T(8,128)(2,1)S(1)}, u32[]{:S(2)}, u32[]{:S(2)}) collective-permute-start(bf16[128,384]{1,0:T(8,128)(2,1)} %held_back.7), channel_id=1, source_target_pairs={{0,2},{1,3},{2,0},{3,1},{4,6},{5,7},{6,4},{7,5},{8,10},{9,11},{10,... | collective-permute-start | bytes 294920 | tf_op jit(solution)/shard_map/ppermute | solution.py:81
  502.3 20.9 %collective-permute-start.59 = (bf16[128,384]{1,0:T(8,128)(2,1)}, bf16[128,384]{1,0:T(8,128)(2,1)S(1)}, u32[]{:S(2)}, u32[]{:S(2)}) collective-permute-start(bf16[128,384]{1,0:T(8,128)(2,1)} %held_back.7), channel_id=1, source_target_pairs={{0,1},{1,2},{2,3},{3,0},{4,5},{5,6},{6,7},{7,4},{8,9},{9,10},{10,1... | collective-permute-start | bytes 294920 | tf_op jit(solution)/shard_map/ppermute | solution.py:81
  512.6 10.7 %collective-permute-start.62 = (bf16[128,384]{1,0:T(8,128)(2,1)S(1)}, bf16[128,384]{1,0:T(8,128)(2,1)S(1)}, u32[]{:S(2)}, u32[]{:S(2)}) collective-permute-start(bf16[128,384]{1,0:T(8,128)(2,1)S(1)} %get-tuple-element.352), channel_id=1, source_target_pairs={{0,3},{1,0},{2,1},{3,2},{4,7},{5,4},{6,5},{7,6},{8,11},{9,8},{10,9... | collective-permute-start | bytes 294920 | tf_op jit(solution)/shard_map/ppermute | solution.py:81
  (270 other events, 3540.2 us)
Sparse Core Ops, SparseCore 0:
  309.4 63.3 reduce-scatter.3
  390.5 47.7 reduce-scatter.7
  441.8 50.5 reduce-scatter.5
